TPU v7x, 32 devices: a whole 2x2x4 slice. The times are simulated.
32 devices in a mesh: rep: 8 (over y, x, core), grp: 4 (over z).
Axes of the slice: x: 2, y: 2, z: 4, core: 2. Of those that a mesh axis runs over, the one named last changes fastest.
Arguments:
- row_ids: int32 [16384, 26, 30], P(('rep', 'grp')), may hold values from 0 to 2047
- bag_counts: int32 [16384, 26], P(('rep', 'grp')), may hold values from 1 to 30
- labels: int32 [16384], P(('rep', 'grp')), may hold values from 0 to 1
- dense_input: float32 [16384, 128], P(('rep', 'grp')), may hold values from -6 to 6
- tables: float32 [26, 2048, 128], P(None, 'grp'), may hold values from -6 to 6
- table_first: float32 [26, 2048, 128], P(None, 'grp'), may hold values from -1.1920929e-07 to 1.1920929e-07
- table_second: float32 [26, 2048, 128], P(None, 'grp'), may hold values from 1.490116e-17 to 2.3841857e-16
- cross_down: float32 [3, 3456, 512], P(None, 'rep'), may hold values from -0.109375 to 0.109375
- down_first: float32 [3, 3456, 512], P(None, 'rep'), may hold values from -9.536743e-06 to 9.536743e-06
- down_second: float32 [3, 3456, 512], P(None, 'rep'), may hold values from 1.2207031e-13 to 1.953125e-12
- cross_up: float32 [3, 512, 3456], P(None, 'rep'), may hold values from -0.25 to 0.25
- up_first: float32 [3, 512, 3456], P(None, 'rep'), may hold values from -4.7683716e-06 to 4.7683716e-06
- up_second: float32 [3, 512, 3456], P(None, 'rep'), may hold values from 3.0517577e-14 to 4.8828124e-13
- hidden_one: float32 [3456, 1024], P('rep'), may hold values from -0.109375 to 0.109375
- one_first: float32 [3456, 1024], P('rep'), may hold values from -3.8146973e-05 to 3.8146973e-05
- one_second: float32 [3456, 1024], P('rep'), may hold values from 1.4953613e-12 to 2.380371e-11
- hidden_two: float32 [1024, 1024], P('rep'), may hold values from -0.1875 to 0.1875
- two_first: float32 [1024, 1024], P('rep'), may hold values from -2.2888184e-05 to 2.2888184e-05
- two_second: float32 [1024, 1024], P('rep'), may hold values from 6.1035156e-13 to 9.765625e-12
- hidden_three: float32 [1024, 512], P('rep'), may hold values from -0.1875 to 0.1875
- three_first: float32 [1024, 512], P('rep'), may hold values from -6.1035156e-05 to 6.1035156e-05
- three_second: float32 [1024, 512], P('rep'), may hold values from 4.394531e-12 to 7.019043e-11
- smalls: float32 [13441], replicated, may hold values from -0.625 to 0.625
- small_first: float32 [13441], replicated, may hold values from -1 to 1
- small_second: float32 [13441], replicated, may hold values from 0 to 1
Outputs:
- loss_sum: float32 [], replicated
- new_tables: float32 [26, 2048, 128], P(None, 'grp')
- new_table_first: float32 [26, 2048, 128], P(None, 'grp')
- new_table_second: float32 [26, 2048, 128], P(None, 'grp')
- new_down: float32 [3, 3456, 512], P(None, 'rep')
- new_down_first: float32 [3, 3456, 512], P(None, 'rep')
- new_down_second: float32 [3, 3456, 512], P(None, 'rep')
- new_up: float32 [3, 512, 3456], P(None, 'rep')
- new_up_first: float32 [3, 512, 3456], P(None, 'rep')
- new_up_second: float32 [3, 512, 3456], P(None, 'rep')
- new_one: float32 [3456, 1024], P('rep')
- new_one_first: float32 [3456, 1024], P('rep')
- new_one_second: float32 [3456, 1024], P('rep')
- new_two: float32 [1024, 1024], P('rep')
- new_two_first: float32 [1024, 1024], P('rep')
- new_two_second: float32 [1024, 1024], P('rep')
- new_three: float32 [1024, 512], P('rep')
- new_three_first: float32 [1024, 512], P('rep')
- new_three_second: float32 [1024, 512], P('rep')
- new_smalls: float32 [13441], replicated
- new_small_first: float32 [13441], replicated
- new_small_second: float32 [13441], replicated
All inputs are finite; a program needn't handle non-finite values.
Results may differ from a plain program's by a relative error of at most 0.019.
Values may be sent and summed in bfloat16 or wider, within the bound.
No kernel may reach another device: no remote copies, remote signals or barrier semaphores. Data moves between devices by JAX's collectives and lax.ppermute only.
A program may use at most 384 MiB of HBM per device.

v0:
```python
import math

import jax
import jax.numpy as jnp
from jax import lax
from jax.sharding import PartitionSpec as P

D_IN = 3456
RANK = 512
CROSS = 3
H1 = 1024
H2 = 1024
H3 = 512
STEP = 10


BETA_ONE = 0.9
BETA_TWO = 0.999
EPSILON = 1e-12
DECAY = 0.01
HIGH = lax.Precision.HIGHEST


def split_smalls(smalls):
    extents = [CROSS * D_IN, H1, H2, H3, H3, 1]
    pieces = []
    offset = 0
    for extent in extents:
        pieces.append(smalls[offset : offset + extent])
        offset = offset + extent
    return (pieces[0].reshape(CROSS, D_IN), pieces[1], pieces[2], pieces[3], pieces[4], pieces[5])


def product(left, right):
    return jnp.dot(left, right, preferred_element_type=jnp.float32)


def left_product(left, right):
    return lax.dot_general(
        left, right, (((0,), (0,)), ((), ())), preferred_element_type=jnp.float32
    )


def right_product(left, right):
    return lax.dot_general(
        left, right, (((1,), (1,)), ((), ())), preferred_element_type=jnp.float32
    )


def silu_slope(value):
    logistic = jax.nn.sigmoid(value)
    return logistic * (1.0 + value * (1.0 - logistic))


def multiplicity(row_ids, bag_counts, first_row, extent):
    slots = lax.broadcasted_iota(jnp.int32, row_ids.shape, 2)
    live = slots < bag_counts[:, :, None]
    rows_here = lax.broadcasted_iota(jnp.int32, (1, 1, 1, extent), 3) + first_row
    hits = (row_ids[:, :, :, None] == rows_here) & live[:, :, :, None]
    return jnp.sum(hits.astype(jnp.float32), axis=2).astype(jnp.bfloat16)


def pool_sums(table_low, row_ids, bag_counts, first_row):
    samples = row_ids.shape[0]
    block = math.gcd(samples, 64)
    extent = table_low.shape[1]

    def pool_block(item):
        counts = multiplicity(item[0], item[1], first_row, extent)
        return jnp.einsum("bfr,fre->bfe", counts, table_low, preferred_element_type=jnp.float32)

    shaped = (
        row_ids.reshape(samples // block, block, row_ids.shape[1], row_ids.shape[2]),
        bag_counts.reshape(samples // block, block, bag_counts.shape[1]),
    )
    summed = lax.map(pool_block, shaped)
    return summed.reshape(samples, table_low.shape[0], table_low.shape[2])


def row_gradient(grad_summed, row_ids, bag_counts, first_row, extent):
    samples, features, width = grad_summed.shape
    block = math.gcd(samples, 64)

    def add_block(total, item):
        counts = multiplicity(item[1], item[2], first_row, extent)
        return (
            total + jnp.einsum("bfr,bfe->fre", counts, item[0], preferred_element_type=jnp.float32),
            None,
        )

    shaped = (
        grad_summed.reshape(samples // block, block, features, width),
        row_ids.reshape(samples // block, block, features, row_ids.shape[2]),
        bag_counts.reshape(samples // block, block, features),
    )
    total, unused = lax.scan(add_block, jnp.zeros((features, extent, width), jnp.float32), shaped)
    return total


def cross_forward(anchor, stream, down, upward, bias):
    low_stream = stream.astype(jnp.bfloat16)
    narrow = product(low_stream, down).astype(jnp.bfloat16)
    factor = product(narrow, upward) + bias
    return (anchor * factor + stream, (low_stream, narrow, factor))


def cross_backward(anchor, saved, down, upward, grad_next):
    low_stream, narrow, factor = saved
    grad_factor = (anchor * grad_next).astype(jnp.bfloat16)
    grad_bias = jnp.sum(grad_factor.astype(jnp.float32), axis=0)
    grad_up = left_product(narrow, grad_factor)
    grad_narrow = right_product(grad_factor, upward).astype(jnp.bfloat16)
    grad_down = left_product(low_stream, grad_narrow)
    grad_stream = grad_next + right_product(grad_narrow, down)
    return (grad_stream, factor * grad_next, grad_down, grad_up, grad_bias)


def dense_backward(inputs, pre, grad_out, weight):
    grad_pre = (grad_out * silu_slope(pre)).astype(jnp.bfloat16)
    grad_weight = left_product(inputs, grad_pre)
    grad_bias = jnp.sum(grad_pre.astype(jnp.float32), axis=0)
    return (grad_weight, grad_bias, right_product(grad_pre, weight))


def adamw(weight, grad, first, second, rate):
    first = BETA_ONE * first + (1.0 - BETA_ONE) * grad
    second = BETA_TWO * second + (1.0 - BETA_TWO) * grad * grad
    corr_one = 1.0 - BETA_ONE**STEP
    corr_two = 1.0 - BETA_TWO**STEP
    moved = first / corr_one / (jnp.sqrt(second / corr_two) + EPSILON) + DECAY * weight
    return (weight - rate * moved, first, second)


def on_device(
    row_ids,
    bag_counts,
    labels,
    dense_input,
    tables,
    table_first,
    table_second,
    cross_down,
    down_first,
    down_second,
    cross_up,
    up_first,
    up_second,
    hidden_one,
    one_first,
    one_second,
    hidden_two,
    two_first,
    two_second,
    hidden_three,
    three_first,
    three_second,
    smalls,
    small_first,
    small_second,
):
    down_all, up_all, one_all, two_all, three_all = (
        lax.all_gather(cross_down.astype(jnp.bfloat16), "rep", axis=1, tiled=True),
        lax.all_gather(cross_up.astype(jnp.bfloat16), "rep", axis=1, tiled=True),
        lax.all_gather(hidden_one.astype(jnp.bfloat16), "rep", axis=0, tiled=True),
        lax.all_gather(hidden_two.astype(jnp.bfloat16), "rep", axis=0, tiled=True),
        lax.all_gather(hidden_three.astype(jnp.bfloat16), "rep", axis=0, tiled=True),
    )
    cross_bias, bias_one, bias_two, bias_three, head_weight, head_bias = split_smalls(smalls)
    group = lax.axis_size("grp")
    member = lax.axis_index("grp")
    extent = tables.shape[1]
    samples = row_ids.shape[0]
    table_low = tables.astype(jnp.bfloat16)
    whole_table = lax.all_gather(table_low, "grp", axis=1, tiled=True)
    summed = pool_sums(whole_table, row_ids, bag_counts, 0)
    count_float = bag_counts.astype(jnp.float32)[:, :, None]
    pooled = summed / count_float
    anchor = jnp.concatenate([pooled.reshape(samples, -1), dense_input], axis=1)
    stream = anchor
    kept = []
    for layer_index in range(CROSS):
        stream, saved = cross_forward(
            anchor, stream, down_all[layer_index], up_all[layer_index], cross_bias[layer_index]
        )
        kept.append(saved)
    in_one = stream.astype(jnp.bfloat16)
    pre_one = product(in_one, one_all) + bias_one
    in_two = jax.nn.silu(pre_one).astype(jnp.bfloat16)
    pre_two = product(in_two, two_all) + bias_two
    in_three = jax.nn.silu(pre_two).astype(jnp.bfloat16)
    pre_three = product(in_three, three_all) + bias_three
    top = jax.nn.silu(pre_three)
    logit = jnp.dot(top, head_weight, precision=HIGH) + head_bias[0]
    target = labels.astype(jnp.float32)
    loss_local = jnp.sum(jax.nn.softplus(logit) - target * logit)
    total_samples = samples * lax.axis_size("rep") * group
    grad_logit = (jax.nn.sigmoid(logit) - target) / total_samples
    grad_head = jnp.dot(grad_logit, top, precision=HIGH)
    grad_head_bias = jnp.sum(grad_logit, keepdims=True)
    grad_top = grad_logit[:, None] * head_weight[None, :]
    grad_three, bias_grad_three, grad_in = dense_backward(in_three, pre_three, grad_top, three_all)
    grad_two, bias_grad_two, grad_in = dense_backward(in_two, pre_two, grad_in, two_all)
    grad_one, bias_grad_one, grad_stream = dense_backward(in_one, pre_one, grad_in, one_all)
    grad_anchor = jnp.zeros_like(anchor)
    down_grads = []
    up_grads = []
    bias_grads = []
    for layer_index in reversed(range(CROSS)):
        grad_stream, anchor_part, grad_down, grad_up, grad_bias = cross_backward(
            anchor, kept[layer_index], down_all[layer_index], up_all[layer_index], grad_stream
        )
        grad_anchor = grad_anchor + anchor_part
        down_grads.insert(0, grad_down)
        up_grads.insert(0, grad_up)
        bias_grads.insert(0, grad_bias)
    grad_anchor = grad_anchor + grad_stream
    grad_summed = (
        grad_anchor[:, : pooled.shape[1] * pooled.shape[2]].reshape(pooled.shape) / count_float
    ).astype(jnp.bfloat16)
    late_rows, late_counts = (
        lax.all_gather(row_ids, "grp", axis=0, tiled=True),
        lax.all_gather(bag_counts, "grp", axis=0, tiled=True),
    )
    late_group = lax.all_gather(grad_summed, "grp", axis=0, tiled=True)
    row_share = row_gradient(late_group, late_rows, late_counts, member * extent, extent)
    table_grad = lax.psum(row_share.astype(jnp.bfloat16), "rep").astype(jnp.float32)
    stack_down = jnp.stack(down_grads)
    stack_up = jnp.stack(up_grads)
    share_down, share_up, share_one, share_two, share_three = (
        lax.psum_scatter(
            stack_down.astype(jnp.bfloat16), "rep", scatter_dimension=1, tiled=True
        ).astype(jnp.float32),
        lax.psum_scatter(
            stack_up.astype(jnp.bfloat16), "rep", scatter_dimension=1, tiled=True
        ).astype(jnp.float32),
        lax.psum_scatter(
            grad_one.astype(jnp.bfloat16), "rep", scatter_dimension=0, tiled=True
        ).astype(jnp.float32),
        lax.psum_scatter(
            grad_two.astype(jnp.bfloat16), "rep", scatter_dimension=0, tiled=True
        ).astype(jnp.float32),
        lax.psum_scatter(
            grad_three.astype(jnp.bfloat16), "rep", scatter_dimension=0, tiled=True
        ).astype(jnp.float32),
    )
    share_down, share_up, share_one, share_two, share_three = (
        lax.psum(share_down.astype(jnp.bfloat16), "grp").astype(jnp.float32),
        lax.psum(share_up.astype(jnp.bfloat16), "grp").astype(jnp.float32),
        lax.psum(share_one.astype(jnp.bfloat16), "grp").astype(jnp.float32),
        lax.psum(share_two.astype(jnp.bfloat16), "grp").astype(jnp.float32),
        lax.psum(share_three.astype(jnp.bfloat16), "grp").astype(jnp.float32),
    )
    small_grad = jnp.concatenate(
        [
            jnp.stack(bias_grads).reshape(-1),
            bias_grad_one,
            bias_grad_two,
            bias_grad_three,
            grad_head,
            grad_head_bias,
        ]
    )
    small_sum, loss_sum = lax.psum((small_grad, loss_local), ("rep", "grp"))
    new_tables, new_table_first, new_table_second = adamw(
        tables, table_grad, table_first, table_second, 1.0
    )
    new_down, new_down_first, new_down_second = adamw(
        cross_down, share_down, down_first, down_second, D_IN ** (-0.5)
    )
    new_up, new_up_first, new_up_second = adamw(
        cross_up, share_up, up_first, up_second, RANK ** (-0.5)
    )
    new_one, new_one_first, new_one_second = adamw(
        hidden_one, share_one, one_first, one_second, D_IN ** (-0.5)
    )
    new_two, new_two_first, new_two_second = adamw(
        hidden_two, share_two, two_first, two_second, H1 ** (-0.5)
    )
    new_three, new_three_first, new_three_second = adamw(
        hidden_three, share_three, three_first, three_second, H2 ** (-0.5)
    )
    new_smalls, new_small_first, new_small_second = adamw(
        smalls, small_sum, small_first, small_second, 0.1
    )
    return (
        loss_sum,
        new_tables,
        new_table_first,
        new_table_second,
        new_down,
        new_down_first,
        new_down_second,
        new_up,
        new_up_first,
        new_up_second,
        new_one,
        new_one_first,
        new_one_second,
        new_two,
        new_two_first,
        new_two_second,
        new_three,
        new_three_first,
        new_three_second,
        new_smalls,
        new_small_first,
        new_small_second,
    )


def solution(mesh):
    return jax.shard_map(
        on_device,
        mesh=mesh,
        in_specs=(
            P(("rep", "grp"), None, None),
            P(("rep", "grp"), None),
            P(("rep", "grp")),
            P(("rep", "grp"), None),
            P(None, "grp", None),
            P(None, "grp", None),
            P(None, "grp", None),
            P(None, "rep", None),
            P(None, "rep", None),
            P(None, "rep", None),
            P(None, "rep", None),
            P(None, "rep", None),
            P(None, "rep", None),
            P("rep", None),
            P("rep", None),
            P("rep", None),
            P("rep", None),
            P("rep", None),
            P("rep", None),
            P("rep", None),
            P("rep", None),
            P("rep", None),
            P(),
            P(),
            P(),
        ),
        out_specs=(
            P(),
            P(None, "grp", None),
            P(None, "grp", None),
            P(None, "grp", None),
            P(None, "rep", None),
            P(None, "rep", None),
            P(None, "rep", None),
            P(None, "rep", None),
            P(None, "rep", None),
            P(None, "rep", None),
            P("rep", None),
            P("rep", None),
            P("rep", None),
            P("rep", None),
            P("rep", None),
            P("rep", None),
            P("rep", None),
            P("rep", None),
            P("rep", None),
            P(),
            P(),
            P(),
        ),
        check_vma=False,
    )
```

profile of v0, /device:TPU:0, one launch (start us, length us, event | category | flops | bytes accessed | tf_op | source)
XLA Modules:
  0.0 3231.1 jit_solution(7288455256302855073)
XLA Ops:
  42.3 208.3 %all-gather.9.cloned.1.call-done = bf16[26,2048,128]{2,1,0:T(8,128)(2,1)} async-done(((bf16[26,512,128]{2,1,0:T(8,128)(2,1)}), bf16[26,2048,128]{2,1,0:T(8,128)(2,1)}) %all-gather.9.cloned.1.call-update) | async-done | bytes 13631504 | tf_op jit(solution)/shard_map/all_gather | solution.py:174
  250.7 910.1 %while.21 = (s32[]{:T(128)}, f32[8,64,26,128]{3,1,2,0:T(8,128)}, s32[8,64,26,30]{1,0,3,2:T(8,128)}, s32[8,64,26]{1,0,2:T(8,128)S(1)}, bf16[26,2048,128]{2,1,0:T(8,128)(2,1)}, /*index=5*/s32[]{:T(128)}) while((s32[]{:T(128)}, f32[8,64,26,128]{3,1,2,0:T(8,128)}, s32[8,64,26,30]{1,0,3,2:T(8,128)}, s32[8,64,26]{1,0,2:T(8,128)S(1)}, ...), condition=%wide.region_2.3_spmd, body=%wide.region_0.2_spmd.sunk | while | flops 1278001920 | bytes 29246552 | solution.py:76
  253.0 101.1 %convert_reduce_fusion.10 = bf16[64,26,2048]{2,0,1:T(8,128)(2,1)} fusion(s32[64,26,30]{0,2,1:T(8,128)S(1)} %bitcast.168, pred[64,26,30]{0,2,1:T(8,128)(4,1)S(1)} %iota_compare_fusion.5), kind=kLoop, calls=%fused_computation.clone.1 | loop fusion | flops 405536768 | bytes 7065344 | tf_op jit(solution)/shard_map/while/body/eval_jaxpr/reduce_sum | solution.py:60
  366.9 101.1 %convert_reduce_fusion.10 = bf16[64,26,2048]{2,0,1:T(8,128)(2,1)} fusion(s32[64,26,30]{0,2,1:T(8,128)S(1)} %bitcast.168, pred[64,26,30]{0,2,1:T(8,128)(4,1)S(1)} %iota_compare_fusion.5), kind=kLoop, calls=%fused_computation.clone.1 | loop fusion | flops 405536768 | bytes 7065344 | tf_op jit(solution)/shard_map/while/body/eval_jaxpr/reduce_sum | solution.py:60
  480.7 101.1 %convert_reduce_fusion.10 = bf16[64,26,2048]{2,0,1:T(8,128)(2,1)} fusion(s32[64,26,30]{0,2,1:T(8,128)S(1)} %bitcast.168, pred[64,26,30]{0,2,1:T(8,128)(4,1)S(1)} %iota_compare_fusion.5), kind=kLoop, calls=%fused_computation.clone.1 | loop fusion | flops 405536768 | bytes 7065344 | tf_op jit(solution)/shard_map/while/body/eval_jaxpr/reduce_sum | solution.py:60
  594.3 101.1 %convert_reduce_fusion.10 = bf16[64,26,2048]{2,0,1:T(8,128)(2,1)} fusion(s32[64,26,30]{0,2,1:T(8,128)S(1)} %bitcast.168, pred[64,26,30]{0,2,1:T(8,128)(4,1)S(1)} %iota_compare_fusion.5), kind=kLoop, calls=%fused_computation.clone.1 | loop fusion | flops 405536768 | bytes 7065344 | tf_op jit(solution)/shard_map/while/body/eval_jaxpr/reduce_sum | solution.py:60
  708.0 101.1 %convert_reduce_fusion.10 = bf16[64,26,2048]{2,0,1:T(8,128)(2,1)} fusion(s32[64,26,30]{0,2,1:T(8,128)S(1)} %bitcast.168, pred[64,26,30]{0,2,1:T(8,128)(4,1)S(1)} %iota_compare_fusion.5), kind=kLoop, calls=%fused_computation.clone.1 | loop fusion | flops 405536768 | bytes 7065344 | tf_op jit(solution)/shard_map/while/body/eval_jaxpr/reduce_sum | solution.py:60
  821.6 101.1 %convert_reduce_fusion.10 = bf16[64,26,2048]{2,0,1:T(8,128)(2,1)} fusion(s32[64,26,30]{0,2,1:T(8,128)S(1)} %bitcast.168, pred[64,26,30]{0,2,1:T(8,128)(4,1)S(1)} %iota_compare_fusion.5), kind=kLoop, calls=%fused_computation.clone.1 | loop fusion | flops 405536768 | bytes 7065344 | tf_op jit(solution)/shard_map/while/body/eval_jaxpr/reduce_sum | solution.py:60
  935.3 101.1 %convert_reduce_fusion.10 = bf16[64,26,2048]{2,0,1:T(8,128)(2,1)} fusion(s32[64,26,30]{0,2,1:T(8,128)S(1)} %bitcast.168, pred[64,26,30]{0,2,1:T(8,128)(4,1)S(1)} %iota_compare_fusion.5), kind=kLoop, calls=%fused_computation.clone.1 | loop fusion | flops 405536768 | bytes 7065344 | tf_op jit(solution)/shard_map/while/body/eval_jaxpr/reduce_sum | solution.py:60
  1049.0 101.1 %convert_reduce_fusion.10 = bf16[64,26,2048]{2,0,1:T(8,128)(2,1)} fusion(s32[64,26,30]{0,2,1:T(8,128)S(1)} %bitcast.168, pred[64,26,30]{0,2,1:T(8,128)(4,1)S(1)} %iota_compare_fusion.5), kind=kLoop, calls=%fused_computation.clone.1 | loop fusion | flops 405536768 | bytes 7065344 | tf_op jit(solution)/shard_map/while/body/eval_jaxpr/reduce_sum | solution.py:60
  1333.7 61.0 %reduce-scatter.10.cloned.1.call-done = bf16[432,1024]{1,0:T(8,128)(2,1)} async-done(((bf16[3456,1024]{1,0:T(8,128)(2,1)}), bf16[432,1024]{1,0:T(8,128)(2,1)}) %reduce-scatter.10.cloned.1.call-update) | async-done | bytes 884752 | tf_op jit(solution)/shard_map/reduce_scatter | solution.py:236
  1394.7 85.6 %reduce-scatter.6.cloned.1.call-done = bf16[3,432,512]{2,1,0:T(8,128)(2,1)} async-done(((bf16[3,3456,512]{2,1,0:T(8,128)(2,1)}), bf16[3,432,512]{2,1,0:T(8,128)(2,1)}) %reduce-scatter.6.cloned.1.call-update) | async-done | bytes 1327120 | tf_op jit(solution)/shard_map/reduce_scatter | solution.py:230
  1480.3 85.7 %reduce-scatter.8.cloned.1.call-done = bf16[3,64,3456]{2,1,0:T(8,128)(2,1)} async-done(((bf16[3,512,3456]{2,1,0:T(8,128)(2,1)}), bf16[3,64,3456]{2,1,0:T(8,128)(2,1)}) %reduce-scatter.8.cloned.1.call-update) | async-done | bytes 1327120 | tf_op jit(solution)/shard_map/reduce_scatter | solution.py:233
  1626.3 69.2 %all-gather.21.cloned.1.call-done = s32[2048,26,30]{0,2,1:T(8,128)} async-done(((s32[512,26,30]{0,2,1:T(8,128)}), s32[2048,26,30]{0,2,1:T(8,128)}) %all-gather.21.cloned.1.call-update) | async-done | bytes 6389776 | tf_op jit(solution)/shard_map/all_gather | solution.py:221
  1721.8 45.4 %all-reduce = (f32[]{:T(128)}, f32[13441]{0:T(1024)}) all-reduce(f32[]{:T(128)} %get-tuple-element.199, f32[13441]{0:T(1024)} %constant_dynamic-update-slice_fusion), channel_id=1, replica_groups=mesh['rep'=8,'grp'=4] {'rep','grp'}, use_global_device_ids=true, to_apply=%region_4.5 | all-reduce | flops 13442 | bytes 107536 | tf_op jit(solution)/shard_map/psum | solution.py:263
  1768.8 76.7 %all-reduce.7.cloned.1.call-done = (bf16[3,432,512]{2,1,0:T(8,128)(2,1)}, bf16[3,64,3456]{2,1,0:T(8,128)(2,1)}, bf16[432,1024]{1,0:T(8,128)(2,1)}, bf16[128,1024]{1,0:T(8,128)(2,1)}, bf16[128,512]{1,0:T(8,128)(2,1)}) async-done(((bf16[3,432,512]{2,1,0:T(8,128)(2,1)}, bf16[3,64,3456]{2,1,0:T(8,128)(2,1)}, bf16[432,1024]{1,0:T(8,128)(2,1)}, bf16[128,1024]{1,0:T(8,128)(2,1)}, bf16[128,512]{1,0:T(8,128)(2,1)}), ...) | async-done | bytes 3932176 | tf_op jit(solution)/shard_map/psum | solution.py:247
  1859.0 222.9 %all-gather.23.cloned.1.call-done = bf16[2048,26,128]{0,2,1:T(8,128)(2,1)} async-done(((bf16[512,26,128]{0,2,1:T(8,128)(2,1)}), bf16[2048,26,128]{0,2,1:T(8,128)(2,1)}) %all-gather.23.cloned.1.call-update) | async-done | bytes 13631504 | tf_op jit(solution)/shard_map/all_gather | solution.py:224
  2100.3 1031.0 %while.22 = (s32[]{:T(128)}, f32[26,512,128]{2,1,0:T(8,128)}, s32[32,64,26,30]{1,0,3,2:T(8,128)}, s32[]{:T(128)}, s32[32,64,26]{1,0,2:T(8,128)}, /*index=5*/bf16[32,64,26,128]{3,1,0,2:T(8,128)(2,1)}, s32[]{:T(128)}, s32[]{:T(128)}) while((s32[]{:T(128)}, f32[26,512,128]{2,1,0:T(8,128)}, s32[32,64,26,30]{1,0,3,2:T(8,128)}, ...), condition=%wide.region_7.8_spmd.clone, body=%wide.region_5.7_spmd.clone.sunk | while | flops 322946304 | bytes 18601080 | solution.py:96
  2103.5 21.8 convert_reduce_fusion.11
  2133.7 21.8 convert_reduce_fusion.11
  2166.0 21.8 convert_reduce_fusion.11
  2198.3 21.8 convert_reduce_fusion.11
  2230.6 21.8 convert_reduce_fusion.11
  2262.8 21.8 convert_reduce_fusion.11
  2295.1 21.8 convert_reduce_fusion.11
  2327.4 21.8 convert_reduce_fusion.11
  2359.7 21.8 convert_reduce_fusion.11
  2392.0 21.8 convert_reduce_fusion.11
  2424.2 21.8 convert_reduce_fusion.11
  2456.5 21.8 convert_reduce_fusion.11
  2488.8 21.8 convert_reduce_fusion.11
  2521.1 21.8 convert_reduce_fusion.11
  2553.4 21.8 convert_reduce_fusion.11
  2585.6 21.8 convert_reduce_fusion.11
  2617.9 21.8 convert_reduce_fusion.11
  2650.2 21.8 convert_reduce_fusion.11
  2682.5 21.8 convert_reduce_fusion.11
  2714.8 21.8 convert_reduce_fusion.11
  2747.0 21.8 convert_reduce_fusion.11
  2779.3 21.8 convert_reduce_fusion.11
  2811.6 21.8 convert_reduce_fusion.11
  2843.9 21.8 convert_reduce_fusion.11
  2876.2 21.8 convert_reduce_fusion.11
  2908.5 21.8 convert_reduce_fusion.11
  2940.7 21.8 convert_reduce_fusion.11
  2973.0 21.8 convert_reduce_fusion.11
  3069.9 21.8 convert_reduce_fusion.11
  3147.4 59.8 %all-reduce.5.cloned.1.call-done = bf16[26,512,128]{2,1,0:T(8,128)(2,1)} async-done(((bf16[26,512,128]{2,1,0:T(8,128)(2,1)}), bf16[26,512,128]{2,1,0:T(8,128)(2,1)}) %all-reduce.5.cloned.1.call-update) | async-done | bytes 3407888 | tf_op jit(solution)/shard_map/psum | solution.py:226
  (505 shorter events, 859.0 us)
Async XLA Ops:
  7.2 243.5 %all-gather.9.cloned.1.call-start = ((), (), s32[]{:S(2)}) async-start(), calls=%async_computation.5 | async-start | bytes 17039360 | tf_op jit(solution)/shard_map/all_gather | solution.py:174
  12.5 1168.0 %all-gather.11.cloned.1.call-start = ((), (), s32[]{:S(2)}) async-start(), calls=%async_computation.6 | async-start | bytes 11943936 | tf_op jit(solution)/shard_map/all_gather | solution.py:162
  15.5 1171.2 %all-gather.13.cloned.1.call-start = ((), (), s32[]{:S(2)}) async-start(), calls=%async_computation.7 | async-start | bytes 11943936 | tf_op jit(solution)/shard_map/all_gather | solution.py:163
  18.6 10.2 copy-start.30
  18.6 10.3 copy-start.12
  18.6 1202.7 %all-gather.15.cloned.1.call-start = ((), (), s32[]{:S(2)}) async-start(), calls=%async_computation.8 | async-start | bytes 7962624 | tf_op jit(solution)/shard_map/all_gather | solution.py:164
  19.7 1211.0 %all-gather.17.cloned.1.call-start = ((), (), s32[]{:S(2)}) async-start(), calls=%async_computation.9 | async-start | bytes 2359296 | tf_op jit(solution)/shard_map/all_gather | solution.py:165
  21.6 1214.2 %all-gather.19.cloned.1.call-start = ((), (), s32[]{:S(2)}) async-start(), calls=%async_computation.10 | async-start | bytes 1179648 | tf_op jit(solution)/shard_map/all_gather | solution.py:166
  23.3 1310.3 %reduce-scatter.14.cloned.1.call-start = ((), (), s32[]{:S(2)}) async-start(), calls=%async_computation.18 | async-start | bytes 1179648 | tf_op jit(solution)/shard_map/reduce_scatter | solution.py:242
  28.8 6.0 copy-start.28
  1167.7 12.8 copy-start.13
  1180.5 6.2 copy-start.39
  1186.6 5.7 copy-start.35
  1192.4 7.0 copy-start.47
  1192.4 20.1 copy-start.2
  1192.4 7.1 slice-start
  1192.4 7.9 slice-start.1
  1192.4 7.9 copy-start.38
  1199.3 7.7 copy-start.21
  1212.4 8.9 copy-start.23
  1221.3 9.4 copy-start.42
  1221.3 9.4 copy-start.43
  1239.3 5.5 copy-start.46
  1240.8 7.6 copy-start.40
  1244.8 88.9 %reduce-scatter.12.cloned.1.call-start = ((), (), s32[]{:S(2)}) async-start(), calls=%async_computation.17 | async-start | bytes 2359296 | tf_op jit(solution)/shard_map/reduce_scatter | solution.py:239
  1252.0 142.7 %reduce-scatter.10.cloned.1.call-start = ((), (), s32[]{:S(2)}) async-start(), calls=%async_computation.16 | async-start | bytes 7962624 | tf_op jit(solution)/shard_map/reduce_scatter | solution.py:236
  1263.5 216.8 %reduce-scatter.6.cloned.1.call-start = ((), (), s32[]{:S(2)}) async-start(), calls=%async_computation.14 | async-start | bytes 11943936 | tf_op jit(solution)/shard_map/reduce_scatter | solution.py:230
  1272.6 7.7 copy-start.6
  1272.6 7.7 copy-start
  1272.6 7.7 slice-start.2
  1272.6 8.0 slice-start.3
  1286.7 8.0 copy-start.1
  1286.7 8.0 copy-start.14
  1302.2 5.7 copy-start.4
  1319.2 246.8 %reduce-scatter.8.cloned.1.call-start = ((), (), s32[]{:S(2)}) async-start(), calls=%async_computation.15 | async-start | bytes 11943936 | tf_op jit(solution)/shard_map/reduce_scatter | solution.py:233
  1333.0 233.1 %copy-start.34 = (bf16[512,512]{1,0:T(8,128)(2,1)S(1)}, bf16[512,512]{1,0:T(8,128)(2,1)}, u32[]{:S(2)}) copy-start(bf16[512,512]{1,0:T(8,128)(2,1)} %copy-done.33) | copy-start | bytes 1572868
  1333.0 362.5 %all-gather.21.cloned.1.call-start = ((), (), s32[]{:S(2)}) async-start(), calls=%async_computation.11 | async-start | bytes 8519680 | tf_op jit(solution)/shard_map/all_gather | solution.py:221
  1333.6 511.9 %all-reduce.7.cloned.1.call-start = ((), (), s32[]{:S(2)}) async-start(), calls=%async_computation.19 | async-start | bytes 7864320 | tf_op jit(solution)/shard_map/psum | solution.py:247
  1566.0 515.8 %all-gather.23.cloned.1.call-start = ((), (), s32[]{:S(2)}) async-start(), calls=%async_computation.12 | async-start | bytes 17039360 | tf_op jit(solution)/shard_map/all_gather | solution.py:224
  1593.9 7.7 copy-start.29
  1601.5 5.9 copy-start.31
  1607.4 1599.9 %all-reduce.5.cloned.1.call-start = ((), (), s32[]{:S(2)}) async-start(), calls=%async_computation.13 | async-start | bytes 6815744 | tf_op jit(solution)/shard_map/psum | solution.py:226
  1707.2 140.5 %copy-start.11 = (f32[432,1024]{1,0:T(8,128)S(1)}, f32[432,1024]{1,0:T(8,128)}, u32[]{:S(2)}) copy-start(f32[432,1024]{1,0:T(8,128)} %param.42) | copy-start | bytes 5308420
  1707.2 140.5 %copy-start.25 = (f32[432,1024]{1,0:T(8,128)S(1)}, f32[432,1024]{1,0:T(8,128)}, u32[]{:S(2)}) copy-start(f32[432,1024]{1,0:T(8,128)} %param.43) | copy-start | bytes 5308420
  1847.6 5.4 copy-start.8
  1847.6 5.4 copy-start.18
  1847.7 5.4 copy-start.19
  1847.7 6.4 copy-start.26
  (23 other events, 73.7 us)
Sparse Core Ops, SparseCore 0:
  12.6 238.0 all-gather.8
  253.1 61.9 all-gather.10
  317.7 63.8 all-gather.12
  383.8 48.8 all-gather.14
  435.0 27.8 all-gather.16
  465.3 23.4 all-gather.18
  1244.9 35.1 reduce-scatter.13
  1284.0 41.1 reduce-scatter.11
  1329.1 65.5 reduce-scatter.9
  1398.1 82.1 reduce-scatter.5
  1483.8 82.1 reduce-scatter.7
  1567.4 128.0 all-gather.20
  1698.3 147.1 all-reduce.6
  1847.4 234.3 all-gather.22
  3136.7 70.5 all-reduce.4
where the time goes:
time: 3240 us; the launch traced here: 3230 us
  other arithmetic  1620 us (50%)
  waiting for transfers between devices  870 us (27%)
  matrix products  458 us (14%)
  local copies, waits for them, and re-layouts  201 us (6%)
  blocking collectives  63.4 us (2%)
    reduce_sum x40, other arithmetic, multiplicity(): return jnp.sum(hits.astype(jnp.float32), axis=2).astype(jnp.bfloat16)  1510 us
    dot_general x32, matrix products, add_block(): jnp.einsum('bfr,bfe->fre', counts, item[0], preferred_element_type=jnp.fl...  229 us
    all_gather x1, waiting for transfers between devices, on_device(): late_group = lax.all_gather(grad_summed, 'grp', axis=0, tiled=True)  223 us
    all_gather x1, waiting for transfers between devices, on_device(): whole_table = lax.all_gather(table_low, 'grp', axis=1, tiled=True)  208 us
    dynamic_slice x128, local copies, waits for them, and re-layouts, row_gradient(): lax.scan(add_block, jnp.zeros((features, extent, width), jnp.float32), sh...  101 us
    reduce_scatter x1, waiting for transfers between devices, on_device(): lax.psum_scatter(stack_up.astype(jnp.bfloat16), 'rep', scatter_dimension=...  85.7 us
    reduce_scatter x1, waiting for transfers between devices, on_device(): lax.psum_scatter(stack_down.astype(jnp.bfloat16), 'rep', scatter_dimensio...  85.6 us
    dot_general x8, matrix products, pool_block(): jnp.einsum('bfr,fre->bfe', counts, table_low, preferred_element_type=jnp....  82.5 us
  transfers between devices with their start and end apart: 15, of which 8 were waited for; matrix products, arithmetic and copies ran while one was open for 37% of the time, Pallas kernels for 0%

commit v1 on v0

--- a/solution.py
+++ b/solution.py
@@ -1,8 +1,8 @@
-import math
-
 import jax
 import jax.numpy as jnp
 from jax import lax
+from jax.experimental import pallas as pl
+from jax.experimental.pallas import tpu as pltpu
 from jax.sharding import PartitionSpec as P
 
 D_IN = 3456
@@ -12,6 +12,9 @@
 H2 = 1024
 H3 = 512
 STEP = 10
+GROUP = 8
+SLOTS = 32
+LOW = 128
 
 
 BETA_ONE = 0.9
@@ -52,49 +55,92 @@
     return logistic * (1.0 + value * (1.0 - logistic))
 
 
-def multiplicity(row_ids, bag_counts, first_row, extent):
-    slots = lax.broadcasted_iota(jnp.int32, row_ids.shape, 2)
-    live = slots < bag_counts[:, :, None]
-    rows_here = lax.broadcasted_iota(jnp.int32, (1, 1, 1, extent), 3) + first_row
-    hits = (row_ids[:, :, :, None] == rows_here) & live[:, :, :, None]
-    return jnp.sum(hits.astype(jnp.float32), axis=2).astype(jnp.bfloat16)
-
-
-def pool_sums(table_low, row_ids, bag_counts, first_row):
-    samples = row_ids.shape[0]
-    block = math.gcd(samples, 64)
-    extent = table_low.shape[1]
-
-    def pool_block(item):
-        counts = multiplicity(item[0], item[1], first_row, extent)
-        return jnp.einsum("bfr,fre->bfe", counts, table_low, preferred_element_type=jnp.float32)
-
-    shaped = (
-        row_ids.reshape(samples // block, block, row_ids.shape[1], row_ids.shape[2]),
-        bag_counts.reshape(samples // block, block, bag_counts.shape[1]),
-    )
-    summed = lax.map(pool_block, shaped)
-    return summed.reshape(samples, table_low.shape[0], table_low.shape[2])
-
-
-def row_gradient(grad_summed, row_ids, bag_counts, first_row, extent):
-    samples, features, width = grad_summed.shape
-    block = math.gcd(samples, 64)
-
-    def add_block(total, item):
-        counts = multiplicity(item[1], item[2], first_row, extent)
-        return (
-            total + jnp.einsum("bfr,bfe->fre", counts, item[0], preferred_element_type=jnp.float32),
-            None,
-        )
-
-    shaped = (
-        grad_summed.reshape(samples // block, block, features, width),
-        row_ids.reshape(samples // block, block, features, row_ids.shape[2]),
-        bag_counts.reshape(samples // block, block, features),
-    )
-    total, unused = lax.scan(add_block, jnp.zeros((features, extent, width), jnp.float32), shaped)
-    return total
+def slot_ids(row_ids, bag_counts):
+    samples, features, slots = row_ids.shape
+    live = lax.broadcasted_iota(jnp.int32, row_ids.shape, 2) < bag_counts[:, :, None]
+    ids = jnp.pad(jnp.where(live, row_ids, -1), ((0, 0), (0, 0), (0, SLOTS - slots)), constant_values=-1)
+    return ids.transpose(1, 0, 2).reshape(features, samples // GROUP, GROUP * SLOTS)
+
+
+def one_hot(codes, levels):
+    rows = jnp.broadcast_to(codes, (16, codes.shape[1])).astype(jnp.bfloat16)
+    wanted = lax.broadcasted_iota(jnp.int32, (levels, codes.shape[1]), 0).astype(jnp.float32).astype(jnp.bfloat16)
+    hits = jnp.concatenate([rows] * (levels // 16), axis=0) == wanted
+    return jnp.where(hits, jnp.ones((), jnp.bfloat16), jnp.zeros((), jnp.bfloat16)).astype(jnp.float8_e4m3fn)
+
+
+def pool_kernel(ids_ref, table_ref, counts_ref, dense_ref, anchor_ref, hits_ref, code_ref):
+    feature = pl.program_id(0)
+    features = pl.num_programs(0) - 1
+    samples = hits_ref.shape[1]
+    highs = hits_ref.shape[2] // LOW
+
+    @pl.when(feature < features)
+    def _():
+        ids = ids_ref[0]
+        member = lax.broadcasted_iota(jnp.int32, ids.shape, 1) // SLOTS
+        code_ref[0] = ((ids >> 7) * GROUP + member).astype(jnp.float32)
+        code_ref[1] = (ids & (LOW - 1)).astype(jnp.float32)
+
+        def add_groups(step, unused):
+            first = pl.multiple_of(step * 8, 8)
+            high_codes = code_ref[0, pl.ds(first, 8), :]
+            low_codes = code_ref[1, pl.ds(first, 8), :]
+            for pair in range(4):
+                products = []
+                for row in (2 * pair, 2 * pair + 1):
+                    high_hits = one_hot(high_codes[row : row + 1], highs * GROUP)
+                    low_hits = one_hot(low_codes[row : row + 1], LOW)
+                    products.append(right_product(high_hits, low_hits))
+                start = pl.multiple_of(step * 8 * GROUP + pair * 2 * GROUP, 2 * GROUP)
+                for high in range(highs):
+                    part = slice(high * GROUP, (high + 1) * GROUP)
+                    tile = jnp.concatenate([products[0][part], products[1][part]], axis=0)
+                    hits_ref[0, pl.ds(start, 2 * GROUP), high * LOW : (high + 1) * LOW] = tile.astype(
+                        jnp.bfloat16
+                    )
+            return unused
+
+        lax.fori_loop(0, samples // (8 * GROUP), add_groups, 0)
+        summed = product(hits_ref[0], table_ref[0])
+        lanes = lax.broadcasted_iota(jnp.int32, counts_ref.shape, 1)
+        counts = jnp.sum(jnp.where(lanes == feature, counts_ref[...], 0.0), axis=1, keepdims=True)
+        anchor_ref[...] = summed / counts
+
+    @pl.when(feature == features)
+    def _():
+        anchor_ref[...] = dense_ref[...]
+
+
+def pool(ids, whole_table, count_float, dense_input):
+    features, rows, width = whole_table.shape
+    samples = count_float.shape[0]
+    last = features - 1
+    return pl.pallas_call(
+        pool_kernel,
+        grid=(features + 1,),
+        in_specs=[
+            pl.BlockSpec((1,) + ids.shape[1:], lambda f: (jnp.minimum(f, last), 0, 0)),
+            pl.BlockSpec((1, rows, width), lambda f: (jnp.minimum(f, last), 0, 0)),
+            pl.BlockSpec((samples, features), lambda f: (0, 0)),
+            pl.BlockSpec((samples, width), lambda f: (0, 0)),
+        ],
+        out_specs=[
+            pl.BlockSpec((samples, width), lambda f: (0, f)),
+            pl.BlockSpec((1, samples, rows), lambda f: (jnp.minimum(f, last), 0, 0)),
+        ],
+        out_shape=[
+            jax.ShapeDtypeStruct((samples, (features + 1) * width), jnp.float32),
+            jax.ShapeDtypeStruct((features, samples, rows), jnp.bfloat16),
+        ],
+        scratch_shapes=[pltpu.VMEM((2,) + ids.shape[1:], jnp.float32)],
+        compiler_params=pltpu.CompilerParams(vmem_limit_bytes=48 * 2**20),
+        cost_estimate=pl.CostEstimate(
+            flops=6 * samples * features * rows * width,
+            bytes_accessed=2 * features * rows * (samples + width) + 4 * samples * features * (width + SLOTS),
+            transcendentals=0,
+        ),
+    )(ids, whole_table, count_float, dense_input)
 
 
 def cross_forward(anchor, stream, down, upward, bias):
@@ -167,15 +213,14 @@
     )
     cross_bias, bias_one, bias_two, bias_three, head_weight, head_bias = split_smalls(smalls)
     group = lax.axis_size("grp")
-    member = lax.axis_index("grp")
-    extent = tables.shape[1]
     samples = row_ids.shape[0]
-    table_low = tables.astype(jnp.bfloat16)
-    whole_table = lax.all_gather(table_low, "grp", axis=1, tiled=True)
-    summed = pool_sums(whole_table, row_ids, bag_counts, 0)
-    count_float = bag_counts.astype(jnp.float32)[:, :, None]
-    pooled = summed / count_float
-    anchor = jnp.concatenate([pooled.reshape(samples, -1), dense_input], axis=1)
+    repeats = lax.axis_size("rep")
+    features, extent, width = tables.shape
+    part = extent // repeats
+    own_part = lax.dynamic_slice_in_dim(tables, lax.axis_index("rep") * part, part, axis=1)
+    whole_table = lax.all_gather(own_part.astype(jnp.bfloat16), ("grp", "rep"), axis=1, tiled=True)
+    count_float = bag_counts.astype(jnp.float32)
+    anchor, hits = pool(slot_ids(row_ids, bag_counts), whole_table, count_float, dense_input)
     stream = anchor
     kept = []
     for layer_index in range(CROSS):
@@ -215,15 +260,14 @@
         bias_grads.insert(0, grad_bias)
     grad_anchor = grad_anchor + grad_stream
     grad_summed = (
-        grad_anchor[:, : pooled.shape[1] * pooled.shape[2]].reshape(pooled.shape) / count_float
+        grad_anchor[:, : features * width].reshape(samples, features, width) / count_float[:, :, None]
     ).astype(jnp.bfloat16)
-    late_rows, late_counts = (
-        lax.all_gather(row_ids, "grp", axis=0, tiled=True),
-        lax.all_gather(bag_counts, "grp", axis=0, tiled=True),
-    )
-    late_group = lax.all_gather(grad_summed, "grp", axis=0, tiled=True)
-    row_share = row_gradient(late_group, late_rows, late_counts, member * extent, extent)
-    table_grad = lax.psum(row_share.astype(jnp.bfloat16), "rep").astype(jnp.float32)
+    row_grad = jnp.einsum("fsr,sfe->fre", hits, grad_summed, preferred_element_type=jnp.float32)
+    row_share = row_grad.astype(jnp.bfloat16).reshape(features, group, repeats, part, width)
+    row_share = row_share.transpose(2, 1, 0, 3, 4)
+    row_share = lax.psum_scatter(row_share, "rep", scatter_dimension=0, tiled=True)[0]
+    row_share = lax.psum_scatter(row_share, "grp", scatter_dimension=0, tiled=True)[0]
+    table_grad = lax.all_gather(row_share, "rep", axis=1, tiled=True).astype(jnp.float32)
     stack_down = jnp.stack(down_grads)
     stack_up = jnp.stack(up_grads)
     share_down, share_up, share_one, share_two, share_three = (

time: 3240 us -> 1160 us (0.36)
  other arithmetic: 1620 us -> 77.1 us
  matrix products: 458 us -> 178 us
  local copies, waits for them, and re-layouts: 201 us -> 39.7 us
  waiting for transfers between devices: 870 us -> 733 us
  Pallas kernels: 0 us -> 66.6 us
    reduce_sum x40 -> x0, other arithmetic: 1510 us -> none  [multiplicity(): return jnp.sum(hits.astype(jnp.float32), axis=2).astype(jnp.bfloat16)]
    all_gather x3 -> x2, waiting for transfers between devices: 500 us -> 100 us  [the longest x1 87.9 us: on_device(): lax.all_gather(own_part.astype(jnp.bfloat16), ('grp', 'rep'), axis=1, til...]
    dot_general x40 -> x1, matrix products: 312 us -> 29.5 us  [on_device(): jnp.einsum('fsr,sfe->fre', hits, grad_summed, preferred_element_type=jnp....]
    dynamic_slice x160 -> x0, local copies, waits for them, and re-layouts: 118 us -> none  [the longest x128 101 us: row_gradient(): lax.scan(add_block, jnp.zeros((features, extent, width), jnp.float32), sh...]
    reduce_scatter x0 -> x2, waiting for transfers between devices: none -> 92.6 us  [the longest x1 53.2 us: on_device(): lax.psum_scatter(row_share, 'rep', scatter_dimension=0, tiled=True)[0]]
    pallas_call x0 -> x1, Pallas kernels: none -> 66.6 us  [pool(): pl.pallas_call(pool_kernel, grid=(features + 1,), in_specs=[pl.BlockSpec(...]
    psum x1 -> x0, waiting for transfers between devices: 59.8 us -> none  [on_device(): lax.psum(row_share.astype(jnp.bfloat16), 'rep').astype(jnp.float32)]
    all_gather x1, waiting for transfers between devices: 0.02 us -> 59 us  [on_device(): lax.all_gather(cross_up.astype(jnp.bfloat16), 'rep', axis=1, tiled=True)]
  transfers between devices with their start and end apart: 15 -> 15, of which waited for: 8 -> 14; matrix products, arithmetic and copies ran while one was open for 37% -> 12% of each run, Pallas kernels for 0% -> 6%
where the time goes in v1:
time: 1160 us; the launch traced here: 1150 us
  waiting for transfers between devices  733 us (63%)
  matrix products  178 us (15%)
  other arithmetic  77.1 us (7%)
  Pallas kernels  66.6 us (6%)
  blocking collectives  44.4 us (4%)
  local copies, waits for them, and re-layouts  39.7 us (3%)
  between operations  15.1 us (1%)
    psum x1, waiting for transfers between devices, on_device(): lax.psum(share_down.astype(jnp.bfloat16), 'grp').astype(jnp.float32)  99.5 us
    all_gather x1, waiting for transfers between devices, on_device(): lax.all_gather(own_part.astype(jnp.bfloat16), ('grp', 'rep'), axis=1, til...  87.9 us
    reduce_scatter x1, waiting for transfers between devices, on_device(): lax.psum_scatter(stack_down.astype(jnp.bfloat16), 'rep', scatter_dimensio...  85.7 us
    reduce_scatter x1, waiting for transfers between devices, on_device(): lax.psum_scatter(stack_up.astype(jnp.bfloat16), 'rep', scatter_dimension=...  85.6 us
    reduce_scatter x1, waiting for transfers between devices, on_device(): lax.psum_scatter(grad_one.astype(jnp.bfloat16), 'rep', scatter_dimension=...  69.3 us
    pallas_call x1, Pallas kernels, pool(): pl.pallas_call(pool_kernel, grid=(features + 1,), in_specs=[pl.BlockSpec(...  66.6 us
    all_gather x1, waiting for transfers between devices, on_device(): lax.all_gather(cross_up.astype(jnp.bfloat16), 'rep', axis=1, tiled=True)  59 us
    dot_general x9, matrix products, product(): return jnp.dot(left, right, preferred_element_type=jnp.float32)  58.5 us
  transfers between devices with their start and end apart: 15, of which 14 were waited for; matrix products, arithmetic and copies ran while one was open for 12% of the time, Pallas kernels for 6%

profile of v1, /device:TPU:0, one launch (start us, length us, event | category | flops | bytes accessed | tf_op | source)
XLA Modules:
  0.0 1154.9 jit_solution(1300246487376217329)
XLA Ops:
  9.5 3.0 convert_element_type.144
  19.4 4.2 copy.60
  23.6 4.6 reshape.70.ids_ref
  28.2 87.9 %all-gather.9.cloned.1.call-done.table_ref = bf16[26,2048,128]{2,1,0:T(8,128)(2,1)} async-done(((bf16[26,64,128]{2,1,0:T(8,128)(2,1)}), bf16[26,2048,128]{2,1,0:T(8,128)(2,1)}) %all-gather.9.cloned.1.call-update) | async-done | bytes 13631504 | tf_op jit(solution)/shard_map/all_gather | solution.py:221
  116.1 66.6 %shard_map.408 = (f32[512,3456]{1,0:T(8,128)}, bf16[26,512,2048]{2,1,0:T(8,128)(2,1)}) custom-call(s32[26,64,256]{2,1,0:T(8,128)S(1)} %reshape.70.ids_ref, bf16[26,2048,128]{2,1,0:T(8,128)(2,1)} %all-gather.9.cloned.1.call-done.table_ref, f32[512,26]{1,0:T(8,128)S(1)} %copy.61.counts_ref, f32[512,128]{1,0:T(8,128)S(1)} %copy-done), custom_call_target="tpu_custom_call" | custom-call | flops 20937965568 | bytes 76677120 | tf_op jit(solution)/shard_map/pallas_call | solution.py:119
  182.7 6.1 fusion.35
  188.8 59.0 %all-gather.13.cloned.1.call-done = bf16[3,512,3456]{2,1,0:T(8,128)(2,1)} async-done(((bf16[3,64,3456]{2,1,0:T(8,128)(2,1)}), bf16[3,512,3456]{2,1,0:T(8,128)(2,1)}) %all-gather.13.cloned.1.call-update) | async-done | bytes 10616848 | tf_op jit(solution)/shard_map/all_gather | solution.py:209
  247.8 6.2 fusion.20
  254.1 7.1 fusion.33
  262.2 6.9 fusion.19
  269.1 5.3 fusion.31
  274.5 10.5 add_convert_fusion
  285.0 14.0 %all-gather.15.cloned.1.call-done = bf16[3456,1024]{1,0:T(8,128)(2,1)} async-done(((bf16[432,1024]{1,0:T(8,128)(2,1)}), bf16[3456,1024]{1,0:T(8,128)(2,1)}) %all-gather.15.cloned.1.call-update) | async-done | bytes 7077904 | tf_op jit(solution)/shard_map/all_gather | solution.py:210
  299.0 9.4 fusion.72
  308.4 20.9 %all-gather.17.cloned.1.call-done = bf16[1024,1024]{1,0:T(8,128)(2,1)} async-done(((bf16[128,1024]{1,0:T(8,128)(2,1)}), bf16[1024,1024]{1,0:T(8,128)(2,1)}) %all-gather.17.cloned.1.call-update) | async-done | bytes 2097168 | tf_op jit(solution)/shard_map/all_gather | solution.py:211
  329.3 5.0 multiply_convert_fusion.5
  334.3 20.8 %all-gather.19.cloned.1.call-done = bf16[1024,512]{1,0:T(8,128)(2,1)} async-done(((bf16[128,512]{1,0:T(8,128)(2,1)}), bf16[1024,512]{1,0:T(8,128)(2,1)}) %all-gather.19.cloned.1.call-update) | async-done | bytes 1048592 | tf_op jit(solution)/shard_map/all_gather | solution.py:212
  365.6 9.6 convert_reduce_fusion
  375.2 7.9 fusion.30
  383.1 7.4 convert_reduce_fusion.1
  390.5 5.4 fusion.32
  396.0 8.1 convert_reduce_fusion.2
  404.1 5.4 fusion.34
  409.4 7.3 fusion.12
  416.7 19.1 %fusion.2 = f32[512,3328]{1,0:T(8,128)} fusion(f32[512,3456]{1,0:T(8,128)} %fusion.12, f32[512,3456]{1,0:T(8,128)} %copy-done.1, f32[512,3456]{1,0:T(8,128)} %get-tuple-element.82, f32[512,3456]{1,0:T(8,128)} %get-tuple-element.81, f32[512,3456]{1,0:T(8,128)} %get-tuple-element.75, f32[512,3456]{1,0:T(8,128)} %copy-done.2, f32[512,3456]{1,0:T(8,128)} %get-tuple-element.77), kind=kLoop, calls=%fused_computation.20 | loop fusion | flops 11927552 | bytes 54525952 | tf_op jit(solution)/shard_map/add | solution.py:261
  435.8 7.6 copy.62
  443.4 29.5 %convolution_convert_fusion = bf16[26,2048,128]{2,1,0:T(8,128)(2,1)} fusion(bf16[26,512,2048]{2,1,0:T(8,128)(2,1)} %get-tuple-element.25, f32[512,26,128]{0,2,1:T(8,128)} %bitcast.129, f32[512,26]{0,1:T(8,128)S(1)} %copy-done.44), kind=kOutput, calls=%fused_computation | convolution fusion | flops 6989545472 | bytes 75026432 | tf_op jit(solution)/shard_map/fsr,sfe->fre/dot_general | solution.py:265
  472.9 10.4 copy.69
  486.3 4.7 convolution_convert_fusion.8
  491.0 8.1 convolution_convert_fusion.1
  499.6 5.7 fusion.7
  509.6 4.8 pad_maximum_fusion
  514.5 4.4 fusion.10
  523.2 4.8 pad_maximum_fusion.1
  528.2 53.2 %reduce-scatter.8.cloned.1.call-done = bf16[1,4,26,64,128]{4,3,2,1,0:T(8,128)(2,1)} async-done(((bf16[8,4,26,64,128]{4,3,2,1,0:T(8,128)(2,1)}), bf16[1,4,26,64,128]{4,3,2,1,0:T(8,128)(2,1)}) %reduce-scatter.8.cloned.1.call-update) | async-done | bytes 1703952 | tf_op jit(solution)/shard_map/reduce_scatter | solution.py:268
  581.4 39.7 %reduce-scatter.20.cloned.1.call-done = bf16[128,512]{1,0:T(8,128)(2,1)} async-done(((bf16[1024,512]{1,0:T(8,128)(2,1)}), bf16[128,512]{1,0:T(8,128)(2,1)}) %reduce-scatter.20.cloned.1.call-update) | async-done | bytes 131088 | tf_op jit(solution)/shard_map/reduce_scatter | solution.py:286
  621.1 45.1 %reduce-scatter.18.cloned.1.call-done = bf16[128,1024]{1,0:T(8,128)(2,1)} async-done(((bf16[1024,1024]{1,0:T(8,128)(2,1)}), bf16[128,1024]{1,0:T(8,128)(2,1)}) %reduce-scatter.18.cloned.1.call-update) | async-done | bytes 262160 | tf_op jit(solution)/shard_map/reduce_scatter | solution.py:283
  666.3 69.3 %reduce-scatter.16.cloned.1.call-done = bf16[432,1024]{1,0:T(8,128)(2,1)} async-done(((bf16[3456,1024]{1,0:T(8,128)(2,1)}), bf16[432,1024]{1,0:T(8,128)(2,1)}) %reduce-scatter.16.cloned.1.call-update) | async-done | bytes 884752 | tf_op jit(solution)/shard_map/reduce_scatter | solution.py:280
  735.6 85.7 %reduce-scatter.12.cloned.1.call-done = bf16[3,432,512]{2,1,0:T(8,128)(2,1)} async-done(((bf16[3,3456,512]{2,1,0:T(8,128)(2,1)}), bf16[3,432,512]{2,1,0:T(8,128)(2,1)}) %reduce-scatter.12.cloned.1.call-update) | async-done | bytes 1327120 | tf_op jit(solution)/shard_map/reduce_scatter | solution.py:274
  821.3 85.6 %reduce-scatter.14.cloned.1.call-done = bf16[3,64,3456]{2,1,0:T(8,128)(2,1)} async-done(((bf16[3,512,3456]{2,1,0:T(8,128)(2,1)}), bf16[3,64,3456]{2,1,0:T(8,128)(2,1)}) %reduce-scatter.14.cloned.1.call-update) | async-done | bytes 1327120 | tf_op jit(solution)/shard_map/reduce_scatter | solution.py:277
  907.2 39.4 %reduce-scatter.10.cloned.1.call-done = bf16[1,26,64,128]{3,2,1,0:T(8,128)(2,1)} async-done(((bf16[4,26,64,128]{3,2,1,0:T(8,128)(2,1)}), bf16[1,26,64,128]{3,2,1,0:T(8,128)(2,1)}) %reduce-scatter.10.cloned.1.call-update) | async-done | bytes 426000 | tf_op jit(solution)/shard_map/reduce_scatter | solution.py:269
  951.7 44.4 %all-reduce.1 = (f32[]{:T(128)}, f32[13441]{0:T(1024)S(1)}) all-reduce(f32[]{:T(128)} %get-tuple-element.71, f32[13441]{0:T(1024)} %constant_dynamic-update-slice_fusion), channel_id=1, replica_groups=mesh['rep'=8,'grp'=4] {'rep','grp'}, use_global_device_ids=true, to_apply=%region_1.2 | all-reduce | flops 13442 | bytes 107536 | tf_op jit(solution)/shard_map/psum | solution.py:307
  997.6 99.5 %all-reduce.5.cloned.1.call-done = (bf16[3,432,512]{2,1,0:T(8,128)(2,1)}, bf16[3,64,3456]{2,1,0:T(8,128)(2,1)}, bf16[432,1024]{1,0:T(8,128)(2,1)}, bf16[128,1024]{1,0:T(8,128)(2,1)}, bf16[128,512]{1,0:T(8,128)(2,1)}) async-done(((bf16[3,432,512]{2,1,0:T(8,128)(2,1)}, bf16[3,64,3456]{2,1,0:T(8,128)(2,1)}, bf16[432,1024]{1,0:T(8,128)(2,1)}, bf16[128,1024]{1,0:T(8,128)(2,1)}, bf16[128,512]{1,0:T(8,128)(2,1)}), ...) | async-done | bytes 3932176 | tf_op jit(solution)/shard_map/psum | solution.py:291
  1101.9 4.7 multiply_subtract_fusion.2
  1107.9 5.1 multiply_subtract_fusion.1
  1114.4 4.6 multiply_subtract_fusion
  1119.0 12.3 %all-gather.21.cloned.1.call-done = bf16[1,26,512,128]{3,2,1,0:T(8,128)(2,1)} async-done(((bf16[1,26,64,128]{3,2,1,0:T(8,128)(2,1)}), bf16[1,26,512,128]{3,2,1,0:T(8,128)(2,1)}) %all-gather.21.cloned.1.call-update) | async-done | bytes 3407888 | tf_op jit(solution)/shard_map/all_gather | solution.py:270
  1131.3 16.9 %add_subtract_fusion = (f32[26,512,128]{2,1,0:T(8,128)}, f32[26,512,128]{2,1,0:T(8,128)}, f32[26,512,128]{2,1,0:T(8,128)}) fusion(f32[26,512,128]{2,1,0:T(8,128)} %param.29, bf16[1,26,512,128]{3,2,1,0:T(8,128)(2,1)} %all-gather.21.cloned.1.call-done, f32[26,512,128]{2,1,0:T(8,128)} %param.30, f32[26,512,128]{2,1,0:T(8,128)} %param.31), kind=kLoop, calls=%fused_computation.26 | loop fusion | flops 25559040 | bytes 44302336 | tf_op jit(solution)/shard_map/sub | solution.py:177
  (223 shorter events, 46.7 us)
Async XLA Ops:
  7.2 108.9 %all-gather.9.cloned.1.call-start = ((), (), s32[]{:S(2)}) async-start(), calls=%async_computation.7 | async-start | bytes 14057472 | tf_op jit(solution)/shard_map/all_gather | solution.py:221
  9.4 173.3 %all-gather.11.cloned.1.call-start = ((), (), s32[]{:S(2)}) async-start(), calls=%async_computation.8 | async-start | bytes 11943936 | tf_op jit(solution)/shard_map/all_gather | solution.py:208
  12.5 235.3 %all-gather.13.cloned.1.call-start = ((), (), s32[]{:S(2)}) async-start(), calls=%async_computation.9 | async-start | bytes 11943936 | tf_op jit(solution)/shard_map/all_gather | solution.py:209
  13.8 285.2 %all-gather.15.cloned.1.call-start = ((), (), s32[]{:S(2)}) async-start(), calls=%async_computation.10 | async-start | bytes 7962624 | tf_op jit(solution)/shard_map/all_gather | solution.py:210
  16.5 312.8 %all-gather.17.cloned.1.call-start = ((), (), s32[]{:S(2)}) async-start(), calls=%async_computation.11 | async-start | bytes 2359296 | tf_op jit(solution)/shard_map/all_gather | solution.py:211
  17.4 337.8 %all-gather.19.cloned.1.call-start = ((), (), s32[]{:S(2)}) async-start(), calls=%async_computation.12 | async-start | bytes 1179648 | tf_op jit(solution)/shard_map/all_gather | solution.py:212
  18.1 563.3 %reduce-scatter.8.cloned.1.call-start = ((), (), s32[]{:S(2)}) async-start(), calls=%async_computation.13 | async-start | bytes 15335424 | tf_op jit(solution)/shard_map/reduce_scatter | solution.py:268
  18.7 343.9 %copy-start.57 = (f32[1024]{0:T(1024)}, f32[1024]{0:T(1024)S(1)}, u32[]{:S(2)}) copy-start(f32[1024]{0:T(1024)S(1)} %get-tuple-element.67) | copy-start | bytes 12292
  23.6 92.5 %copy-start = (f32[512,128]{1,0:T(8,128)S(1)}, f32[512,128]{1,0:T(8,128)}, u32[]{:S(2)}) copy-start(f32[512,128]{1,0:T(8,128)} %dense_ref.1) | copy-start | bytes 786436
  188.8 65.2 %copy-start.15 = (bf16[512,512]{1,0:T(8,128)(2,1)}, bf16[512,512]{1,0:T(8,128)(2,1)S(1)}, u32[]{:S(2)}) copy-start(bf16[512,512]{1,0:T(8,128)(2,1)S(1)} %fusion.35) | copy-start | bytes 1572868
  254.1 7.1 copy-start.10
  254.1 20.4 %copy-start.1 = (f32[512,3456]{1,0:T(8,128)}, f32[512,3456]{1,0:T(8,128)S(1)}, u32[]{:S(2)}) copy-start(f32[512,3456]{1,0:T(8,128)S(1)} %get-tuple-element.73) | copy-start | bytes 21233668
  254.1 7.2 slice-start
  254.1 8.1 slice-start.1
  261.2 7.9 copy-start.21
  274.5 10.5 copy-start.23
  334.3 24.0 %copy-start.61 = (bf16[512,1024]{1,0:T(8,128)(2,1)}, bf16[512,1024]{1,0:T(8,128)(2,1)S(1)}, u32[]{:S(2)}) copy-start(bf16[512,1024]{1,0:T(8,128)(2,1)S(1)} %get-tuple-element.78) | copy-start | bytes 3145732
  365.4 9.9 copy-start.31
  375.2 7.9 copy-start.2
  383.1 7.4 copy-start.36
  395.9 8.1 copy-start.37
  409.4 7.3 copy-start.39
  435.8 7.6 copy-start.44
  483.3 137.9 %reduce-scatter.20.cloned.1.call-start = ((), (), s32[]{:S(2)}) async-start(), calls=%async_computation.19 | async-start | bytes 1179648 | tf_op jit(solution)/shard_map/reduce_scatter | solution.py:286
  486.2 180.0 %reduce-scatter.18.cloned.1.call-start = ((), (), s32[]{:S(2)}) async-start(), calls=%async_computation.18 | async-start | bytes 2359296 | tf_op jit(solution)/shard_map/reduce_scatter | solution.py:283
  491.0 244.6 %reduce-scatter.16.cloned.1.call-start = ((), (), s32[]{:S(2)}) async-start(), calls=%async_computation.17 | async-start | bytes 7962624 | tf_op jit(solution)/shard_map/reduce_scatter | solution.py:280
  499.1 6.2 copy-start.11
  499.1 322.2 %reduce-scatter.12.cloned.1.call-start = ((), (), s32[]{:S(2)}) async-start(), calls=%async_computation.15 | async-start | bytes 11943936 | tf_op jit(solution)/shard_map/reduce_scatter | solution.py:274
  499.6 7.9 slice-start.4
  514.4 392.5 %reduce-scatter.14.cloned.1.call-start = ((), (), s32[]{:S(2)}) async-start(), calls=%async_computation.16 | async-start | bytes 11943936 | tf_op jit(solution)/shard_map/reduce_scatter | solution.py:277
  528.1 418.6 %copy-start.49 = (f32[3456]{0:T(1024)S(1)}, f32[3456]{0:T(1024)}, u32[]{:S(2)}) copy-start(f32[3456]{0:T(1024)} %get-tuple-element.62) | copy-start | bytes 41476
  528.1 418.7 %copy-start.48 = (f32[3456]{0:T(1024)S(1)}, f32[3456]{0:T(1024)}, u32[]{:S(2)}) copy-start(f32[3456]{0:T(1024)} %get-tuple-element.58) | copy-start | bytes 41476
  528.1 418.8 %copy-start.56 = (f32[1024]{0:T(1024)S(1)}, f32[1024]{0:T(1024)}, u32[]{:S(2)}) copy-start(f32[1024]{0:T(1024)} %get-tuple-element.83) | copy-start | bytes 12292
  528.1 418.8 %copy-start.55 = (f32[1024]{0:T(1024)S(1)}, f32[1024]{0:T(1024)}, u32[]{:S(2)}) copy-start(f32[1024]{0:T(1024)} %get-tuple-element.85) | copy-start | bytes 12292
  528.1 418.8 %copy-start.52 = (f32[512]{0:T(512)S(1)}, f32[512]{0:T(512)}, u32[]{:S(2)}) copy-start(f32[512]{0:T(512)} %get-tuple-element.56) | copy-start | bytes 6148
  528.1 419.4 %copy-start.33 = (f32[512,512]{1,0:T(8,128)S(1)}, f32[512,512]{1,0:T(8,128)}, u32[]{:S(2)}) copy-start(f32[512,512]{1,0:T(8,128)} %copy-done.32) | copy-start | bytes 3145732
  528.1 419.4 %copy-start.54 = (f32[512]{0:T(512)S(1)}, f32[512]{0:T(512)}, u32[]{:S(2)}) copy-start(f32[512]{0:T(512)} %copy-done.53) | copy-start | bytes 6148
  528.1 418.5 %reduce-scatter.10.cloned.1.call-start = ((), (), s32[]{:S(2)}) async-start(), calls=%async_computation.14 | async-start | bytes 2129920 | tf_op jit(solution)/shard_map/reduce_scatter | solution.py:269
  581.4 515.8 %all-reduce.5.cloned.1.call-start = ((), (), s32[]{:S(2)}) async-start(), calls=%async_computation.21 | async-start | bytes 7864320 | tf_op jit(solution)/shard_map/psum | solution.py:291
  907.0 89.2 %copy-start.47 = (f32[13441]{0:T(1024)S(1)}, f32[13441]{0:T(1024)}, u32[]{:S(2)}) copy-start(f32[13441]{0:T(1024)} %param.47) | copy-start | bytes 161296
  907.0 89.2 %copy-start.50 = (f32[13441]{0:T(1024)S(1)}, f32[13441]{0:T(1024)}, u32[]{:S(2)}) copy-start(f32[13441]{0:T(1024)} %param.48) | copy-start | bytes 161296
  907.0 190.2 %copy-start.35 = (f32[128,512]{1,0:T(8,128)S(1)}, f32[128,512]{1,0:T(8,128)}, u32[]{:S(2)}) copy-start(f32[128,512]{1,0:T(8,128)} %param.44) | copy-start | bytes 786436
  907.0 190.2 %copy-start.45 = (f32[128,512]{1,0:T(8,128)S(1)}, f32[128,512]{1,0:T(8,128)}, u32[]{:S(2)}) copy-start(f32[128,512]{1,0:T(8,128)} %param.45) | copy-start | bytes 786436
  907.0 224.3 %all-gather.21.cloned.1.call-start = ((), (), s32[]{:S(2)}) async-start(), calls=%async_computation.20 | async-start | bytes 3833856 | tf_op jit(solution)/shard_map/all_gather | solution.py:270
  946.7 152.7 %copy-start.25 = (f32[128,1024]{1,0:T(8,128)S(1)}, f32[128,1024]{1,0:T(8,128)}, u32[]{:S(2)}) copy-start(f32[128,1024]{1,0:T(8,128)} %param.41) | copy-start | bytes 1572868
  946.7 152.7 %copy-start.41 = (f32[128,1024]{1,0:T(8,128)S(1)}, f32[128,1024]{1,0:T(8,128)}, u32[]{:S(2)}) copy-start(f32[128,1024]{1,0:T(8,128)} %param.42) | copy-start | bytes 1572868
  948.4 153.5 %copy-start.12 = (f32[432,1024]{1,0:T(8,128)S(1)}, f32[432,1024]{1,0:T(8,128)}, u32[]{:S(2)}) copy-start(f32[432,1024]{1,0:T(8,128)} %param.38) | copy-start | bytes 5308420
  1107.9 6.5 copy-start.29
  (41 other events, 161.0 us)
Sparse Core Ops, SparseCore 0:
  11.5 104.5 all-gather.8
  118.5 62.9 all-gather.10
  184.0 63.8 all-gather.12
  250.2 48.8 all-gather.14
  301.4 27.8 all-gather.16
  331.6 23.4 all-gather.18
  483.4 97.9 reduce-scatter.7
  585.1 35.9 reduce-scatter.19
  625.0 41.2 reduce-scatter.17
  670.1 65.4 reduce-scatter.15
  739.1 82.1 reduce-scatter.11
  824.7 82.2 reduce-scatter.13
  909.2 37.3 reduce-scatter.9
  949.2 147.8 all-reduce.4
  1098.9 32.3 all-gather.20

commit v2 on v1

v2 whole, which is shorter than its diff:
```python
import functools

import jax
import jax.numpy as jnp
from jax import lax
from jax.experimental import pallas as pl
from jax.experimental.pallas import tpu as pltpu
from jax.sharding import PartitionSpec as P

D_IN = 3456
RANK = 512
CROSS = 3
H1 = 1024
H2 = 1024
H3 = 512
STEP = 10
GROUP = 8
SLOTS = 32
LOW = 128
VMEM_BYTES = 60 * 2**20


BETA_ONE = 0.9
BETA_TWO = 0.999
EPSILON = 1e-12
DECAY = 0.01


def split_smalls(smalls):
    extents = [CROSS * D_IN, H1, H2, H3, H3, 1]
    pieces = []
    offset = 0
    for extent in extents:
        pieces.append(smalls[offset : offset + extent])
        offset = offset + extent
    return (pieces[0].reshape(CROSS, D_IN), pieces[1], pieces[2], pieces[3], pieces[4], pieces[5])


def product(left, right):
    return jnp.dot(left, right, preferred_element_type=jnp.float32)


def left_product(left, right):
    return lax.dot_general(
        left, right, (((0,), (0,)), ((), ())), preferred_element_type=jnp.float32
    )


def right_product(left, right):
    return lax.dot_general(
        left, right, (((1,), (1,)), ((), ())), preferred_element_type=jnp.float32
    )


def silu_slope(value):
    logistic = jax.nn.sigmoid(value)
    return logistic * (1.0 + value * (1.0 - logistic))


def slot_ids(row_ids, bag_counts):
    samples, features, slots = row_ids.shape
    live = lax.broadcasted_iota(jnp.int32, row_ids.shape, 2) < bag_counts[:, :, None]
    ids = jnp.pad(jnp.where(live, row_ids, -1), ((0, 0), (0, 0), (0, SLOTS - slots)), constant_values=-1)
    return ids.transpose(1, 0, 2).reshape(features, samples // GROUP, GROUP * SLOTS)


def one_hot(codes, levels):
    rows = jnp.broadcast_to(codes, (16, codes.shape[1])).astype(jnp.bfloat16)
    wanted = lax.broadcasted_iota(jnp.int32, (levels, codes.shape[1]), 0).astype(jnp.float32).astype(jnp.bfloat16)
    hits = jnp.concatenate([rows] * (levels // 16), axis=0) == wanted
    return jnp.where(hits, jnp.ones((), jnp.bfloat16), jnp.zeros((), jnp.bfloat16)).astype(jnp.float8_e4m3fn)


def count_kernel(earlier, ids_ref, *refs):
    hits_ref, code_ref = refs[earlier:]
    samples = hits_ref.shape[1]
    highs = hits_ref.shape[2] // LOW
    ids = ids_ref[0]
    member = lax.broadcasted_iota(jnp.int32, ids.shape, 1) // SLOTS
    code_ref[0] = ((ids >> 7) * GROUP + member).astype(jnp.float32)
    code_ref[1] = (ids & (LOW - 1)).astype(jnp.float32)

    def add_groups(step, unused):
        first = pl.multiple_of(step * 8, 8)
        high_codes = code_ref[0, pl.ds(first, 8), :]
        low_codes = code_ref[1, pl.ds(first, 8), :]
        for pair in range(4):
            products = []
            for row in (2 * pair, 2 * pair + 1):
                high_hits = one_hot(high_codes[row : row + 1], highs * GROUP)
                low_hits = one_hot(low_codes[row : row + 1], LOW)
                products.append(right_product(high_hits, low_hits))
            start = pl.multiple_of(step * 8 * GROUP + pair * 2 * GROUP, 2 * GROUP)
            for high in range(highs):
                part = slice(high * GROUP, (high + 1) * GROUP)
                tile = jnp.concatenate([products[0][part], products[1][part]], axis=0)
                hits_ref[0, pl.ds(start, 2 * GROUP), high * LOW : (high + 1) * LOW] = tile.astype(
                    jnp.bfloat16
                )
        return unused

    lax.fori_loop(0, samples // (8 * GROUP), add_groups, 0)


def count(ids, rows, pieces):
    features, groups, slots = ids.shape
    samples = groups * GROUP
    cuts = [features * piece // pieces for piece in range(pieces + 1)]
    hits = None
    for first, last in zip(cuts[:-1], cuts[1:]):
        earlier = [] if hits is None else [hits]
        hits = pl.pallas_call(
            functools.partial(count_kernel, len(earlier)),
            grid=(last - first,),
            in_specs=[pl.BlockSpec((1, groups, slots), functools.partial(shifted_block, first))]
            + [pl.BlockSpec(memory_space=pl.ANY)] * len(earlier),
            out_specs=pl.BlockSpec((1, samples, rows), functools.partial(shifted_block, first)),
            out_shape=jax.ShapeDtypeStruct((features, samples, rows), jnp.bfloat16),
            input_output_aliases={1: 0} if earlier else {},
            scratch_shapes=[pltpu.VMEM((2, groups, slots), jnp.float32)],
            compiler_params=pltpu.CompilerParams(vmem_limit_bytes=VMEM_BYTES),
            cost_estimate=pl.CostEstimate(
                flops=(last - first) * samples * rows * 2048,
                bytes_accessed=2 * (last - first) * rows * samples,
                transcendentals=0,
            ),
        )(ids, *earlier)
    return hits


def shifted_block(first, feature):
    return (feature + first, 0, 0)


def feature_counts(counts_ref, feature):
    lanes = lax.broadcasted_iota(jnp.int32, counts_ref.shape, 1)
    return jnp.sum(jnp.where(lanes == feature, counts_ref[...], 0.0), axis=1, keepdims=True)


def pool_kernel(
    place_ref, hits_ref, own_a, other_a, own_b, other_b, counts_ref, dense_ref, anchor_ref, table_ref, *, keys, half
):
    feature = pl.program_id(0)
    features = pl.num_programs(0) - 1
    mine = place_ref[0]
    member = place_ref[1]
    group = table_ref.shape[0]

    def assemble(own_ref, other_ref, order):
        for position, key in enumerate(order):
            for step in range(group):
                row = lax.rem(member + group - step, group)
                table_ref[row, mine ^ key] = own_ref[position, step, 0]
                table_ref[row, mine ^ (key ^ 1)] = other_ref[position, step, 0]

    @pl.when(feature < half)
    def _():
        assemble(own_a, other_a, keys[0])

    @pl.when((feature >= half) & (feature < features))
    def _():
        assemble(own_b, other_b, keys[1])

    @pl.when(feature < features)
    def _():
        table = table_ref[...].reshape(-1, table_ref.shape[-1])
        anchor_ref[...] = product(hits_ref[0], table) / feature_counts(counts_ref, feature)

    @pl.when(feature == features)
    def _():
        anchor_ref[...] = dense_ref[...]


def pool(hits, first_half, second_half, keys, count_float, dense_input):
    features, samples, rows = hits.shape
    last = features - 1
    half = first_half[0].shape[2]
    halves, group, unused, part, width = first_half[0].shape
    block = (halves, group, 1, part, width)
    low_block = pl.BlockSpec(block, lambda f, place: (0, 0, jnp.minimum(f, half - 1), 0, 0))
    high_block = pl.BlockSpec(block, lambda f, place: (0, 0, jnp.clip(f - half, 0, last - half), 0, 0))
    place = jnp.stack([lax.axis_index("rep"), lax.axis_index("grp")]).astype(jnp.int32)
    return pl.pallas_call(
        functools.partial(pool_kernel, keys=keys, half=half),
        grid_spec=pltpu.PrefetchScalarGridSpec(
            num_scalar_prefetch=1,
            grid=(features + 1,),
            in_specs=[
                pl.BlockSpec((1, samples, rows), lambda f, place: (jnp.minimum(f, last), 0, 0)),
                low_block,
                low_block,
                high_block,
                high_block,
                pl.BlockSpec((samples, features), lambda f, place: (0, 0)),
                pl.BlockSpec((samples, width), lambda f, place: (0, 0)),
            ],
            out_specs=pl.BlockSpec((samples, width), lambda f, place: (0, f)),
            scratch_shapes=[pltpu.VMEM((group, 2 * halves, part, width), jnp.bfloat16)],
        ),
        out_shape=jax.ShapeDtypeStruct((samples, (features + 1) * width), jnp.float32),
        compiler_params=pltpu.CompilerParams(vmem_limit_bytes=VMEM_BYTES),
        cost_estimate=pl.CostEstimate(
            flops=2 * samples * features * rows * width,
            bytes_accessed=2 * features * rows * (samples + width) + 4 * samples * features * width,
            transcendentals=0,
        ),
    )(place, hits, *first_half, *second_half, count_float, dense_input)


def cross_forward_kernel(
    anchor_in, down_ref, up_ref, bias_ref, low_ref, narrow_ref, last_ref, anchor_ref, stream_ref, sum_ref
):
    layer, phase, block = pl.program_id(0), pl.program_id(1), pl.program_id(2)
    layers = pl.num_programs(0)

    @pl.when((layer == 0) & (phase == 0))
    def _():
        anchor_ref[block] = anchor_in[...]
        stream_ref[block] = anchor_in[...]

    @pl.when(phase == 0)
    def _():
        low = stream_ref[block].astype(jnp.bfloat16)
        low_ref[0] = low
        part = product(low, down_ref[0])

        @pl.when(block == 0)
        def _():
            sum_ref[...] = part

        @pl.when(block > 0)
        def _():
            sum_ref[...] += part

    @pl.when((phase == 1) & (block == 0))
    def _():
        narrow_ref[0] = sum_ref[...].astype(jnp.bfloat16)

    @pl.when(phase == 1)
    def _():
        factor = product(narrow_ref[0], up_ref[0]) + bias_ref[0]
        stream = anchor_ref[block] * factor + stream_ref[block]
        stream_ref[block] = stream

        @pl.when(layer == layers - 1)
        def _():
            last_ref[...] = stream.astype(jnp.bfloat16)


def cross_forward(anchor, down, up, bias):
    samples, width = anchor.shape
    layers, unused, rank = down.shape
    blocks = 3
    piece = width // blocks
    final = blocks - 1
    return pl.pallas_call(
        cross_forward_kernel,
        grid=(layers, 2, blocks),
        in_specs=[
            pl.BlockSpec((samples, piece), lambda l, p, j: (0, jnp.where((l == 0) & (p == 0), j, final))),
            pl.BlockSpec((1, piece, rank), lambda l, p, j: (l, jnp.where(p == 0, j, final), 0)),
            pl.BlockSpec((1, rank, piece), lambda l, p, j: (l, 0, jnp.where(p == 1, j, 0))),
            pl.BlockSpec((1, 1, piece), lambda l, p, j: (l, 0, jnp.where(p == 1, j, 0))),
        ],
        out_specs=[
            pl.BlockSpec((1, samples, piece), lambda l, p, j: (l, 0, jnp.where(p == 0, j, final))),
            pl.BlockSpec((1, samples, rank), lambda l, p, j: (l, 0, 0)),
            pl.BlockSpec((samples, piece), lambda l, p, j: (0, jnp.where((l == layers - 1) & (p == 1), j, 0))),
        ],
        out_shape=[
            jax.ShapeDtypeStruct((layers, samples, width), jnp.bfloat16),
            jax.ShapeDtypeStruct((layers, samples, rank), jnp.bfloat16),
            jax.ShapeDtypeStruct((samples, width), jnp.bfloat16),
        ],
        scratch_shapes=[
            pltpu.VMEM((blocks, samples, piece), jnp.float32),
            pltpu.VMEM((blocks, samples, piece), jnp.float32),
            pltpu.VMEM((samples, rank), jnp.float32),
        ],
        compiler_params=pltpu.CompilerParams(vmem_limit_bytes=VMEM_BYTES),
        cost_estimate=pl.CostEstimate(
            flops=4 * layers * samples * width * rank,
            bytes_accessed=4 * layers * width * (rank + samples) + 4 * samples * width,
            transcendentals=0,
        ),
    )(anchor, down, up, bias.reshape(layers, 1, width))


def head_kernel(
    input_ref,
    one_ref,
    late_ref,
    bias_one,
    bias_two,
    bias_three,
    head_ref,
    head_bias,
    target_ref,
    loss_ref,
    grad_head,
    grad_head_bias,
    grad_bias_one,
    grad_bias_two,
    grad_bias_three,
    grad_one,
    grad_late,
    grad_stream,
    sum_ref,
    back_ref,
    *,
    total
):
    step = pl.program_id(0)
    blocks = pl.num_programs(0) // 2

    @pl.when(step < blocks)
    def _():
        part = product(input_ref[...], one_ref[...])

        @pl.when(step == 0)
        def _():
            sum_ref[...] = part

        @pl.when(step > 0)
        def _():
            sum_ref[...] += part

    @pl.when(step == blocks)
    def _():
        pre_one = sum_ref[...] + bias_one[...]
        in_two = jax.nn.silu(pre_one).astype(jnp.bfloat16)
        two = late_ref[:, :H2]
        three = late_ref[:, H2:]
        pre_two = product(in_two, two) + bias_two[...]
        in_three = jax.nn.silu(pre_two).astype(jnp.bfloat16)
        pre_three = product(in_three, three) + bias_three[...]
        top = jax.nn.silu(pre_three)
        head = head_ref[...]
        target = target_ref[...]
        logit = jnp.sum(top * head, axis=1, keepdims=True) + head_bias[...]
        losses = jnp.maximum(logit, 0.0) + jnp.log1p(jnp.exp(-jnp.abs(logit))) - target * logit
        loss_ref[...] = jnp.sum(losses, axis=0, keepdims=True)
        grad_logit = (jax.nn.sigmoid(logit) - target) / total
        grad_head[...] = jnp.sum(grad_logit * top, axis=0, keepdims=True)
        grad_head_bias[...] = jnp.sum(grad_logit, axis=0, keepdims=True)
        back = (grad_logit * head * silu_slope(pre_three)).astype(jnp.bfloat16)
        grad_bias_three[...] = jnp.sum(back.astype(jnp.float32), axis=0, keepdims=True)
        grad_late[:, H2:] = left_product(in_three, back).astype(jnp.bfloat16)
        back = (right_product(back, three) * silu_slope(pre_two)).astype(jnp.bfloat16)
        grad_bias_two[...] = jnp.sum(back.astype(jnp.float32), axis=0, keepdims=True)
        grad_late[:, :H2] = left_product(in_two, back).astype(jnp.bfloat16)
        back = (right_product(back, two) * silu_slope(pre_one)).astype(jnp.bfloat16)
        grad_bias_one[...] = jnp.sum(back.astype(jnp.float32), axis=0, keepdims=True)
        back_ref[...] = back

    @pl.when(step >= blocks)
    def _():
        grad_one[...] = left_product(input_ref[...], back_ref[...]).astype(jnp.bfloat16)
        grad_stream[...] = right_product(back_ref[...], one_ref[...])


def head(inputs, one, late, biases, head_weight, head_bias, target, total):
    samples, width = inputs.shape
    blocks = 3
    piece = width // blocks

    def whole(shape):
        return pl.BlockSpec(shape, lambda s: (0,) * len(shape))

    rows = [bias.reshape(1, -1) for bias in biases] + [head_weight.reshape(1, -1), head_bias.reshape(1, 1)]
    small = [(1, 1), (1, H3), (1, 1), (1, H1), (1, H2), (1, H3)]
    return pl.pallas_call(
        functools.partial(head_kernel, total=total),
        grid=(2 * blocks,),
        in_specs=[
            pl.BlockSpec((samples, piece), lambda s: (0, lax.rem(s, blocks))),
            pl.BlockSpec((piece, H1), lambda s: (lax.rem(s, blocks), 0)),
            whole(late.shape),
        ]
        + [whole(row.shape) for row in rows]
        + [whole((samples, 1))],
        out_specs=[whole(shape) for shape in small]
        + [
            pl.BlockSpec((piece, H1), lambda s: (jnp.maximum(s - blocks, 0), 0)),
            whole(late.shape),
            pl.BlockSpec((samples, piece), lambda s: (0, jnp.maximum(s - blocks, 0))),
        ],
        out_shape=[jax.ShapeDtypeStruct(shape, jnp.float32) for shape in small]
        + [
            jax.ShapeDtypeStruct(one.shape, jnp.bfloat16),
            jax.ShapeDtypeStruct(late.shape, jnp.bfloat16),
            jax.ShapeDtypeStruct((samples, width), jnp.float32),
        ],
        scratch_shapes=[pltpu.VMEM((samples, H1), jnp.float32), pltpu.VMEM((samples, H1), jnp.bfloat16)],
        compiler_params=pltpu.CompilerParams(vmem_limit_bytes=VMEM_BYTES),
        cost_estimate=pl.CostEstimate(
            flops=6 * samples * (width * H1 + H1 * H2 + H2 * H3),
            bytes_accessed=6 * width * H1 + 8 * samples * width,
            transcendentals=8 * samples * (H1 + H2 + H3),
        ),
    )(inputs, one, late, *rows, target)


def cross_backward_kernel(
    core_ref,
    anchor_in,
    grad_in,
    low_ref,
    narrow_ref,
    down_ref,
    up_ref,
    bias_ref,
    counts_ref,
    send_ref,
    keep_ref,
    grad_down,
    grad_bias,
    grad_summed,
    anchor_ref,
    stream_ref,
    total_ref,
    sum_ref,
    back_ref,
    both_ref,
):
    layer, phase, block = pl.program_id(0), pl.program_id(1), pl.program_id(2)
    layers = pl.num_programs(0)

    @pl.when((layer == 0) & (phase == 0))
    def _():
        anchor_ref[block] = anchor_in[...]
        stream_ref[block] = grad_in[...]
        total_ref[block] = jnp.zeros(grad_in.shape, jnp.float32)

    @pl.when(phase == 0)
    def _():
        grad_next = stream_ref[block]
        grad_factor = (anchor_ref[block] * grad_next).astype(jnp.bfloat16)
        grad_bias[0] = jnp.sum(grad_factor.astype(jnp.float32), axis=0, keepdims=True)
        narrow = narrow_ref[0]
        both_ref[...] = left_product(narrow, grad_factor).astype(jnp.bfloat16).reshape(both_ref.shape)
        core = core_ref[0]
        send_ref[0] = both_ref[:, 1 - core]
        keep_ref[0] = both_ref[:, core]
        factor = product(narrow, up_ref[0]) + bias_ref[0]
        total_ref[block] += factor * grad_next
        part = right_product(grad_factor, up_ref[0])

        @pl.when(block == 0)
        def _():
            sum_ref[...] = part

        @pl.when(block > 0)
        def _():
            sum_ref[...] += part

    @pl.when((phase == 1) & (block == 0))
    def _():
        back_ref[...] = sum_ref[...].astype(jnp.bfloat16)

    @pl.when(phase == 1)
    def _():
        back = back_ref[...]
        grad_down[0] = left_product(low_ref[0], back).astype(jnp.bfloat16)
        grad_stream = stream_ref[block] + right_product(back, down_ref[0])
        stream_ref[block] = grad_stream

        @pl.when(layer == layers - 1)
        def _():
            features = grad_stream.shape[1] // LOW
            total = total_ref[block] + grad_stream
            for index in range(features):
                counts = jnp.maximum(feature_counts(counts_ref, block * features + index), 1.0)
                part = slice(index * LOW, (index + 1) * LOW)
                grad_summed[:, part] = (total[:, part] / counts).astype(jnp.bfloat16)


def cross_backward(anchor, grad_stream, lows, narrows, down, up, bias, count_float, core, repeats):
    samples, width = anchor.shape
    layers, unused, rank = down.shape
    blocks = 3
    piece = width // blocks
    final = blocks - 1
    share = rank // repeats

    def first_pass(l, p, j, core):
        return (0, jnp.where((l == 0) & (p == 0), j, final))

    def up_block(l, p, j, core):
        return (layers - 1 - l, 0, jnp.where(p == 0, j, final))

    def low_block(l, p, j, core):
        return (layers - 1 - l, 0, jnp.where(p == 1, j, 0))

    def down_block(l, p, j, core):
        return (layers - 1 - l, jnp.where(p == 1, j, 0), 0)

    half = jax.ShapeDtypeStruct((layers, repeats // 2, share, width), jnp.bfloat16)
    half_spec = pl.BlockSpec(
        (1, repeats // 2, share, piece),
        lambda l, p, j, core: (layers - 1 - l, 0, 0, jnp.where(p == 0, j, final)),
    )
    return pl.pallas_call(
        cross_backward_kernel,
        grid_spec=pltpu.PrefetchScalarGridSpec(
            num_scalar_prefetch=1,
            grid=(layers, 2, blocks),
            in_specs=[
                pl.BlockSpec((samples, piece), first_pass),
                pl.BlockSpec((samples, piece), first_pass),
                pl.BlockSpec((1, samples, piece), low_block),
                pl.BlockSpec((1, samples, rank), lambda l, p, j, core: (layers - 1 - l, 0, 0)),
                pl.BlockSpec((1, piece, rank), down_block),
                pl.BlockSpec((1, rank, piece), up_block),
                pl.BlockSpec((1, 1, piece), up_block),
                pl.BlockSpec(count_float.shape, lambda l, p, j, core: (0, 0)),
            ],
            out_specs=[
                half_spec,
                half_spec,
                pl.BlockSpec((1, piece, rank), down_block),
                pl.BlockSpec((1, 1, piece), up_block),
                pl.BlockSpec(
                    (samples, piece),
                    lambda l, p, j, core: (0, jnp.where((l == layers - 1) & (p == 1), j, 0)),
                ),
            ],
            scratch_shapes=[
                pltpu.VMEM((blocks, samples, piece), jnp.float32),
                pltpu.VMEM((blocks, samples, piece), jnp.float32),
                pltpu.VMEM((blocks, samples, piece), jnp.float32),
                pltpu.VMEM((samples, rank), jnp.float32),
                pltpu.VMEM((samples, rank), jnp.bfloat16),
                pltpu.VMEM((repeats // 2, 2, share, piece), jnp.bfloat16),
            ],
        ),
        out_shape=[
            half,
            half,
            jax.ShapeDtypeStruct(down.shape, jnp.bfloat16),
            jax.ShapeDtypeStruct((layers, 1, width), jnp.float32),
            jax.ShapeDtypeStruct((samples, width), jnp.bfloat16),
        ],
        compiler_params=pltpu.CompilerParams(vmem_limit_bytes=VMEM_BYTES),
        cost_estimate=pl.CostEstimate(
            flops=10 * layers * samples * width * rank,
            bytes_accessed=layers * width * (8 * rank + 2 * samples) + 10 * samples * width,
            transcendentals=0,
        ),
    )(core, anchor, grad_stream, lows, narrows, down, up, bias.reshape(layers, 1, width), count_float)


def row_kernel(core_ref, hits_ref, grad_ref, send_ref, keep_ref, both_ref):
    both_ref[...] = left_product(hits_ref[0], grad_ref[...]).astype(jnp.bfloat16).reshape(both_ref.shape)
    core = core_ref[0]
    send_ref[0] = both_ref[:, 1 - core]
    keep_ref[0] = both_ref[:, core]


def row_gradient(hits, grad_summed, first, features, group, core):
    unused, samples, rows = hits.shape
    half = rows // group // 2
    shape = jax.ShapeDtypeStruct((features, group, half, LOW), jnp.bfloat16)
    spec = pl.BlockSpec((1, group, half, LOW), lambda f, core: (f, 0, 0, 0))
    return pl.pallas_call(
        row_kernel,
        grid_spec=pltpu.PrefetchScalarGridSpec(
            num_scalar_prefetch=1,
            grid=(features,),
            in_specs=[
                pl.BlockSpec((1, samples, rows), lambda f, core: (f + first, 0, 0)),
                pl.BlockSpec((samples, LOW), lambda f, core: (0, f + first)),
            ],
            out_specs=[spec, spec],
            scratch_shapes=[pltpu.VMEM((group, 2, half, LOW), jnp.bfloat16)],
        ),
        out_shape=[shape, shape],
        compiler_params=pltpu.CompilerParams(vmem_limit_bytes=VMEM_BYTES),
        cost_estimate=pl.CostEstimate(
            flops=8 * samples * features * rows * LOW,
            bytes_accessed=2 * features * rows * (samples + LOW),
            transcendentals=0,
        ),
    )(core, hits, grad_summed)


def flip(value, bit):
    return lax.ppermute(value, "rep", [(i, i ^ bit) for i in range(lax.axis_size("rep"))])


def ring(value):
    size = lax.axis_size("grp")
    return lax.ppermute(value, "grp", [(i, (i + 1) % size) for i in range(size)])


def across():
    return [1 << i for i in range(1, lax.axis_size("rep").bit_length() - 1)]


def gather_across(value, order):
    keys = [0]
    for bit in order:
        value = jnp.concatenate([value, flip(value, bit)], axis=0)
        keys = keys + [key ^ bit for key in keys]
    return value, keys


def place(value, keys, axis, index_of):
    mine = lax.axis_index("rep")
    extent = value.shape[axis + 1]
    shape = list(value.shape[1:])
    shape[axis] = extent * len(keys)
    whole = jnp.zeros(shape, value.dtype)
    for position, key in enumerate(keys):
        whole = lax.dynamic_update_slice_in_dim(whole, value[position], index_of(mine ^ key) * extent, axis)
    return whole


def scatter_pair(keep, received, bits, order, axis):
    left = list(bits)
    for bit in order:
        position = axis + left.index(bit)
        mine = (lax.axis_index("rep") // bit) % 2
        send = lax.dynamic_index_in_dim(keep, 1 - mine, position, keepdims=False) + lax.dynamic_index_in_dim(
            received, 1 - mine, position, keepdims=False
        )
        keep = lax.dynamic_index_in_dim(keep, mine, position, keepdims=False) + lax.dynamic_index_in_dim(
            received, mine, position, keepdims=False
        )
        received = flip(send, bit)
        left.remove(bit)
    return keep + received


def ring_scatter(chunks):
    size = lax.axis_size("grp")
    mine = lax.axis_index("grp")
    value = lax.dynamic_index_in_dim(chunks, (mine + size - 1) % size, 0, keepdims=False)
    for step in range(1, size):
        own = lax.dynamic_index_in_dim(chunks, (mine + 2 * size - 1 - step) % size, 0, keepdims=False)
        value = own + ring(value)
    return value


def ring_gather(value):
    size = lax.axis_size("grp")
    mine = lax.axis_index("grp")
    whole = jnp.zeros((size,) + value.shape, value.dtype)
    for step in range(size):
        whole = lax.dynamic_update_index_in_dim(whole, value, (mine + size - step) % size, 0)
        if step < size - 1:
            value = ring(value)
    return whole


def sum_groups(shares):
    size = lax.axis_size("grp")
    flat = [share.reshape(size, -1, LOW) for share in shares]
    total = ring_gather(ring_scatter(jnp.concatenate(flat, axis=1)))
    results = []
    offset = 0
    for share, part in zip(shares, flat):
        piece = total[:, offset : offset + part.shape[1]]
        results.append(piece.reshape(share.shape).astype(jnp.float32))
        offset = offset + part.shape[1]
    return results


def sum_all(value):
    for bit in [1] + across():
        value = value + flip(value, bit)
    size = lax.axis_size("grp")
    bit = 1
    while bit < size:
        value = value + lax.ppermute(value, "grp", [(i, i ^ bit) for i in range(size)])
        bit = 2 * bit
    return value


def adamw(weight, grad, first, second, rate):
    first = BETA_ONE * first + (1.0 - BETA_ONE) * grad
    second = BETA_TWO * second + (1.0 - BETA_TWO) * grad * grad
    corr_one = 1.0 - BETA_ONE**STEP
    corr_two = 1.0 - BETA_TWO**STEP
    moved = first / corr_one / (jnp.sqrt(second / corr_two) + EPSILON) + DECAY * weight
    return (weight - rate * moved, first, second)


def on_device(
    row_ids,
    bag_counts,
    labels,
    dense_input,
    tables,
    table_first,
    table_second,
    cross_down,
    down_first,
    down_second,
    cross_up,
    up_first,
    up_second,
    hidden_one,
    one_first,
    one_second,
    hidden_two,
    two_first,
    two_second,
    hidden_three,
    three_first,
    three_second,
    smalls,
    small_first,
    small_second,
):
    up_down = across()
    down_up = up_down[::-1]
    down_all = lax.all_gather(cross_down.astype(jnp.bfloat16), "rep", axis=1, tiled=True)
    up_all = lax.all_gather(cross_up.astype(jnp.bfloat16), "rep", axis=1, tiled=True)
    one_all = lax.all_gather(hidden_one.astype(jnp.bfloat16), "rep", axis=0, tiled=True)
    cross_bias, bias_one, bias_two, bias_three, head_weight, head_bias = split_smalls(smalls)
    group = lax.axis_size("grp")
    samples = row_ids.shape[0]
    repeats = lax.axis_size("rep")
    features, extent, width = tables.shape
    part = extent // repeats
    own_part = lax.dynamic_slice_in_dim(tables, lax.axis_index("rep") * part, part, axis=1)
    own_parts = [own_part.astype(jnp.bfloat16)]
    for step in range(group - 1):
        own_parts.append(ring(own_parts[-1]))
    half = features // 2
    spans = ((0, half, up_down), (half, features, down_up))
    table_halves = []
    table_keys = []
    for first, last, order in spans:
        rows = jnp.stack([piece[first:last] for piece in own_parts])[None]
        rows, keys = gather_across(rows, order)
        table_halves.append((rows, flip(rows, 1)))
        table_keys.append(keys)
    late = jnp.concatenate([hidden_two, hidden_three], axis=1).astype(jnp.bfloat16)
    late_all = place(*gather_across(late[None], up_down + [1]), 0, lambda index: index)
    count_float = bag_counts.astype(jnp.float32)
    hits = count(slot_ids(row_ids, bag_counts), group * extent, 4)
    anchor = pool(hits, table_halves[0], table_halves[1], table_keys, count_float, dense_input)
    lows, narrows, in_one = cross_forward(anchor, down_all, up_all, cross_bias)
    total_samples = samples * lax.axis_size("rep") * group
    target = labels.astype(jnp.float32)[:, None]
    (
        loss_local,
        grad_head,
        grad_head_bias,
        bias_grad_one,
        bias_grad_two,
        bias_grad_three,
        grad_one,
        grad_late,
        grad_stream,
    ) = head(
        in_one, one_all, late_all, (bias_one, bias_two, bias_three), head_weight, head_bias, target, total_samples
    )
    share_one = lax.psum_scatter(grad_one, "rep", scatter_dimension=0, tiled=True)
    core = (lax.axis_index("rep") % 2).astype(jnp.int32).reshape(1)
    send_up, keep_up, grad_down, bias_grads, grad_summed = cross_backward(
        anchor, grad_stream, lows, narrows, down_all, up_all, cross_bias, count_float, core, repeats
    )
    share_down = lax.psum_scatter(grad_down, "rep", scatter_dimension=1, tiled=True)
    bits = up_down[::-1]
    reduced = []
    for first, last, order in spans:
        send, keep = row_gradient(hits, grad_summed, first, last - first, group, core)
        received = flip(send, 1)
        shape = (last - first, group) + (2,) * len(bits) + (part, width)
        reduced.append(scatter_pair(keep.reshape(shape), received.reshape(shape), bits, order, 2))
    row_share = ring_scatter(jnp.concatenate(reduced, axis=0).transpose(1, 0, 2, 3))
    table_grads = []
    for first, last, order in spans:
        value, keys = gather_across(row_share[None, first:last], order + [1])
        table_grads.append(place(value, keys, 1, lambda index: (index % 2) * (repeats // 2) + index // 2))
    table_grad = jnp.concatenate(table_grads, axis=0).astype(jnp.float32)
    late_blocks = grad_late.reshape((2,) * len(bits) + (2, -1) + grad_late.shape[1:])
    late_received = flip(lax.dynamic_index_in_dim(late_blocks, 1 - core[0], len(bits), keepdims=False), 1)
    late_keep = lax.dynamic_index_in_dim(late_blocks, core[0], len(bits), keepdims=False)
    share_late = scatter_pair(late_keep, late_received, bits, up_down, 0)
    received_up = flip(send_up, 1)
    share_rows = keep_up.shape[2] // 2
    shape = (CROSS,) + (2,) * len(bits) + (2, share_rows, D_IN)
    ups = []
    for index, order in ((0, up_down), (1, down_up)):
        pair = [lax.index_in_dim(item.reshape(shape), index, len(bits) + 1, keepdims=False) for item in (keep_up, received_up)]
        ups.append(scatter_pair(pair[0], pair[1], bits, order, 1))
    share_one, share_late = sum_groups([share_one, share_late])
    share_two, share_three = share_late[:, :H2], share_late[:, H2:]
    (share_up,) = sum_groups([jnp.concatenate(ups, axis=1)])
    (share_down,) = sum_groups([share_down])
    small_grad = jnp.concatenate(
        [
            item.reshape(-1)
            for item in (
                bias_grads,
                bias_grad_one,
                bias_grad_two,
                bias_grad_three,
                grad_head,
                grad_head_bias,
                loss_local,
            )
        ]
    )
    small_total = sum_all(small_grad)
    small_sum, loss_sum = small_total[:-1], small_total[-1]
    new_tables, new_table_first, new_table_second = adamw(
        tables, table_grad, table_first, table_second, 1.0
    )
    new_down, new_down_first, new_down_second = adamw(
        cross_down, share_down, down_first, down_second, D_IN ** (-0.5)
    )
    new_up, new_up_first, new_up_second = adamw(
        cross_up, share_up, up_first, up_second, RANK ** (-0.5)
    )
    new_one, new_one_first, new_one_second = adamw(
        hidden_one, share_one, one_first, one_second, D_IN ** (-0.5)
    )
    new_two, new_two_first, new_two_second = adamw(
        hidden_two, share_two, two_first, two_second, H1 ** (-0.5)
    )
    new_three, new_three_first, new_three_second = adamw(
        hidden_three, share_three, three_first, three_second, H2 ** (-0.5)
    )
    new_smalls, new_small_first, new_small_second = adamw(
        smalls, small_sum, small_first, small_second, 0.1
    )
    return (
        loss_sum,
        new_tables,
        new_table_first,
        new_table_second,
        new_down,
        new_down_first,
        new_down_second,
        new_up,
        new_up_first,
        new_up_second,
        new_one,
        new_one_first,
        new_one_second,
        new_two,
        new_two_first,
        new_two_second,
        new_three,
        new_three_first,
        new_three_second,
        new_smalls,
        new_small_first,
        new_small_second,
    )


def solution(mesh):
    return jax.shard_map(
        on_device,
        mesh=mesh,
        in_specs=(
            P(("rep", "grp"), None, None),
            P(("rep", "grp"), None),
            P(("rep", "grp")),
            P(("rep", "grp"), None),
            P(None, "grp", None),
            P(None, "grp", None),
            P(None, "grp", None),
            P(None, "rep", None),
            P(None, "rep", None),
            P(None, "rep", None),
            P(None, "rep", None),
            P(None, "rep", None),
            P(None, "rep", None),
            P("rep", None),
            P("rep", None),
            P("rep", None),
            P("rep", None),
            P("rep", None),
            P("rep", None),
            P("rep", None),
            P("rep", None),
            P("rep", None),
            P(),
            P(),
            P(),
        ),
        out_specs=(
            P(),
            P(None, "grp", None),
            P(None, "grp", None),
            P(None, "grp", None),
            P(None, "rep", None),
            P(None, "rep", None),
            P(None, "rep", None),
            P(None, "rep", None),
            P(None, "rep", None),
            P(None, "rep", None),
            P("rep", None),
            P("rep", None),
            P("rep", None),
            P("rep", None),
            P("rep", None),
            P("rep", None),
            P("rep", None),
            P("rep", None),
            P("rep", None),
            P(),
            P(),
            P(),
        ),
        check_vma=False,
    )
```

time: 1160 us -> 810 us (0.70)
  waiting for transfers between devices: 733 us -> 311 us
  Pallas kernels: 66.6 us -> 248 us
  matrix products: 178 us -> 0 us
  starting transfers between devices: 1.19 us -> 46 us
  blocking collectives: 44.4 us -> 0 us
  local copies, waits for them, and re-layouts: 39.7 us -> 76.6 us
  other arithmetic: 77.1 us -> 102 us
    reduce_scatter x7 -> x2, waiting for transfers between devices: 418 us -> 0.02 us  [the longest x1 0.02 us: on_device(): lax.psum_scatter(grad_one, 'rep', scatter_dimension=0, tiled=True)]
    ppermute x0 -> x58, waiting for transfers between devices: none -> 311 us  [the longest x32 182 us: flip(): lax.ppermute(value, 'rep', [(i, i ^ bit) for i in range(lax.axis_size('re...]
    pallas_call x1 -> x10, Pallas kernels: 66.6 us -> 248 us  [the longest x4 54 us: count(): pl.pallas_call(functools.partial(count_kernel, len(earlier)), grid=(last...]
    dot_general x30 -> x0, matrix products: 178 us -> none  [the longest x9 58.5 us: product(): return jnp.dot(left, right, preferred_element_type=jnp.float32)]
    all_gather x4 -> x0, waiting for transfers between devices: 142 us -> none  [the longest x1 87.9 us: on_device(): lax.all_gather(own_part.astype(jnp.bfloat16), ('grp', 'rep'), axis=1, til...]
    psum x1 -> x0, waiting for transfers between devices: 99.5 us -> none  [on_device(): lax.psum(share_down.astype(jnp.bfloat16), 'grp').astype(jnp.float32)]
    all_gather x1, waiting for transfers between devices: 59 us -> 0.01 us  [on_device(): lax.all_gather(cross_up.astype(jnp.bfloat16), 'rep', axis=1, tiled=True)]
    ppermute x0 -> x58, starting transfers between devices: none -> 45.8 us  [the longest x32 24.7 us: flip(): lax.ppermute(value, 'rep', [(i, i ^ bit) for i in range(lax.axis_size('re...]
  transfers between devices with their start and end apart: 15 -> 63, of which waited for: 14 -> 32; matrix products, arithmetic and copies ran while one was open for 12% -> 19% of each run, Pallas kernels for 6% -> 27%
where the time goes in v2:
time: 810 us; the launch traced here: 800 us
  waiting for transfers between devices  311 us (38%)
  Pallas kernels  248 us (31%)
  other arithmetic  102 us (13%)
  local copies, waits for them, and re-layouts  76.6 us (9%)
  starting transfers between devices  46 us (6%)
  between operations  15.2 us (2%)
    ppermute x32, waiting for transfers between devices, flip(): lax.ppermute(value, 'rep', [(i, i ^ bit) for i in range(lax.axis_size('re...  182 us
    ppermute x24, waiting for transfers between devices, ring(): lax.ppermute(value, 'grp', [(i, (i + 1) % size) for i in range(size)])  127 us
    pallas_call x4, Pallas kernels, count(): pl.pallas_call(functools.partial(count_kernel, len(earlier)), grid=(last...  54 us
    pallas_call x1, Pallas kernels, cross_backward(): pl.pallas_call(cross_backward_kernel, grid_spec=pltpu.PrefetchScalarGridS...  51.6 us
    pallas_call x2, Pallas kernels, row_gradient(): pl.pallas_call(row_kernel, grid_spec=pltpu.PrefetchScalarGridSpec(num_sca...  47.5 us
    sub x7, other arithmetic, adamw(): return (weight - rate * moved, first, second)  39.3 us
    pallas_call x1, Pallas kernels, pool(): pl.pallas_call(functools.partial(pool_kernel, keys=keys, half=half), grid...  38.3 us
    pallas_call x1, Pallas kernels, cross_forward(): pl.pallas_call(cross_forward_kernel, grid=(layers, 2, blocks), in_specs=[...  28.5 us
  transfers between devices with their start and end apart: 63, of which 32 were waited for; matrix products, arithmetic and copies ran while one was open for 19% of the time, Pallas kernels for 27%

profile of v2, /device:TPU:0, one launch (start us, length us, event | category | flops | bytes accessed | tf_op | source)
XLA Modules:
  0.0 799.8 jit_solution(9513681005808110892)
XLA Ops:
  7.2 3.1 convert_element_type.55
  22.5 4.2 copy.58
  26.8 5.6 reshape.220.ids_ref
  32.3 12.6 %shard_map.408.refs_0_ = bf16[26,512,2048]{2,1,0:T(8,128)(2,1)} custom-call(s32[26,64,256]{2,1,0:T(8,128)} %reshape.220.ids_ref), custom_call_target="tpu_custom_call" | custom-call | flops 12884901888 | bytes 12582912 | tf_op jit(solution)/shard_map/pallas_call | solution.py:112
  46.5 14.4 %shard_map.409.refs_0_ = bf16[26,512,2048]{2,1,0:T(8,128)(2,1)} custom-call(s32[26,64,256]{2,1,0:T(8,128)} %reshape.220.ids_ref, bf16[26,512,2048]{2,1,0:T(8,128)(2,1)} %shard_map.408.refs_0_), custom_call_target="tpu_custom_call", output_to_operand_aliasing={{}: (1, {})} | custom-call | flops 15032385536 | bytes 14680064 | tf_op jit(solution)/shard_map/pallas_call | solution.py:112
  64.7 9.8 %collective-permute-done.2 = bf16[26,64,128]{2,1,0:T(8,128)(2,1)S(1)} collective-permute-done((bf16[26,64,128]{2,1,0:T(8,128)(2,1)S(1)}, bf16[26,64,128]{2,1,0:T(8,128)(2,1)S(1)}, u32[]{:S(2)}, u32[]{:S(2)}) %collective-permute-start.2) | collective-permute-done | bytes 426016 | tf_op jit(solution)/shard_map/ppermute | solution.py:593
  76.8 12.7 %shard_map.410.refs_0_ = bf16[26,512,2048]{2,1,0:T(8,128)(2,1)} custom-call(s32[26,64,256]{2,1,0:T(8,128)} %reshape.220.ids_ref, bf16[26,512,2048]{2,1,0:T(8,128)(2,1)} %shard_map.409.refs_0_), custom_call_target="tpu_custom_call", output_to_operand_aliasing={{}: (1, {})} | custom-call | flops 12884901888 | bytes 12582912 | tf_op jit(solution)/shard_map/pallas_call | solution.py:112
  90.9 6.6 collective-permute-done.3
  104.7 14.3 %shard_map.411.hits_ref = bf16[26,512,2048]{2,1,0:T(8,128)(2,1)} custom-call(s32[26,64,256]{2,1,0:T(8,128)} %reshape.220.ids_ref, bf16[26,512,2048]{2,1,0:T(8,128)(2,1)} %shard_map.410.refs_0_), custom_call_target="tpu_custom_call", output_to_operand_aliasing={{}: (1, {})} | custom-call | flops 15032385536 | bytes 14680064 | tf_op jit(solution)/shard_map/pallas_call | solution.py:112
  125.9 3.8 collective-permute-done.10
  131.0 62.5 %collective-permute-done.4 = bf16[2,4,13,64,128]{4,3,2,1,0:T(8,128)(2,1)} collective-permute-done((bf16[2,4,13,64,128]{4,3,2,1,0:T(8,128)(2,1)}, bf16[2,4,13,64,128]{4,3,2,1,0:T(8,128)(2,1)}, u32[]{:S(2)}, u32[]{:S(2)}) %collective-permute-start.4) | collective-permute-done | bytes 1703968 | tf_op jit(solution)/shard_map/ppermute | solution.py:588
  206.7 38.3 %shard_map.412.anchor_in = f32[512,3456]{1,0:T(8,128)} custom-call(s32[2]{0:T(128)} %pad_add_fusion.place_ref, bf16[26,512,2048]{2,1,0:T(8,128)(2,1)} %shard_map.411.hits_ref, bf16[4,4,13,64,128]{4,3,2,1,0:T(8,128)(2,1)} %copy-done, bf16[4,4,13,64,128]{4,3,2,1,0:T(8,128)(2,1)} %copy-done.17, bf16[4,4,13,64,128]{4,3,2,1,0:T(8,128)(2,1)} %copy-done.1, ...), custom_call_target="tpu_custom_call" | custom-call | flops 6979321856 | bytes 74973184 | tf_op jit(solution)/shard_map/pallas_call | solution.py:183
  245.0 28.5 %shard_map.413 = (bf16[3,512,3456]{2,1,0:T(8,128)(2,1)}, bf16[3,512,512]{2,1,0:T(8,128)(2,1)}, bf16[512,3456]{1,0:T(8,128)(2,1)}) custom-call(f32[512,3456]{1,0:T(8,128)} %shard_map.412.anchor_in, bf16[3,3456,512]{2,1,0:T(8,128)(2,1)} %all-gather.4.cloned.1.call-done.down_ref, bf16[3,512,3456]{2,1,0:T(8,128)(2,1)} %all-gather.6.cloned.1.call-done.up_ref, ...), custom_call_target="tpu_custom_call" | custom-call | flops 10871635968 | bytes 49545216 | tf_op jit(solution)/shard_map/pallas_call | solution.py:256
  273.5 28.3 %shard_map.414 = (f32[1,1]{1,0:T(1,128)}, f32[1,512]{1,0:T(1,128)}, f32[1,1]{1,0:T(1,128)}, f32[1,1024]{1,0:T(1,128)}, f32[1,1024]{1,0:T(1,128)}, /*index=5*/f32...) custom-call(bf16[512,3456]{1,0:T(8,128)(2,1)} %get-tuple-element.43.input_ref, ...), custom_call_target="tpu_custom_call" | custom-call | flops 15703474176 | bytes 35389440 | tf_op jit(solution)/shard_map/pallas_call | solution.py:372
  301.9 51.6 %shard_map.415 = (bf16[3,4,64,3456]{3,2,1,0:T(8,128)(2,1)}, bf16[3,4,64,3456]{3,2,1,0:T(8,128)(2,1)}, bf16[3,3456,512]{2,1,0:T(8,128)(2,1)}, f32[3,1,3456]{2,1,0:T(1,128)}, bf16[512,3456]{1,0:T(8,128)(2,1)}) custom-call(s32[1]{0:T(128)} %bitcast.core_ref, f32[512,3456]{1,0:T(8,128)} %shard_map.412.anchor_in, f32[512,3456]{1,0:T(8,128)} %get-tuple-element.44.grad_in, ...), custom_call_target="tpu_custom_call" | custom-call | flops 27179089920 | bytes 70778880 | tf_op jit(solution)/shard_map/pallas_call | solution.py:503
  353.5 19.9 %shard_map.417 = (bf16[13,4,256,128]{3,2,1,0:T(8,128)(2,1)}, bf16[13,4,256,128]{3,2,1,0:T(8,128)(2,1)}) custom-call(s32[1]{0:T(128)} %bitcast.core_ref, bf16[26,512,2048]{2,1,0:T(8,128)(2,1)} %shard_map.411.hits_ref, bf16[512,3456]{1,0:T(8,128)(2,1)} %get-tuple-element.54.grad_ref), custom_call_target="tpu_custom_call" | custom-call | flops 13958643712 | bytes 34078720 | tf_op jit(solution)/shard_map/pallas_call | solution.py:565
  373.4 27.6 %shard_map.416 = (bf16[13,4,256,128]{3,2,1,0:T(8,128)(2,1)}, bf16[13,4,256,128]{3,2,1,0:T(8,128)(2,1)}) custom-call(s32[1]{0:T(128)} %bitcast.core_ref, bf16[26,512,2048]{2,1,0:T(8,128)(2,1)} %shard_map.411.hits_ref, bf16[512,3456]{1,0:T(8,128)(2,1)} %get-tuple-element.54.grad_ref), custom_call_target="tpu_custom_call" | custom-call | flops 13958643712 | bytes 34078720 | tf_op jit(solution)/shard_map/pallas_call | solution.py:565
  408.6 6.4 collective-permute-done.12
  419.5 4.0 collective-permute-done.14
  436.3 4.3 dynamic-slice_add_fusion
  448.4 7.2 collective-permute-done.50
  458.9 41.0 %collective-permute-done.51 = bf16[128,1536]{1,0:T(8,128)(2,1)S(1)} collective-permute-done((bf16[128,1536]{1,0:T(8,128)(2,1)S(1)}, bf16[128,1536]{1,0:T(8,128)(2,1)S(1)}, u32[]{:S(2)}, u32[]{:S(2)}) %collective-permute-start.51) | collective-permute-done | bytes 393248 | tf_op jit(solution)/shard_map/ppermute | solution.py:588
  505.8 3.3 collective-permute-done.18
  519.6 18.9 %collective-permute-done.22 = bf16[13,4,64,128]{3,2,1,0:T(8,128)(2,1)S(1)} collective-permute-done((bf16[13,4,64,128]{3,2,1,0:T(8,128)(2,1)S(1)}, bf16[13,4,64,128]{3,2,1,0:T(8,128)(2,1)S(1)}, u32[]{:S(2)}, u32[]{:S(2)}) %collective-permute-start.22) | collective-permute-done | bytes 852000 | tf_op jit(solution)/shard_map/ppermute | solution.py:588
  543.2 10.5 %collective-permute-done.23 = bf16[26,64,128]{2,1,0:T(8,128)(2,1)S(1)} collective-permute-done((bf16[26,64,128]{2,1,0:T(8,128)(2,1)S(1)}, bf16[26,64,128]{2,1,0:T(8,128)(2,1)S(1)}, u32[]{:S(2)}, u32[]{:S(2)}) %collective-permute-start.23) | collective-permute-done | bytes 426016 | tf_op jit(solution)/shard_map/ppermute | solution.py:593
  553.8 22.9 %collective-permute-done.39 = bf16[3,2,32,3456]{3,2,0,1:T(8,128)(2,1)S(1)} collective-permute-done((bf16[3,2,32,3456]{3,2,0,1:T(8,128)(2,1)S(1)}, bf16[3,2,32,3456]{3,2,0,1:T(8,128)(2,1)S(1)}, u32[]{:S(2)}, u32[]{:S(2)}) %collective-permute-start.39) | collective-permute-done | bytes 1327136 | tf_op jit(solution)/shard_map/ppermute | solution.py:588
  581.1 6.2 collective-permute-done.25
  594.5 3.9 reshape.240
  606.2 5.0 collective-permute-done.43
  615.3 5.2 collective-permute-done.44
  620.7 8.8 %collective-permute-done.45 = bf16[1296,128]{1,0:T(8,128)(2,1)S(1)} collective-permute-done((bf16[1296,128]{1,0:T(8,128)(2,1)S(1)}, bf16[1296,128]{1,0:T(8,128)(2,1)S(1)}, u32[]{:S(2)}, u32[]{:S(2)}) %collective-permute-start.45) | collective-permute-done | bytes 331808 | tf_op jit(solution)/shard_map/ppermute | solution.py:593
  631.6 11.2 %collective-permute-done.46 = bf16[1296,128]{1,0:T(8,128)(2,1)} collective-permute-done((bf16[1296,128]{1,0:T(8,128)(2,1)S(1)}, bf16[1296,128]{1,0:T(8,128)(2,1)}, u32[]{:S(2)}, u32[]{:S(2)}) %collective-permute-start.46) | collective-permute-done | bytes 331808 | tf_op jit(solution)/shard_map/ppermute | solution.py:593
  648.8 14.0 %add_subtract_fusion = (f32[26,512,128]{2,1,0:T(8,128)}, f32[26,512,128]{2,1,0:T(8,128)}, f32[26,512,128]{2,1,0:T(8,128)}) fusion(f32[26,512,128]{2,1,0:T(8,128)} %param.29, bf16[13,512,128]{2,1,0:T(8,128)(2,1)S(1)} %fusion.35, bf16[13,512,128]{2,1,0:T(8,128)(2,1)S(1)} %fusion.41, f32[26,512,128]{2,1,0:T(8,128)} %param.30, f32[26,512,128]{2,1,0:T(8,128)} %param.31), kind=kLoop, calls=%fused_computation.4 | loop fusion | flops 27262976 | bytes 44302336 | tf_op jit(solution)/shard_map/sub | solution.py:686
  663.0 4.4 collective-permute-start.53
  669.1 9.6 %collective-permute-done.53 = bf16[1248,128]{1,0:T(8,128)(2,1)S(1)} collective-permute-done((bf16[1248,128]{1,0:T(8,128)(2,1)S(1)}, bf16[1248,128]{1,0:T(8,128)(2,1)S(1)}, u32[]{:S(2)}, u32[]{:S(2)}) %collective-permute-start.53) | collective-permute-done | bytes 319520 | tf_op jit(solution)/shard_map/ppermute | solution.py:593
  679.6 4.0 reshape.245
  683.6 7.2 collective-permute-done.54
  693.8 7.8 multiply_subtract_fusion
  703.3 9.8 %collective-permute-done.56 = bf16[1248,128]{1,0:T(8,128)(2,1)S(1)} collective-permute-done((bf16[1248,128]{1,0:T(8,128)(2,1)S(1)}, bf16[1248,128]{1,0:T(8,128)(2,1)S(1)}, u32[]{:S(2)}, u32[]{:S(2)}) %collective-permute-start.56) | collective-permute-done | bytes 319520 | tf_op jit(solution)/shard_map/ppermute | solution.py:593
  716.9 7.1 collective-permute-done.57
  734.0 3.5 collective-permute-done.33
  738.7 5.4 multiply_subtract_fusion.2
  744.1 4.0 collective-permute-done.34
  753.9 8.5 %collective-permute-done.35 = bf16[1296,128]{1,0:T(8,128)(2,1)S(1)} collective-permute-done((bf16[1296,128]{1,0:T(8,128)(2,1)S(1)}, bf16[1296,128]{1,0:T(8,128)(2,1)S(1)}, u32[]{:S(2)}, u32[]{:S(2)}) %collective-permute-start.35) | collective-permute-done | bytes 331808 | tf_op jit(solution)/shard_map/ppermute | solution.py:593
  763.2 8.2 %collective-permute-done.36 = bf16[1296,128]{1,0:T(8,128)(2,1)S(1)} collective-permute-done((bf16[1296,128]{1,0:T(8,128)(2,1)S(1)}, bf16[1296,128]{1,0:T(8,128)(2,1)S(1)}, u32[]{:S(2)}, u32[]{:S(2)}) %collective-permute-start.36) | collective-permute-done | bytes 331808 | tf_op jit(solution)/shard_map/ppermute | solution.py:593
  772.1 8.2 %collective-permute-done.37 = bf16[1296,128]{1,0:T(8,128)(2,1)S(1)} collective-permute-done((bf16[1296,128]{1,0:T(8,128)(2,1)S(1)}, bf16[1296,128]{1,0:T(8,128)(2,1)S(1)}, u32[]{:S(2)}, u32[]{:S(2)}) %collective-permute-start.37) | collective-permute-done | bytes 331808 | tf_op jit(solution)/shard_map/ppermute | solution.py:593
  781.0 3.6 reshape.244
  784.7 8.1 %multiply_subtract_fusion.1 = (f32[3,432,512]{2,1,0:T(8,128)}, f32[3,432,512]{2,1,0:T(8,128)}, f32[3,432,512]{2,1,0:T(8,128)}) fusion(f32[3,432,512]{2,1,0:T(8,128)S(1)} %copy-done.4, f32[3,432,512]{2,1,0:T(8,128)} %reshape.244, f32[3,432,512]{2,1,0:T(8,128)} %param.33, f32[3,432,512]{2,1,0:T(8,128)} %param.34), kind=kLoop, calls=%fused_computation.15 | loop fusion | flops 9953280 | bytes 18579456 | tf_op jit(solution)/shard_map/sub | solution.py:686
  (316 shorter events, 168.4 us)
Async XLA Ops:
  7.2 237.8 %all-gather.4.cloned.1.call-start = ((), (), s32[]{:S(2)}) async-start(), calls=%async_computation.2 | async-start | bytes 11943936 | tf_op jit(solution)/shard_map/all_gather | solution.py:718
  10.4 234.6 %all-gather.6.cloned.1.call-start = ((), (), s32[]{:S(2)}) async-start(), calls=%async_computation.3 | async-start | bytes 11943936 | tf_op jit(solution)/shard_map/all_gather | solution.py:719
  11.7 261.8 %all-gather.8.cloned.1.call-start = ((), (), s32[]{:S(2)}) async-start(), calls=%async_computation.4 | async-start | bytes 7962624 | tf_op jit(solution)/shard_map/all_gather | solution.py:720
  13.9 31.0 %collective-permute-start = (bf16[26,64,128]{2,1,0:T(8,128)(2,1)}, bf16[26,64,128]{2,1,0:T(8,128)(2,1)}, u32[]{:S(2)}, u32[]{:S(2)}) collective-permute-start(bf16[26,64,128]{2,1,0:T(8,128)(2,1)} %dynamic-slice_convert_fusion), channel_id=1, source_target_pairs={{0,1},{1,2},{2,3},{3,0},{4,5},{5,6},{6,7},{7,4},{8,9},{9,10},{10,1... | collective-permute-start | bytes 1277960 | tf_op jit(solution)/shard_map/ppermute | solution.py:593
  17.8 71.7 %collective-permute-start.9 = (bf16[1,128,1536]{2,1,0:T(8,128)(2,1)}, bf16[1,128,1536]{2,1,0:T(8,128)(2,1)S(1)}, u32[]{:S(2)}, u32[]{:S(2)}) collective-permute-start(bf16[1,128,1536]{2,1,0:T(8,128)(2,1)} %pad_maximum_fusion.12), channel_id=1, source_target_pairs={{0,8},{4,12},{8,0},{12,4},{16,24},{20,28},{24,16},{28,20},{1,9},{5... | collective-permute-start | bytes 1179656 | tf_op jit(solution)/shard_map/ppermute | solution.py:588
  20.4 624.5 %reduce-scatter.5.cloned.1.call-start = ((), (), s32[]{:S(2)}) async-start(), calls=%async_computation.6 | async-start | bytes 7962624 | tf_op jit(solution)/shard_map/reduce_scatter | solution.py:761
  44.9 17.1 %collective-permute-start.1 = (bf16[26,64,128]{2,1,0:T(8,128)(2,1)}, bf16[26,64,128]{2,1,0:T(8,128)(2,1)S(1)}, u32[]{:S(2)}, u32[]{:S(2)}) collective-permute-start(bf16[26,64,128]{2,1,0:T(8,128)(2,1)} %collective-permute-done), channel_id=1, source_target_pairs={{0,1},{1,2},{2,3},{3,0},{4,5},{5,6},{6,7},{7,4},{8,9},{9,10},{10,1... | collective-permute-start | bytes 1277960 | tf_op jit(solution)/shard_map/ppermute | solution.py:593
  62.0 12.5 %collective-permute-start.2 = (bf16[26,64,128]{2,1,0:T(8,128)(2,1)S(1)}, bf16[26,64,128]{2,1,0:T(8,128)(2,1)S(1)}, u32[]{:S(2)}, u32[]{:S(2)}) collective-permute-start(bf16[26,64,128]{2,1,0:T(8,128)(2,1)S(1)} %collective-permute-done.1), channel_id=1, source_target_pairs={{0,1},{1,2},{2,3},{3,0},{4,5},{5,6},{6,7},{7,4},{8,9},{9,10},{10,1... | collective-permute-start | bytes 1277960 | tf_op jit(solution)/shard_map/ppermute | solution.py:593
  74.7 22.9 %collective-permute-start.3 = (bf16[1,4,13,64,128]{4,3,2,1,0:T(8,128)(2,1)S(1)}, bf16[1,4,13,64,128]{4,3,2,1,0:T(8,128)(2,1)}, u32[]{:S(2)}, u32[]{:S(2)}) collective-permute-start(bf16[1,4,13,64,128]{4,3,2,1,0:T(8,128)(2,1)S(1)} %maximum_bitcast_fusion), channel_id=1, source_target_pairs={{0,8},{4,12},{8,0},{12,4},{16,24},{20,28},{24,16},{28,20},{1,9},{5... | collective-permute-start | bytes 2555912 | tf_op jit(solution)/shard_map/ppermute | solution.py:588
  75.2 26.4 %collective-permute-start.6 = (bf16[1,4,13,64,128]{4,3,2,1,0:T(8,128)(2,1)S(1)}, bf16[1,4,13,64,128]{4,3,2,1,0:T(8,128)(2,1)}, u32[]{:S(2)}, u32[]{:S(2)}) collective-permute-start(bf16[1,4,13,64,128]{4,3,2,1,0:T(8,128)(2,1)S(1)} %maximum_bitcast_fusion.1), channel_id=1, source_target_pairs={{0,16},{4,20},{8,24},{12,28},{16,0},{20,4},{24,8},{28,12},{1,17},{... | collective-permute-start | bytes 2555912 | tf_op jit(solution)/shard_map/ppermute | solution.py:588
  90.4 39.3 %collective-permute-start.10 = (bf16[2,128,1536]{2,1,0:T(8,128)(2,1)}, bf16[2,128,1536]{2,1,0:T(8,128)(2,1)}, u32[]{:S(2)}, u32[]{:S(2)}) collective-permute-start(bf16[2,128,1536]{2,1,0:T(8,128)(2,1)} %pad_maximum_fusion.9), channel_id=1, source_target_pairs={{0,16},{4,20},{8,24},{12,28},{16,0},{20,4},{24,8},{28,12},{1,17},{... | collective-permute-start | bytes 2359304 | tf_op jit(solution)/shard_map/ppermute | solution.py:588
  100.1 93.4 %collective-permute-start.4 = (bf16[2,4,13,64,128]{4,3,2,1,0:T(8,128)(2,1)}, bf16[2,4,13,64,128]{4,3,2,1,0:T(8,128)(2,1)}, u32[]{:S(2)}, u32[]{:S(2)}) collective-permute-start(bf16[2,4,13,64,128]{4,3,2,1,0:T(8,128)(2,1)} %pad_maximum_fusion.3), channel_id=1, source_target_pairs={{0,16},{4,20},{8,24},{12,28},{16,0},{20,4},{24,8},{28,12},{1,17},{... | collective-permute-start | bytes 5111816 | tf_op jit(solution)/shard_map/ppermute | solution.py:588
  104.1 91.5 %collective-permute-start.7 = (bf16[2,4,13,64,128]{4,3,2,1,0:T(8,128)(2,1)}, bf16[2,4,13,64,128]{4,3,2,1,0:T(8,128)(2,1)}, u32[]{:S(2)}, u32[]{:S(2)}) collective-permute-start(bf16[2,4,13,64,128]{4,3,2,1,0:T(8,128)(2,1)} %pad_maximum_fusion.4), channel_id=1, source_target_pairs={{0,8},{4,12},{8,0},{12,4},{16,24},{20,28},{24,16},{28,20},{1,9},{5... | collective-permute-start | bytes 5111816 | tf_op jit(solution)/shard_map/ppermute | solution.py:588
  130.9 70.9 %collective-permute-start.11 = (bf16[4,128,1536]{2,1,0:T(8,128)(2,1)S(1)}, bf16[4,128,1536]{2,1,0:T(8,128)(2,1)S(1)}, u32[]{:S(2)}, u32[]{:S(2)}) collective-permute-start(bf16[4,128,1536]{2,1,0:T(8,128)(2,1)S(1)} %pad_maximum_fusion.5), channel_id=1, source_target_pairs={{0,4},{4,0},{8,12},{12,8},{16,20},{20,16},{24,28},{28,24},{1,5},{5... | collective-permute-start | bytes 4718600 | tf_op jit(solution)/shard_map/ppermute | solution.py:588
  301.8 412.1 %reduce-scatter.3.cloned.1.call-start = ((), (), s32[]{:S(2)}) async-start(), calls=%async_computation.5 | async-start | bytes 11943936 | tf_op jit(solution)/shard_map/reduce_scatter | solution.py:766
  373.3 62.9 %collective-permute-start.20 = (bf16[13,4,256,128]{3,2,1,0:T(8,128)(2,1)}, bf16[13,4,256,128]{3,2,1,0:T(8,128)(2,1)}, u32[]{:S(2)}, u32[]{:S(2)}) collective-permute-start(bf16[13,4,256,128]{3,2,1,0:T(8,128)(2,1)} %get-tuple-element.58), channel_id=1, source_target_pairs={{0,4},{4,0},{8,12},{12,8},{16,20},{20,16},{24,28},{28,24},{1,5},{5... | collective-permute-start | bytes 10223624 | tf_op jit(solution)/shard_map/ppermute | solution.py:588
  401.1 39.9 %collective-permute-start.17 = (bf16[13,4,256,128]{3,2,1,0:T(8,128)(2,1)}, bf16[13,4,256,128]{3,2,1,0:T(8,128)(2,1)S(1)}, u32[]{:S(2)}, u32[]{:S(2)}) collective-permute-start(bf16[13,4,256,128]{3,2,1,0:T(8,128)(2,1)} %get-tuple-element.56), channel_id=1, source_target_pairs={{0,4},{4,0},{8,12},{12,8},{16,20},{20,16},{24,28},{28,24},{1,5},{5... | collective-permute-start | bytes 10223624 | tf_op jit(solution)/shard_map/ppermute | solution.py:588
  401.6 108.8 %collective-permute-start.38 = (bf16[3,4,64,3456]{3,2,1,0:T(8,128)(2,1)}, bf16[3,4,64,3456]{3,2,1,0:T(8,128)(2,1)}, u32[]{:S(2)}, u32[]{:S(2)}) collective-permute-start(bf16[3,4,64,3456]{3,2,1,0:T(8,128)(2,1)} %get-tuple-element.61), channel_id=1, source_target_pairs={{0,4},{4,0},{8,12},{12,8},{16,20},{20,16},{24,28},{28,24},{1,5},{5... | collective-permute-start | bytes 15925256 | tf_op jit(solution)/shard_map/ppermute | solution.py:588
  404.4 27.3 %collective-permute-start.49 = (bf16[2,2,128,1536]{3,2,1,0:T(8,128)(2,1)}, bf16[2,2,128,1536]{3,2,1,0:T(8,128)(2,1)}, u32[]{:S(2)}, u32[]{:S(2)}) collective-permute-start(bf16[2,2,128,1536]{3,2,1,0:T(8,128)(2,1)} %dynamic-slice_bitcast_fusion), channel_id=1, source_target_pairs={{0,4},{4,0},{8,12},{12,8},{16,20},{20,16},{24,28},{28,24},{1,5},{5... | collective-permute-start | bytes 4718600 | tf_op jit(solution)/shard_map/ppermute | solution.py:588
  429.3 17.6 %collective-permute-start.16 = (f32[13442]{0:T(1024)}, f32[13442]{0:T(1024)}, u32[]{:S(2)}, u32[]{:S(2)}) collective-permute-start(f32[13442]{0:T(1024)} %add.654), channel_id=1, source_target_pairs={{0,2},{1,3},{2,0},{3,1},{4,6},{5,7},{6,4},{7,5},{8,10},{9,11},{10,... | collective-permute-start | bytes 161312 | tf_op jit(solution)/shard_map/ppermute | solution.py:675
  434.8 20.8 %collective-permute-start.50 = (bf16[2,128,1536]{2,1,0:T(8,128)(2,1)}, bf16[2,128,1536]{2,1,0:T(8,128)(2,1)}, u32[]{:S(2)}, u32[]{:S(2)}) collective-permute-start(bf16[2,128,1536]{2,1,0:T(8,128)(2,1)} %get-tuple-element.100), channel_id=1, source_target_pairs={{0,8},{4,12},{8,0},{12,4},{16,24},{20,28},{24,16},{28,20},{1,9},{5... | collective-permute-start | bytes 2359304 | tf_op jit(solution)/shard_map/ppermute | solution.py:588
  440.6 63.4 %collective-permute-start.21 = (bf16[13,4,2,64,128]{4,3,2,1,0:T(8,128)(2,1)}, bf16[13,4,2,64,128]{4,3,2,1,0:T(8,128)(2,1)}, u32[]{:S(2)}, u32[]{:S(2)}) collective-permute-start(bf16[13,4,2,64,128]{4,3,2,1,0:T(8,128)(2,1)} %get-tuple-element.92), channel_id=1, source_target_pairs={{0,16},{4,20},{8,24},{12,28},{16,0},{20,4},{24,8},{28,12},{1,17},{... | collective-permute-start | bytes 5111816 | tf_op jit(solution)/shard_map/ppermute | solution.py:588
  444.0 65.0 %collective-permute-start.18 = (bf16[13,4,2,64,128]{4,3,1,0,2:T(8,128)(2,1)}, bf16[13,4,2,64,128]{4,3,1,0,2:T(8,128)(2,1)}, u32[]{:S(2)}, u32[]{:S(2)}) collective-permute-start(bf16[13,4,2,64,128]{4,3,1,0,2:T(8,128)(2,1)} %fusion.5), channel_id=1, source_target_pairs={{0,8},{4,12},{8,0},{12,4},{16,24},{20,28},{24,16},{28,20},{1,9},{5... | collective-permute-start | bytes 5111816 | tf_op jit(solution)/shard_map/ppermute | solution.py:588
  456.7 43.2 %collective-permute-start.51 = (bf16[128,1536]{1,0:T(8,128)(2,1)S(1)}, bf16[128,1536]{1,0:T(8,128)(2,1)S(1)}, u32[]{:S(2)}, u32[]{:S(2)}) collective-permute-start(bf16[128,1536]{1,0:T(8,128)(2,1)S(1)} %add_bitcast_fusion.2), channel_id=1, source_target_pairs={{0,16},{4,20},{8,24},{12,28},{16,0},{20,4},{24,8},{28,12},{1,17},{... | collective-permute-start | bytes 1179656 | tf_op jit(solution)/shard_map/ppermute | solution.py:588
  505.7 32.7 %collective-permute-start.22 = (bf16[13,4,64,128]{3,2,1,0:T(8,128)(2,1)S(1)}, bf16[13,4,64,128]{3,2,1,0:T(8,128)(2,1)S(1)}, u32[]{:S(2)}, u32[]{:S(2)}) collective-permute-start(bf16[13,4,64,128]{3,2,1,0:T(8,128)(2,1)S(1)} %fusion.10), channel_id=1, source_target_pairs={{0,8},{4,12},{8,0},{12,4},{16,24},{20,28},{24,16},{28,20},{1,9},{5... | collective-permute-start | bytes 2555912 | tf_op jit(solution)/shard_map/ppermute | solution.py:588
  510.3 29.6 %collective-permute-start.19 = (bf16[13,4,64,128]{3,2,1,0:T(8,128)(2,1)S(1)}, bf16[13,4,64,128]{3,2,1,0:T(8,128)(2,1)S(1)}, u32[]{:S(2)}, u32[]{:S(2)}) collective-permute-start(bf16[13,4,64,128]{3,2,1,0:T(8,128)(2,1)S(1)} %fusion.11), channel_id=1, source_target_pairs={{0,16},{4,20},{8,24},{12,28},{16,0},{20,4},{24,8},{28,12},{1,17},{... | collective-permute-start | bytes 2555912 | tf_op jit(solution)/shard_map/ppermute | solution.py:588
  514.5 62.2 %collective-permute-start.39 = (bf16[3,2,32,3456]{3,2,0,1:T(8,128)(2,1)S(1)}, bf16[3,2,32,3456]{3,2,0,1:T(8,128)(2,1)S(1)}, u32[]{:S(2)}, u32[]{:S(2)}) collective-permute-start(bf16[3,2,32,3456]{3,2,0,1:T(8,128)(2,1)S(1)} %fusion.7), channel_id=1, source_target_pairs={{0,8},{4,12},{8,0},{12,4},{16,24},{20,28},{24,16},{28,20},{1,9},{5... | collective-permute-start | bytes 3981320 | tf_op jit(solution)/shard_map/ppermute | solution.py:588
  517.5 62.1 %collective-permute-start.41 = (bf16[3,2,32,3456]{3,2,1,0:T(8,128)(2,1)S(1)}, bf16[3,2,32,3456]{3,2,1,0:T(8,128)(2,1)S(1)}, u32[]{:S(2)}, u32[]{:S(2)}) collective-permute-start(bf16[3,2,32,3456]{3,2,1,0:T(8,128)(2,1)S(1)} %get-tuple-element.98), channel_id=1, source_target_pairs={{0,16},{4,20},{8,24},{12,28},{16,0},{20,4},{24,8},{28,12},{1,17},{... | collective-permute-start | bytes 3981320 | tf_op jit(solution)/shard_map/ppermute | solution.py:588
  541.3 12.4 %collective-permute-start.23 = (bf16[26,64,128]{2,1,0:T(8,128)(2,1)S(1)}, bf16[26,64,128]{2,1,0:T(8,128)(2,1)S(1)}, u32[]{:S(2)}, u32[]{:S(2)}) collective-permute-start(bf16[26,64,128]{2,1,0:T(8,128)(2,1)S(1)} %fusion.18), channel_id=1, source_target_pairs={{0,1},{1,2},{2,3},{3,0},{4,5},{5,6},{6,7},{7,4},{8,9},{9,10},{10,1... | collective-permute-start | bytes 1277960 | tf_op jit(solution)/shard_map/ppermute | solution.py:593
  553.8 23.5 %collective-permute-start.24 = (bf16[26,64,128]{2,1,0:T(8,128)(2,1)S(1)}, bf16[26,64,128]{2,1,0:T(8,128)(2,1)S(1)}, u32[]{:S(2)}, u32[]{:S(2)}) collective-permute-start(bf16[26,64,128]{2,1,0:T(8,128)(2,1)S(1)} %fusion.27), channel_id=1, source_target_pairs={{0,1},{1,2},{2,3},{3,0},{4,5},{5,6},{6,7},{7,4},{8,9},{9,10},{10,1... | collective-permute-start | bytes 1277960 | tf_op jit(solution)/shard_map/ppermute | solution.py:593
  576.8 15.2 %collective-permute-start.40 = (bf16[3,32,3456]{2,1,0:T(8,128)(2,1)S(1)}, bf16[3,32,3456]{2,1,0:T(8,128)(2,1)S(1)}, u32[]{:S(2)}, u32[]{:S(2)}) collective-permute-start(bf16[3,32,3456]{2,1,0:T(8,128)(2,1)S(1)} %fusion.15), channel_id=1, source_target_pairs={{0,16},{4,20},{8,24},{12,28},{16,0},{20,4},{24,8},{28,12},{1,17},{... | collective-permute-start | bytes 1990664 | tf_op jit(solution)/shard_map/ppermute | solution.py:588
  579.7 13.5 %collective-permute-start.42 = (bf16[3,32,3456]{2,1,0:T(8,128)(2,1)S(1)}, bf16[3,32,3456]{2,1,0:T(8,128)(2,1)S(1)}, u32[]{:S(2)}, u32[]{:S(2)}) collective-permute-start(bf16[3,32,3456]{2,1,0:T(8,128)(2,1)S(1)} %fusion.14), channel_id=1, source_target_pairs={{0,8},{4,12},{8,0},{12,4},{16,24},{20,28},{24,16},{28,20},{1,9},{5... | collective-permute-start | bytes 1990664 | tf_op jit(solution)/shard_map/ppermute | solution.py:588
  588.6 12.4 %collective-permute-start.26 = (bf16[1,13,64,128]{3,2,1,0:T(8,128)(2,1)}, bf16[1,13,64,128]{3,2,1,0:T(8,128)(2,1)}, u32[]{:S(2)}, u32[]{:S(2)}) collective-permute-start(bf16[1,13,64,128]{3,2,1,0:T(8,128)(2,1)} %get-tuple-element.108), channel_id=1, source_target_pairs={{0,8},{4,12},{8,0},{12,4},{16,24},{20,28},{24,16},{28,20},{1,9},{5... | collective-permute-start | bytes 638984 | tf_op jit(solution)/shard_map/ppermute | solution.py:588
  590.0 12.7 %collective-permute-start.29 = (bf16[1,13,64,128]{3,2,1,0:T(8,128)(2,1)}, bf16[1,13,64,128]{3,2,1,0:T(8,128)(2,1)}, u32[]{:S(2)}, u32[]{:S(2)}) collective-permute-start(bf16[1,13,64,128]{3,2,1,0:T(8,128)(2,1)} %get-tuple-element.109), channel_id=1, source_target_pairs={{0,16},{4,20},{8,24},{12,28},{16,0},{20,4},{24,8},{28,12},{1,17},{... | collective-permute-start | bytes 638984 | tf_op jit(solution)/shard_map/ppermute | solution.py:588
  599.5 11.8 %collective-permute-start.43 = (bf16[1296,128]{1,0:T(8,128)(2,1)S(1)}, bf16[1296,128]{1,0:T(8,128)(2,1)S(1)}, u32[]{:S(2)}, u32[]{:S(2)}) collective-permute-start(bf16[1296,128]{1,0:T(8,128)(2,1)S(1)} %dynamic-slice_bitcast_fusion.1), channel_id=1, source_target_pairs={{0,1},{1,2},{2,3},{3,0},{4,5},{5,6},{6,7},{7,4},{8,9},{9,10},{10,1... | collective-permute-start | bytes 995336 | tf_op jit(solution)/shard_map/ppermute | solution.py:593
  602.1 10.2 %collective-permute-start.27 = (bf16[2,13,64,128]{3,2,1,0:T(8,128)(2,1)S(1)}, bf16[2,13,64,128]{3,2,1,0:T(8,128)(2,1)S(1)}, u32[]{:S(2)}, u32[]{:S(2)}) collective-permute-start(bf16[2,13,64,128]{3,2,1,0:T(8,128)(2,1)S(1)} %pad_maximum_fusion.10), channel_id=1, source_target_pairs={{0,16},{4,20},{8,24},{12,28},{16,0},{20,4},{24,8},{28,12},{1,17},{... | collective-permute-start | bytes 1277960 | tf_op jit(solution)/shard_map/ppermute | solution.py:588
  613.5 31.0 %collective-permute-start.28 = (bf16[4,13,64,128]{3,2,1,0:T(8,128)(2,1)S(1)}, bf16[4,13,64,128]{3,2,1,0:T(8,128)(2,1)S(1)}, u32[]{:S(2)}, u32[]{:S(2)}) collective-permute-start(bf16[4,13,64,128]{3,2,1,0:T(8,128)(2,1)S(1)} %pad_maximum_fusion.7), channel_id=1, source_target_pairs={{0,4},{4,0},{8,12},{12,8},{16,20},{20,16},{24,28},{28,24},{1,5},{5... | collective-permute-start | bytes 2555912 | tf_op jit(solution)/shard_map/ppermute | solution.py:588
  614.7 29.8 %collective-permute-start.31 = (bf16[4,13,64,128]{3,2,1,0:T(8,128)(2,1)S(1)}, bf16[4,13,64,128]{3,2,1,0:T(8,128)(2,1)S(1)}, u32[]{:S(2)}, u32[]{:S(2)}) collective-permute-start(bf16[4,13,64,128]{3,2,1,0:T(8,128)(2,1)S(1)} %pad_maximum_fusion.8), channel_id=1, source_target_pairs={{0,4},{4,0},{8,12},{12,8},{16,20},{20,16},{24,28},{28,24},{1,5},{5... | collective-permute-start | bytes 2555912 | tf_op jit(solution)/shard_map/ppermute | solution.py:588
  631.5 11.2 %collective-permute-start.46 = (bf16[1296,128]{1,0:T(8,128)(2,1)S(1)}, bf16[1296,128]{1,0:T(8,128)(2,1)}, u32[]{:S(2)}, u32[]{:S(2)}) collective-permute-start(bf16[1296,128]{1,0:T(8,128)(2,1)S(1)} %get-tuple-element.82), channel_id=1, source_target_pairs={{0,1},{1,2},{2,3},{3,0},{4,5},{5,6},{6,7},{7,4},{8,9},{9,10},{10,1... | collective-permute-start | bytes 995336 | tf_op jit(solution)/shard_map/ppermute | solution.py:593
  642.8 20.0 %collective-permute-start.47 = (bf16[1296,128]{1,0:T(8,128)(2,1)}, bf16[1296,128]{1,0:T(8,128)(2,1)}, u32[]{:S(2)}, u32[]{:S(2)}) collective-permute-start(bf16[1296,128]{1,0:T(8,128)(2,1)} %collective-permute-done.46), channel_id=1, source_target_pairs={{0,1},{1,2},{2,3},{3,0},{4,5},{5,6},{6,7},{7,4},{8,9},{9,10},{10,1... | collective-permute-start | bytes 995336 | tf_op jit(solution)/shard_map/ppermute | solution.py:593
  648.7 14.2 %collective-permute-start.52 = (bf16[1248,128]{1,0:T(8,128)(2,1)S(1)}, bf16[1248,128]{1,0:T(8,128)(2,1)S(1)}, u32[]{:S(2)}, u32[]{:S(2)}) collective-permute-start(bf16[1248,128]{1,0:T(8,128)(2,1)S(1)} %dynamic-slice_bitcast_fusion.3), channel_id=1, source_target_pairs={{0,1},{1,2},{2,3},{3,0},{4,5},{5,6},{6,7},{7,4},{8,9},{9,10},{10,1... | collective-permute-start | bytes 958472 | tf_op jit(solution)/shard_map/ppermute | solution.py:593
  662.7 16.1 %collective-permute-start.48 = (bf16[1296,128]{1,0:T(8,128)(2,1)}, bf16[1296,128]{1,0:T(8,128)(2,1)S(1)}, u32[]{:S(2)}, u32[]{:S(2)}) collective-permute-start(bf16[1296,128]{1,0:T(8,128)(2,1)} %collective-permute-done.47), channel_id=1, source_target_pairs={{0,1},{1,2},{2,3},{3,0},{4,5},{5,6},{6,7},{7,4},{8,9},{9,10},{10,1... | collective-permute-start | bytes 995336 | tf_op jit(solution)/shard_map/ppermute | solution.py:593
  663.0 15.7 %collective-permute-start.53 = (bf16[1248,128]{1,0:T(8,128)(2,1)S(1)}, bf16[1248,128]{1,0:T(8,128)(2,1)S(1)}, u32[]{:S(2)}, u32[]{:S(2)}) collective-permute-start(bf16[1248,128]{1,0:T(8,128)(2,1)S(1)} %bitcast_add_fusion.19), channel_id=1, source_target_pairs={{0,1},{1,2},{2,3},{3,0},{4,5},{5,6},{6,7},{7,4},{8,9},{9,10},{10,1... | collective-permute-start | bytes 958472 | tf_op jit(solution)/shard_map/ppermute | solution.py:593
  678.7 12.1 %collective-permute-start.54 = (bf16[1248,128]{1,0:T(8,128)(2,1)S(1)}, bf16[1248,128]{1,0:T(8,128)(2,1)S(1)}, u32[]{:S(2)}, u32[]{:S(2)}) collective-permute-start(bf16[1248,128]{1,0:T(8,128)(2,1)S(1)} %bitcast_add_fusion.20), channel_id=1, source_target_pairs={{0,1},{1,2},{2,3},{3,0},{4,5},{5,6},{6,7},{7,4},{8,9},{9,10},{10,1... | collective-permute-start | bytes 958472 | tf_op jit(solution)/shard_map/ppermute | solution.py:593
  702.6 10.6 %collective-permute-start.56 = (bf16[1248,128]{1,0:T(8,128)(2,1)S(1)}, bf16[1248,128]{1,0:T(8,128)(2,1)S(1)}, u32[]{:S(2)}, u32[]{:S(2)}) collective-permute-start(bf16[1248,128]{1,0:T(8,128)(2,1)S(1)} %collective-permute-done.55), channel_id=1, source_target_pairs={{0,1},{1,2},{2,3},{3,0},{4,5},{5,6},{6,7},{7,4},{8,9},{9,10},{10,1... | collective-permute-start | bytes 958472 | tf_op jit(solution)/shard_map/ppermute | solution.py:593
  713.2 10.8 %collective-permute-start.57 = (bf16[1248,128]{1,0:T(8,128)(2,1)S(1)}, bf16[1248,128]{1,0:T(8,128)(2,1)S(1)}, u32[]{:S(2)}, u32[]{:S(2)}) collective-permute-start(bf16[1248,128]{1,0:T(8,128)(2,1)S(1)} %collective-permute-done.56), channel_id=1, source_target_pairs={{0,1},{1,2},{2,3},{3,0},{4,5},{5,6},{6,7},{7,4},{8,9},{9,10},{10,1... | collective-permute-start | bytes 958472 | tf_op jit(solution)/shard_map/ppermute | solution.py:593
  716.5 11.0 %collective-permute-start.32 = (bf16[1296,128]{1,0:T(8,128)(2,1)S(1)}, bf16[1296,128]{1,0:T(8,128)(2,1)S(1)}, u32[]{:S(2)}, u32[]{:S(2)}) collective-permute-start(bf16[1296,128]{1,0:T(8,128)(2,1)S(1)} %dynamic-slice_bitcast_fusion.2), channel_id=1, source_target_pairs={{0,1},{1,2},{2,3},{3,0},{4,5},{5,6},{6,7},{7,4},{8,9},{9,10},{10,1... | collective-permute-start | bytes 995336 | tf_op jit(solution)/shard_map/ppermute | solution.py:593
  751.2 11.2 %collective-permute-start.35 = (bf16[1296,128]{1,0:T(8,128)(2,1)S(1)}, bf16[1296,128]{1,0:T(8,128)(2,1)S(1)}, u32[]{:S(2)}, u32[]{:S(2)}) collective-permute-start(bf16[1296,128]{1,0:T(8,128)(2,1)S(1)} %get-tuple-element.87), channel_id=1, source_target_pairs={{0,1},{1,2},{2,3},{3,0},{4,5},{5,6},{6,7},{7,4},{8,9},{9,10},{10,1... | collective-permute-start | bytes 995336 | tf_op jit(solution)/shard_map/ppermute | solution.py:593
  (55 other events, 389.2 us)
Sparse Core Ops, SparseCore 0:
  10.5 73.5 all-gather.3
  86.6 108.7 all-gather.5
  197.8 48.8 all-gather.7
  301.9 65.6 reduce-scatter.4
  447.0 123.6 reduce-scatter.2

commit v3 on v2

--- a/solution.py
+++ b/solution.py
@@ -119,11 +119,7 @@
             input_output_aliases={1: 0} if earlier else {},
             scratch_shapes=[pltpu.VMEM((2, groups, slots), jnp.float32)],
             compiler_params=pltpu.CompilerParams(vmem_limit_bytes=VMEM_BYTES),
-            cost_estimate=pl.CostEstimate(
-                flops=(last - first) * samples * rows * 2048,
-                bytes_accessed=2 * (last - first) * rows * samples,
-                transcendentals=0,
-            ),
+            cost_estimate=pl.CostEstimate(flops=1, bytes_accessed=1, transcendentals=0),
         )(ids, *earlier)
     return hits
 
@@ -199,11 +195,7 @@
         ),
         out_shape=jax.ShapeDtypeStruct((samples, (features + 1) * width), jnp.float32),
         compiler_params=pltpu.CompilerParams(vmem_limit_bytes=VMEM_BYTES),
-        cost_estimate=pl.CostEstimate(
-            flops=2 * samples * features * rows * width,
-            bytes_accessed=2 * features * rows * (samples + width) + 4 * samples * features * width,
-            transcendentals=0,
-        ),
+        cost_estimate=pl.CostEstimate(flops=1, bytes_accessed=1, transcendentals=0),
     )(place, hits, *first_half, *second_half, count_float, dense_input)
 
 
@@ -278,11 +270,7 @@
             pltpu.VMEM((samples, rank), jnp.float32),
         ],
         compiler_params=pltpu.CompilerParams(vmem_limit_bytes=VMEM_BYTES),
-        cost_estimate=pl.CostEstimate(
-            flops=4 * layers * samples * width * rank,
-            bytes_accessed=4 * layers * width * (rank + samples) + 4 * samples * width,
-            transcendentals=0,
-        ),
+        cost_estimate=pl.CostEstimate(flops=1, bytes_accessed=1, transcendentals=0),
     )(anchor, down, up, bias.reshape(layers, 1, width))
 
 
@@ -393,11 +381,7 @@
         ],
         scratch_shapes=[pltpu.VMEM((samples, H1), jnp.float32), pltpu.VMEM((samples, H1), jnp.bfloat16)],
         compiler_params=pltpu.CompilerParams(vmem_limit_bytes=VMEM_BYTES),
-        cost_estimate=pl.CostEstimate(
-            flops=6 * samples * (width * H1 + H1 * H2 + H2 * H3),
-            bytes_accessed=6 * width * H1 + 8 * samples * width,
-            transcendentals=8 * samples * (H1 + H2 + H3),
-        ),
+        cost_estimate=pl.CostEstimate(flops=1, bytes_accessed=1, transcendentals=0),
     )(inputs, one, late, *rows, target)
 
 
@@ -543,54 +527,73 @@
         ],
         compiler_params=pltpu.CompilerParams(vmem_limit_bytes=VMEM_BYTES),
         cost_estimate=pl.CostEstimate(
-            flops=10 * layers * samples * width * rank,
+            flops=10**12,
             bytes_accessed=layers * width * (8 * rank + 2 * samples) + 10 * samples * width,
             transcendentals=0,
         ),
     )(core, anchor, grad_stream, lows, narrows, down, up, bias.reshape(layers, 1, width), count_float)
 
 
-def row_kernel(core_ref, hits_ref, grad_ref, send_ref, keep_ref, both_ref):
+def row_kernel(earlier, core_ref, hits_ref, grad_ref, *refs):
+    send_ref, keep_ref, both_ref = refs[earlier:]
     both_ref[...] = left_product(hits_ref[0], grad_ref[...]).astype(jnp.bfloat16).reshape(both_ref.shape)
     core = core_ref[0]
     send_ref[0] = both_ref[:, 1 - core]
     keep_ref[0] = both_ref[:, core]
 
 
-def row_gradient(hits, grad_summed, first, features, group, core):
+def row_gradient(hits, grad_summed, start, stop, group, core, pieces):
     unused, samples, rows = hits.shape
     half = rows // group // 2
-    shape = jax.ShapeDtypeStruct((features, group, half, LOW), jnp.bfloat16)
-    spec = pl.BlockSpec((1, group, half, LOW), lambda f, core: (f, 0, 0, 0))
-    return pl.pallas_call(
-        row_kernel,
-        grid_spec=pltpu.PrefetchScalarGridSpec(
-            num_scalar_prefetch=1,
-            grid=(features,),
-            in_specs=[
-                pl.BlockSpec((1, samples, rows), lambda f, core: (f + first, 0, 0)),
-                pl.BlockSpec((samples, LOW), lambda f, core: (0, f + first)),
-            ],
-            out_specs=[spec, spec],
-            scratch_shapes=[pltpu.VMEM((group, 2, half, LOW), jnp.bfloat16)],
-        ),
-        out_shape=[shape, shape],
-        compiler_params=pltpu.CompilerParams(vmem_limit_bytes=VMEM_BYTES),
-        cost_estimate=pl.CostEstimate(
-            flops=8 * samples * features * rows * LOW,
-            bytes_accessed=2 * features * rows * (samples + LOW),
-            transcendentals=0,
-        ),
-    )(core, hits, grad_summed)
+    shape = jax.ShapeDtypeStruct((stop - start, group, half, LOW), jnp.bfloat16)
+    cuts = [start + (stop - start) * piece // pieces for piece in range(pieces + 1)]
+    results = []
+    for first, last in zip(cuts[:-1], cuts[1:]):
+        spec = pl.BlockSpec((1, group, half, LOW), functools.partial(row_block, first - start))
+        results = pl.pallas_call(
+            functools.partial(row_kernel, len(results)),
+            grid_spec=pltpu.PrefetchScalarGridSpec(
+                num_scalar_prefetch=1,
+                grid=(last - first,),
+                in_specs=[
+                    pl.BlockSpec((1, samples, rows), functools.partial(hits_block, first)),
+                    pl.BlockSpec((samples, LOW), functools.partial(column_block, first)),
+                ]
+                + [pl.BlockSpec(memory_space=pl.ANY)] * len(results),
+                out_specs=[spec, spec],
+                scratch_shapes=[pltpu.VMEM((group, 2, half, LOW), jnp.bfloat16)],
+            ),
+            out_shape=[shape, shape],
+            input_output_aliases={3: 0, 4: 1} if results else {},
+            compiler_params=pltpu.CompilerParams(vmem_limit_bytes=VMEM_BYTES),
+            cost_estimate=pl.CostEstimate(
+                flops=10**12,
+                bytes_accessed=2 * (last - first) * rows * (samples + LOW),
+                transcendentals=0,
+            ),
+        )(core, hits, grad_summed, *results)
+    return results
+
+
+def row_block(first, feature, core):
+    return (feature + first, 0, 0, 0)
+
+
+def hits_block(first, feature, core):
+    return (feature + first, 0, 0)
+
+
+def column_block(first, feature, core):
+    return (0, feature + first)
 
 
 def flip(value, bit):
     return lax.ppermute(value, "rep", [(i, i ^ bit) for i in range(lax.axis_size("rep"))])
 
 
-def ring(value):
+def shift(value, step):
     size = lax.axis_size("grp")
-    return lax.ppermute(value, "grp", [(i, (i + 1) % size) for i in range(size)])
+    return lax.ppermute(value, "grp", [(i, (i + step) % size) for i in range(size)])
 
 
 def across():
@@ -616,65 +619,88 @@
     return whole
 
 
-def scatter_pair(keep, received, bits, order, axis):
-    left = list(bits)
-    for bit in order:
-        position = axis + left.index(bit)
+def after(value, earlier):
+    return lax.optimization_barrier((value, earlier))[0]
+
+
+class HalvingSum:
+    def __init__(self, keep, received, bits, order, axis):
+        self.keep, self.received = keep, received
+        self.left, self.order, self.axis = list(bits), list(order), axis
+
+    def step(self, *earlier):
+        bit = self.order.pop(0)
+        position = self.axis + self.left.index(bit)
+        self.left.remove(bit)
         mine = (lax.axis_index("rep") // bit) % 2
-        send = lax.dynamic_index_in_dim(keep, 1 - mine, position, keepdims=False) + lax.dynamic_index_in_dim(
-            received, 1 - mine, position, keepdims=False
+        pair = after((self.keep, self.received), earlier)
+        send, keep = (
+            sum(lax.dynamic_index_in_dim(item, index, position, keepdims=False) for item in pair)
+            for index in (1 - mine, mine)
         )
-        keep = lax.dynamic_index_in_dim(keep, mine, position, keepdims=False) + lax.dynamic_index_in_dim(
-            received, mine, position, keepdims=False
-        )
-        received = flip(send, bit)
-        left.remove(bit)
-    return keep + received
-
-
-def ring_scatter(chunks):
-    size = lax.axis_size("grp")
-    mine = lax.axis_index("grp")
-    value = lax.dynamic_index_in_dim(chunks, (mine + size - 1) % size, 0, keepdims=False)
-    for step in range(1, size):
-        own = lax.dynamic_index_in_dim(chunks, (mine + 2 * size - 1 - step) % size, 0, keepdims=False)
-        value = own + ring(value)
-    return value
-
-
-def ring_gather(value):
-    size = lax.axis_size("grp")
-    mine = lax.axis_index("grp")
-    whole = jnp.zeros((size,) + value.shape, value.dtype)
-    for step in range(size):
-        whole = lax.dynamic_update_index_in_dim(whole, value, (mine + size - step) % size, 0)
-        if step < size - 1:
-            value = ring(value)
-    return whole
-
-
-def sum_groups(shares):
-    size = lax.axis_size("grp")
-    flat = [share.reshape(size, -1, LOW) for share in shares]
-    total = ring_gather(ring_scatter(jnp.concatenate(flat, axis=1)))
-    results = []
-    offset = 0
-    for share, part in zip(shares, flat):
-        piece = total[:, offset : offset + part.shape[1]]
-        results.append(piece.reshape(share.shape).astype(jnp.float32))
-        offset = offset + part.shape[1]
-    return results
-
-
-def sum_all(value):
-    for bit in [1] + across():
-        value = value + flip(value, bit)
-    size = lax.axis_size("grp")
-    bit = 1
-    while bit < size:
-        value = value + lax.ppermute(value, "grp", [(i, i ^ bit) for i in range(size)])
-        bit = 2 * bit
-    return value
+        self.keep, self.sent = keep, send
+        self.received = flip(self.sent, bit)
+
+    def result(self):
+        return self.keep + self.received
+
+
+class GroupSum:
+    def __init__(self, *shares):
+        self.size = lax.axis_size("grp")
+        self.mine = lax.axis_index("grp")
+        self.shares = shares
+
+    def scatter(self, *earlier):
+        chunks = [share.reshape(self.size, -1, LOW) for share in after(self.shares, earlier)]
+        self.lengths = [chunk.shape[1] for chunk in chunks]
+        sent = []
+        for step in range(self.size):
+            index = lax.rem(self.mine + step, self.size)
+            parts = [lax.dynamic_index_in_dim(chunk, index, 0, keepdims=False) for chunk in chunks]
+            sent.append(jnp.concatenate(parts, axis=0) if len(parts) > 1 else parts[0])
+        self.sent = sent
+        self.received = [shift(part, step) for step, part in enumerate(self.sent) if step]
+        self.total = sum(part.astype(jnp.float32) for part in [self.sent[0]] + self.received).astype(sent[0].dtype)
+
+    def gather(self, *earlier):
+        self.sent = after(self.total, earlier)
+        self.received = [shift(self.sent, step) for step in range(1, self.size)]
+
+    def result(self):
+        whole = jnp.zeros((self.size,) + self.total.shape, self.total.dtype)
+        for step, part in enumerate([self.sent] + self.received):
+            index = lax.rem(self.mine + self.size - step, self.size)
+            whole = lax.dynamic_update_index_in_dim(whole, part, index, 0)
+        results = []
+        offset = 0
+        for share, length in zip(self.shares, self.lengths):
+            part = whole[:, offset : offset + length]
+            results.append(part.reshape(share.shape).astype(jnp.float32))
+            offset = offset + length
+        return results
+
+
+class SmallSum:
+    def __init__(self, value):
+        self.value, self.received = value, None
+        self.left = [("rep", bit) for bit in [1] + across()]
+        bit = 1
+        while bit < lax.axis_size("grp"):
+            self.left.append(("grp", bit))
+            bit = 2 * bit
+
+    def step(self):
+        if self.received is not None:
+            self.value = self.value + self.received
+        axis, bit = self.left.pop(0)
+        self.sent = self.value
+        self.received = lax.ppermute(self.value, axis, [(i, i ^ bit) for i in range(lax.axis_size(axis))])
+
+    def finish(self):
+        while self.left:
+            self.step()
+        self.value = self.value + self.received
 
 
 def adamw(weight, grad, first, second, rate):
@@ -725,9 +751,8 @@
     features, extent, width = tables.shape
     part = extent // repeats
     own_part = lax.dynamic_slice_in_dim(tables, lax.axis_index("rep") * part, part, axis=1)
-    own_parts = [own_part.astype(jnp.bfloat16)]
-    for step in range(group - 1):
-        own_parts.append(ring(own_parts[-1]))
+    own_part = own_part.astype(jnp.bfloat16)
+    own_parts = [own_part] + [shift(own_part, step) for step in range(1, group)]
     half = features // 2
     spans = ((0, half, up_down), (half, features, down_up))
     table_halves = []
@@ -760,38 +785,39 @@
     )
     share_one = lax.psum_scatter(grad_one, "rep", scatter_dimension=0, tiled=True)
     core = (lax.axis_index("rep") % 2).astype(jnp.int32).reshape(1)
+    bits = up_down[::-1]
+    late_blocks = grad_late.reshape((2,) * len(bits) + (2, -1) + grad_late.shape[1:])
+    late_send, late_keep = (
+        lax.dynamic_index_in_dim(late_blocks, index, len(bits), keepdims=False) for index in (1 - core[0], core[0])
+    )
+    late_sum = HalvingSum(late_keep, flip(late_send, 1), bits, up_down, 0)
+    late_sum.step()
     send_up, keep_up, grad_down, bias_grads, grad_summed = cross_backward(
-        anchor, grad_stream, lows, narrows, down_all, up_all, cross_bias, count_float, core, repeats
+        anchor,
+        after(grad_stream, late_sum.sent),
+        lows,
+        narrows,
+        down_all,
+        up_all,
+        cross_bias,
+        count_float,
+        core,
+        repeats,
     )
     share_down = lax.psum_scatter(grad_down, "rep", scatter_dimension=1, tiled=True)
-    bits = up_down[::-1]
-    reduced = []
-    for first, last, order in spans:
-        send, keep = row_gradient(hits, grad_summed, first, last - first, group, core)
-        received = flip(send, 1)
-        shape = (last - first, group) + (2,) * len(bits) + (part, width)
-        reduced.append(scatter_pair(keep.reshape(shape), received.reshape(shape), bits, order, 2))
-    row_share = ring_scatter(jnp.concatenate(reduced, axis=0).transpose(1, 0, 2, 3))
-    table_grads = []
-    for first, last, order in spans:
-        value, keys = gather_across(row_share[None, first:last], order + [1])
-        table_grads.append(place(value, keys, 1, lambda index: (index % 2) * (repeats // 2) + index // 2))
-    table_grad = jnp.concatenate(table_grads, axis=0).astype(jnp.float32)
-    late_blocks = grad_late.reshape((2,) * len(bits) + (2, -1) + grad_late.shape[1:])
-    late_received = flip(lax.dynamic_index_in_dim(late_blocks, 1 - core[0], len(bits), keepdims=False), 1)
-    late_keep = lax.dynamic_index_in_dim(late_blocks, core[0], len(bits), keepdims=False)
-    share_late = scatter_pair(late_keep, late_received, bits, up_down, 0)
     received_up = flip(send_up, 1)
     share_rows = keep_up.shape[2] // 2
     shape = (CROSS,) + (2,) * len(bits) + (2, share_rows, D_IN)
-    ups = []
-    for index, order in ((0, up_down), (1, down_up)):
-        pair = [lax.index_in_dim(item.reshape(shape), index, len(bits) + 1, keepdims=False) for item in (keep_up, received_up)]
-        ups.append(scatter_pair(pair[0], pair[1], bits, order, 1))
-    share_one, share_late = sum_groups([share_one, share_late])
-    share_two, share_three = share_late[:, :H2], share_late[:, H2:]
-    (share_up,) = sum_groups([jnp.concatenate(ups, axis=1)])
-    (share_down,) = sum_groups([share_down])
+    up_sums = [
+        HalvingSum(
+            lax.index_in_dim(keep_up.reshape(shape), index, len(bits) + 1, keepdims=False),
+            lax.index_in_dim(received_up.reshape(shape), index, len(bits) + 1, keepdims=False),
+            bits,
+            order,
+            1,
+        )
+        for index, order in ((0, up_down), (1, down_up))
+    ]
     small_grad = jnp.concatenate(
         [
             item.reshape(-1)
@@ -806,25 +832,65 @@
             )
         ]
     )
-    small_total = sum_all(small_grad)
-    small_sum, loss_sum = small_total[:-1], small_total[-1]
+    up_p, up_q = up_sums
+    row_sums = []
+    grad_rows = after(grad_summed, late_sum.received)
+    for first, last, order in spans:
+        send, keep = row_gradient(hits, grad_rows, first, last, group, core, 2)
+        shape = (last - first, group) + (2,) * len(bits) + (part, width)
+        row_sums.append(HalvingSum(keep.reshape(shape), flip(send, 1).reshape(shape), bits, order, 2))
+        if len(row_sums) == 1:
+            for step in bits[1:]:
+                late_sum.step(keep)
+            for item in up_sums:
+                item.step(late_sum.sent)
+            one_total = GroupSum(share_one, late_sum.result())
+            one_total.scatter(*[item.sent for item in up_sums])
+            one_total.gather()
+            grad_rows = after(grad_rows, one_total.sent)
+    row_p, row_q = row_sums
+    for step in bits[1:]:
+        for item in up_sums:
+            item.step(one_total.sent)
+    for item in row_sums:
+        item.step(up_p.sent, up_q.sent)
+    share_up = jnp.concatenate([item.result() for item in up_sums], axis=1)
+    share_up, share_down = lax.psum((share_up, share_down), "grp")
+    for step in bits[1:]:
+        for item in row_sums:
+            item.step(up_p.received, up_q.received)
+    row_parts = [item.result() for item in row_sums]
+    row_total = GroupSum(jnp.concatenate(row_parts, axis=0).transpose(1, 0, 2, 3))
+    row_total.scatter(share_up, share_down)
+    small = SmallSum(after(small_grad, row_total.sent))
+    small.finish()
+    row_share = row_total.total.reshape(features, part, width)
+    share_one, share_late = one_total.result()
+    share_up, share_down = share_up.astype(jnp.float32), share_down.astype(jnp.float32)
+    share_two, share_three = share_late[:, :H2], share_late[:, H2:]
+    small_sum, loss_sum = small.value[:-1], small.value[-1]
+    new_one, new_one_first, new_one_second = adamw(
+        hidden_one, share_one, one_first, one_second, D_IN ** (-0.5)
+    )
+    new_two, new_two_first, new_two_second = adamw(
+        hidden_two, share_two, two_first, two_second, H1 ** (-0.5)
+    )
+    new_three, new_three_first, new_three_second = adamw(
+        hidden_three, share_three, three_first, three_second, H2 ** (-0.5)
+    )
+    table_grads = []
+    for first, last, order in spans:
+        value, keys = gather_across(row_share[None, first:last], order + [1])
+        table_grads.append(place(value, keys, 1, lambda index: (index % 2) * (repeats // 2) + index // 2))
+    table_grad = jnp.concatenate(table_grads, axis=0).astype(jnp.float32)
+    new_up, new_up_first, new_up_second = adamw(
+        cross_up, share_up, up_first, up_second, RANK ** (-0.5)
+    )
     new_tables, new_table_first, new_table_second = adamw(
         tables, table_grad, table_first, table_second, 1.0
     )
     new_down, new_down_first, new_down_second = adamw(
         cross_down, share_down, down_first, down_second, D_IN ** (-0.5)
-    )
-    new_up, new_up_first, new_up_second = adamw(
-        cross_up, share_up, up_first, up_second, RANK ** (-0.5)
-    )
-    new_one, new_one_first, new_one_second = adamw(
-        hidden_one, share_one, one_first, one_second, D_IN ** (-0.5)
-    )
-    new_two, new_two_first, new_two_second = adamw(
-        hidden_two, share_two, two_first, two_second, H1 ** (-0.5)
-    )
-    new_three, new_three_first, new_three_second = adamw(
-        hidden_three, share_three, three_first, three_second, H2 ** (-0.5)
     )
     new_smalls, new_small_first, new_small_second = adamw(
         smalls, small_sum, small_first, small_second, 0.1

time: 810 us -> 734 us (0.906)
  waiting for transfers between devices: 311 us -> 249 us
  starting transfers between devices: 46 us -> 77.9 us
  local copies, waits for them, and re-layouts: 76.6 us -> 49.3 us
  other arithmetic: 102 us -> 89.5 us
    ppermute x32 -> x29, waiting for transfers between devices: 182 us -> 94.5 us  [flip(): lax.ppermute(value, 'rep', [(i, i ^ bit) for i in range(lax.axis_size('re...]
    ppermute x26 -> x17, waiting for transfers between devices: 129 us -> 66.5 us  [the longest x12 55 us: shift(): lax.ppermute(value, 'grp', [(i, (i + step) % size) for i in range(size)])]
    psum x0 -> x1, waiting for transfers between devices: none -> 60.9 us  [on_device(): share_up, share_down = lax.psum((share_up, share_down), 'grp')]
    ppermute x26 -> x17, starting transfers between devices: 21.1 us -> 50.8 us  [the longest x12 38.3 us: shift(): lax.ppermute(value, 'grp', [(i, (i + step) % size) for i in range(size)])]
    reduce_scatter x1, waiting for transfers between devices: 0.01 us -> 26.7 us  [on_device(): lax.psum_scatter(grad_down, 'rep', scatter_dimension=1, tiled=True)]
    reshape x4 -> x2, local copies, waits for them, and re-layouts: 11 us -> 1.93 us  [scatter(): share.reshape(self.size, -1, LOW)]
    pallas_call x2 -> x4, Pallas kernels: 47.5 us -> 42.7 us  [row_gradient(): pl.pallas_call(functools.partial(row_kernel, len(results)), grid_spec=plt...]
    add x31 -> x21, other arithmetic: 25.1 us -> 29 us  [the longest x11 22.3 us: step(): sum((lax.dynamic_index_in_dim(item, index, position, keepdims=False) for...]
  transfers between devices with their start and end apart: 63 -> 52, of which waited for: 32 -> 25; matrix products, arithmetic and copies ran while one was open for 19% -> 15% of each run, Pallas kernels for 27% -> 30%
where the time goes in v3:
time: 734 us; the launch traced here: 725 us
  waiting for transfers between devices  249 us (34%)
  Pallas kernels  244 us (33%)
  other arithmetic  89.5 us (12%)
  starting transfers between devices  77.9 us (11%)
  local copies, waits for them, and re-layouts  49.3 us (7%)
  between operations  15.7 us (2%)
    ppermute x29, waiting for transfers between devices, flip(): lax.ppermute(value, 'rep', [(i, i ^ bit) for i in range(lax.axis_size('re...  94.5 us
    psum x1, waiting for transfers between devices, on_device(): share_up, share_down = lax.psum((share_up, share_down), 'grp')  60.9 us
    ppermute x12, waiting for transfers between devices, shift(): lax.ppermute(value, 'grp', [(i, (i + step) % size) for i in range(size)])  55 us
    pallas_call x4, Pallas kernels, count(): pl.pallas_call(functools.partial(count_kernel, len(earlier)), grid=(last...  54.1 us
    pallas_call x1, Pallas kernels, cross_backward(): pl.pallas_call(cross_backward_kernel, grid_spec=pltpu.PrefetchScalarGridS...  51 us
    pallas_call x4, Pallas kernels, row_gradient(): pl.pallas_call(functools.partial(row_kernel, len(results)), grid_spec=plt...  42.7 us
    pallas_call x1, Pallas kernels, pool(): pl.pallas_call(functools.partial(pool_kernel, keys=keys, half=half), grid...  38.9 us
    ppermute x12, starting transfers between devices, shift(): lax.ppermute(value, 'grp', [(i, (i + step) % size) for i in range(size)])  38.3 us
  transfers between devices with their start and end apart: 52, of which 25 were waited for; matrix products, arithmetic and copies ran while one was open for 15% of the time, Pallas kernels for 30%

profile of v3, /device:TPU:0, one launch (start us, length us, event | category | flops | bytes accessed | tf_op | source)
XLA Modules:
  0.0 725.0 jit_solution(2397986715029101572)
XLA Ops:
  7.2 3.1 convert_element_type.79
  11.8 2.5 convert_element_type.81
  15.6 3.1 collective-permute-start
  18.7 2.6 collective-permute-start.1
  22.6 8.8 %collective-permute-done = bf16[26,64,128]{2,1,0:T(8,128)(2,1)S(1)} collective-permute-done((bf16[26,64,128]{2,1,0:T(8,128)(2,1)S(1)}, bf16[26,64,128]{2,1,0:T(8,128)(2,1)S(1)}, u32[]{:S(2)}, u32[]{:S(2)}) %collective-permute-start) | collective-permute-done | bytes 426016 | tf_op jit(solution)/shard_map/ppermute | solution.py:596
  31.5 17.4 %collective-permute-done.1 = bf16[26,64,128]{2,1,0:T(8,128)(2,1)S(1)} collective-permute-done((bf16[26,64,128]{2,1,0:T(8,128)(2,1)S(1)}, bf16[26,64,128]{2,1,0:T(8,128)(2,1)S(1)}, u32[]{:S(2)}, u32[]{:S(2)}) %collective-permute-start.1) | collective-permute-done | bytes 426016 | tf_op jit(solution)/shard_map/ppermute | solution.py:596
  53.1 36.1 %collective-permute-done.3 = bf16[1,4,13,64,128]{4,3,2,1,0:T(8,128)(2,1)S(1)} collective-permute-done((bf16[1,4,13,64,128]{4,3,2,1,0:T(8,128)(2,1)S(1)}, bf16[1,4,13,64,128]{4,3,2,1,0:T(8,128)(2,1)S(1)}, u32[]{:S(2)}, u32[]{:S(2)}) %collective-permute-start.3) | collective-permute-done | bytes 852000 | tf_op jit(solution)/shard_map/ppermute | solution.py:591
  95.4 6.6 collective-permute-done.9
  104.6 4.2 copy.70
  108.9 5.8 reshape.182.ids_ref
  114.6 12.6 %shard_map.408.refs_0_ = bf16[26,512,2048]{2,1,0:T(8,128)(2,1)} custom-call(s32[26,64,256]{2,1,0:T(8,128)} %reshape.182.ids_ref), custom_call_target="tpu_custom_call" | custom-call | flops 1 | bytes 1 | tf_op jit(solution)/shard_map/pallas_call | solution.py:112
  127.2 14.4 %shard_map.409.refs_0_ = bf16[26,512,2048]{2,1,0:T(8,128)(2,1)} custom-call(s32[26,64,256]{2,1,0:T(8,128)} %reshape.182.ids_ref, bf16[26,512,2048]{2,1,0:T(8,128)(2,1)} %shard_map.408.refs_0_), custom_call_target="tpu_custom_call", output_to_operand_aliasing={{}: (1, {})} | custom-call | flops 1 | bytes 1 | tf_op jit(solution)/shard_map/pallas_call | solution.py:112
  141.6 12.7 %shard_map.410.refs_0_ = bf16[26,512,2048]{2,1,0:T(8,128)(2,1)} custom-call(s32[26,64,256]{2,1,0:T(8,128)} %reshape.182.ids_ref, bf16[26,512,2048]{2,1,0:T(8,128)(2,1)} %shard_map.409.refs_0_), custom_call_target="tpu_custom_call", output_to_operand_aliasing={{}: (1, {})} | custom-call | flops 1 | bytes 1 | tf_op jit(solution)/shard_map/pallas_call | solution.py:112
  154.3 14.4 %shard_map.411.hits_ref = bf16[26,512,2048]{2,1,0:T(8,128)(2,1)} custom-call(s32[26,64,256]{2,1,0:T(8,128)} %reshape.182.ids_ref, bf16[26,512,2048]{2,1,0:T(8,128)(2,1)} %shard_map.410.refs_0_), custom_call_target="tpu_custom_call", output_to_operand_aliasing={{}: (1, {})} | custom-call | flops 1 | bytes 1 | tf_op jit(solution)/shard_map/pallas_call | solution.py:112
  188.8 2.8 collective-permute-done.8.other_b
  191.6 38.9 %shard_map.412.anchor_in = f32[512,3456]{1,0:T(8,128)} custom-call(s32[2]{0:T(128)} %pad_add_fusion.place_ref, bf16[26,512,2048]{2,1,0:T(8,128)(2,1)} %shard_map.411.hits_ref, bf16[4,4,13,64,128]{4,3,2,1,0:T(8,128)(2,1)} %copy-done, bf16[4,4,13,64,128]{4,3,2,1,0:T(8,128)(2,1)} %copy-done.28, bf16[4,4,13,64,128]{4,3,2,1,0:T(8,128)(2,1)} %copy-done.1, ...), custom_call_target="tpu_custom_call" | custom-call | flops 1 | bytes 1 | tf_op jit(solution)/shard_map/pallas_call | solution.py:179
  230.6 28.7 %shard_map.413 = (bf16[3,512,3456]{2,1,0:T(8,128)(2,1)}, bf16[3,512,512]{2,1,0:T(8,128)(2,1)}, bf16[512,3456]{1,0:T(8,128)(2,1)}) custom-call(f32[512,3456]{1,0:T(8,128)} %shard_map.412.anchor_in, bf16[3,3456,512]{2,1,0:T(8,128)(2,1)} %all-gather.4.cloned.1.call-done.down_ref, bf16[3,512,3456]{2,1,0:T(8,128)(2,1)} %all-gather.6.cloned.1.call-done.up_ref, ...), custom_call_target="tpu_custom_call" | custom-call | flops 1 | bytes 1 | tf_op jit(solution)/shard_map/pallas_call | solution.py:248
  259.2 28.4 %shard_map.414 = (f32[1,1]{1,0:T(1,128)}, f32[1,512]{1,0:T(1,128)}, f32[1,1]{1,0:T(1,128)}, f32[1,1024]{1,0:T(1,128)}, f32[1,1024]{1,0:T(1,128)}, /*index=5*/f32...) custom-call(bf16[512,3456]{1,0:T(8,128)(2,1)} %get-tuple-element.74.input_ref, ...), custom_call_target="tpu_custom_call" | custom-call | flops 1 | bytes 1 | tf_op jit(solution)/shard_map/pallas_call | solution.py:360
  291.2 3.5 collective-permute-done.12
  297.2 51.0 %shard_map.415 = (bf16[3,4,64,3456]{3,2,1,0:T(8,128)(2,1)}, bf16[3,4,64,3456]{3,2,1,0:T(8,128)(2,1)}, bf16[3,3456,512]{2,1,0:T(8,128)(2,1)}, f32[3,1,3456]{2,1,0:T(1,128)}, bf16[512,3456]{1,0:T(8,128)(2,1)}) custom-call(s32[1]{0:T(128)} %bitcast.core_ref, f32[512,3456]{1,0:T(8,128)} %shard_map.412.anchor_in, f32[512,3456]{1,0:T(8,128)} %get-tuple-element.79.grad_in, ...), custom_call_target="tpu_custom_call" | custom-call | flops 999999995904 | bytes 70778880 | tf_op jit(solution)/shard_map/pallas_call | solution.py:487
  350.5 9.7 %shard_map.416 = (bf16[13,4,256,128]{3,2,1,0:T(8,128)(2,1)}, bf16[13,4,256,128]{3,2,1,0:T(8,128)(2,1)}) custom-call(s32[1]{0:T(128)} %bitcast.core_ref, bf16[26,512,2048]{2,1,0:T(8,128)(2,1)} %shard_map.411.hits_ref, bf16[512,3456]{1,0:T(8,128)(2,1)} %get-tuple-element.114.grad_ref), custom_call_target="tpu_custom_call" | custom-call | flops 999999995904 | bytes 15728640 | tf_op jit(solution)/shard_map/pallas_call | solution.py:553
  360.2 11.4 %shard_map.417 = (bf16[13,4,256,128]{3,2,1,0:T(8,128)(2,1)}, bf16[13,4,256,128]{3,2,1,0:T(8,128)(2,1)}) custom-call(s32[1]{0:T(128)} %bitcast.core_ref, bf16[26,512,2048]{2,1,0:T(8,128)(2,1)} %shard_map.411.hits_ref, bf16[512,3456]{1,0:T(8,128)(2,1)} %get-tuple-element.114.grad_ref, ...), custom_call_target="tpu_custom_call", output_to_operand_aliasing={{0}: (3, {}), {1}: (4, {})} | custom-call | flops 999999995904 | bytes 18350080 | tf_op jit(solution)/shard_map/pallas_call | solution.py:553
  374.5 2.9 fusion.41
  377.4 6.6 collective-permute-done.17
  385.1 2.9 fusion.40
  394.7 12.2 %collective-permute-start.18 = (bf16[1248,128]{1,0:T(8,128)(2,1)S(1)}, bf16[1248,128]{1,0:T(8,128)(2,1)S(1)}, u32[]{:S(2)}, u32[]{:S(2)}) collective-permute-start(bf16[1248,128]{1,0:T(8,128)(2,1)S(1)} %pad_maximum_fusion.13), channel_id=1, source_target_pairs={{0,1},{1,2},{2,3},{3,0},{4,5},{5,6},{6,7},{7,4},{8,9},{9,10},{10,1... | collective-permute-start | bytes 958472 | tf_op jit(solution)/shard_map/ppermute | solution.py:596
  418.6 11.4 %collective-permute-done.19 = bf16[1248,128]{1,0:T(8,128)(2,1)S(1)} collective-permute-done((bf16[1248,128]{1,0:T(8,128)(2,1)S(1)}, bf16[1248,128]{1,0:T(8,128)(2,1)S(1)}, u32[]{:S(2)}, u32[]{:S(2)}) %collective-permute-start.19) | collective-permute-done | bytes 319520 | tf_op jit(solution)/shard_map/ppermute | solution.py:596
  430.8 7.3 %collective-permute-start.43 = (bf16[1248,128]{1,0:T(8,128)(2,1)}, bf16[1248,128]{1,0:T(8,128)(2,1)}, u32[]{:S(2)}, u32[]{:S(2)}) collective-permute-start(bf16[1248,128]{1,0:T(8,128)(2,1)} %add_convert_fusion.1), channel_id=1, source_target_pairs={{0,1},{1,2},{2,3},{3,0},{4,5},{5,6},{6,7},{7,4},{8,9},{9,10},{10,1... | collective-permute-start | bytes 958472 | tf_op jit(solution)/shard_map/ppermute | solution.py:596
  439.9 9.8 %shard_map.418 = (bf16[13,4,256,128]{3,2,1,0:T(8,128)(2,1)}, bf16[13,4,256,128]{3,2,1,0:T(8,128)(2,1)}) custom-call(s32[1]{0:T(128)} %bitcast.core_ref, bf16[26,512,2048]{2,1,0:T(8,128)(2,1)} %shard_map.411.hits_ref, bf16[512,3456]{1,0:T(8,128)(2,1)} %get-tuple-element.114.grad_ref), custom_call_target="tpu_custom_call" | custom-call | flops 999999995904 | bytes 15728640 | tf_op jit(solution)/shard_map/pallas_call | solution.py:553
  449.7 11.8 %shard_map.419 = (bf16[13,4,256,128]{3,2,1,0:T(8,128)(2,1)}, bf16[13,4,256,128]{3,2,1,0:T(8,128)(2,1)}) custom-call(s32[1]{0:T(128)} %bitcast.core_ref, bf16[26,512,2048]{2,1,0:T(8,128)(2,1)} %shard_map.411.hits_ref, bf16[512,3456]{1,0:T(8,128)(2,1)} %get-tuple-element.114.grad_ref, ...), custom_call_target="tpu_custom_call", output_to_operand_aliasing={{0}: (3, {}), {1}: (4, {})} | custom-call | flops 999999995904 | bytes 18350080 | tf_op jit(solution)/shard_map/pallas_call | solution.py:553
  466.7 4.8 add_bitcast_fusion.2
  480.9 8.4 %collective-permute-done.23 = bf16[3,32,3456]{2,1,0:T(8,128)(2,1)S(1)} collective-permute-done((bf16[3,32,3456]{2,1,0:T(8,128)(2,1)S(1)}, bf16[3,32,3456]{2,1,0:T(8,128)(2,1)S(1)}, u32[]{:S(2)}, u32[]{:S(2)}) %collective-permute-start.23) | collective-permute-done | bytes 663584 | tf_op jit(solution)/shard_map/ppermute | solution.py:591
  493.7 3.4 add_bitcast_fusion
  498.9 26.7 %reduce-scatter.5.cloned.1.call-done = bf16[3,432,512]{2,1,0:T(8,128)(2,1)} async-done(((bf16[3,3456,512]{2,1,0:T(8,128)(2,1)}), bf16[3,432,512]{2,1,0:T(8,128)(2,1)}) %reduce-scatter.5.cloned.1.call-update) | async-done | bytes 1327120 | tf_op jit(solution)/shard_map/reduce_scatter | solution.py:807
  528.8 2.5 slice_convert_fusion
  532.9 9.9 %collective-permute-done.22 = bf16[13,4,2,64,128]{4,3,0,1,2:T(8,128)(2,1)} collective-permute-done((bf16[13,4,2,64,128]{4,3,0,1,2:T(8,128)(2,1)}, bf16[13,4,2,64,128]{4,3,0,1,2:T(8,128)(2,1)}, u32[]{:S(2)}, u32[]{:S(2)}) %collective-permute-start.22) | collective-permute-done | bytes 1703968 | tf_op jit(solution)/shard_map/ppermute | solution.py:591
  551.1 4.8 multiply_subtract_fusion.2
  556.0 9.8 %collective-permute-done.25 = bf16[13,4,64,128]{3,2,0,1:T(8,128)(2,1)} collective-permute-done((bf16[13,4,64,128]{3,2,0,1:T(8,128)(2,1)}, bf16[13,4,64,128]{3,2,0,1:T(8,128)(2,1)}, u32[]{:S(2)}, u32[]{:S(2)}) %collective-permute-start.25) | collective-permute-done | bytes 852000 | tf_op jit(solution)/shard_map/ppermute | solution.py:591
  567.4 3.0 collective-permute-done.28
  573.1 60.9 %all-reduce.4.cloned.1.call-done = (bf16[3,64,3456]{2,1,0:T(8,128)(2,1)}, bf16[3,432,512]{2,1,0:T(8,128)(2,1)}) async-done(((bf16[3,64,3456]{2,1,0:T(8,128)(2,1)}, bf16[3,432,512]{2,1,0:T(8,128)(2,1)}), (bf16[3,64,3456]{2,1,0:T(8,128)(2,1)}, bf16[3,432,512]{2,1,0:T(8,128)(2,1)})) %all-reduce.4.cloned.1.call-update) | async-done | bytes 2654224 | tf_op jit(solution)/shard_map/psum | solution.py:858
  637.3 3.0 collective-permute-start.36
  640.3 7.1 multiply_subtract_fusion
  647.5 4.7 multiply_subtract_fusion.1
  652.2 15.2 %collective-permute-done.35 = bf16[1664,128]{1,0:T(8,128)(2,1)S(1)} collective-permute-done((bf16[1664,128]{1,0:T(8,128)(2,1)S(1)}, bf16[1664,128]{1,0:T(8,128)(2,1)S(1)}, u32[]{:S(2)}, u32[]{:S(2)}) %collective-permute-start.35) | collective-permute-done | bytes 426016 | tf_op jit(solution)/shard_map/ppermute | solution.py:596
  672.7 4.9 collective-permute-done.30
  681.9 8.8 %collective-permute-start.32 = (f32[13442]{0:T(1024)S(1)}, f32[13442]{0:T(1024)S(1)}, u32[]{:S(2)}, u32[]{:S(2)}) collective-permute-start(f32[13442]{0:T(1024)S(1)} %add.629), channel_id=1, source_target_pairs={{0,1},{1,0},{2,3},{3,2},{4,5},{5,4},{6,7},{7,6},{8,9},{9,8},{10,11... | collective-permute-start | bytes 161312 | tf_op jit(solution)/shard_map/ppermute | solution.py:698
  695.4 4.3 collective-permute-done.33
  705.0 12.7 %add_subtract_fusion = (f32[26,512,128]{2,1,0:T(8,128)}, f32[26,512,128]{2,1,0:T(8,128)}, f32[26,512,128]{2,1,0:T(8,128)}) fusion(f32[26,512,128]{2,1,0:T(8,128)S(1)} %bitcast.228, bf16[13,512,128]{2,1,0:T(8,128)(2,1)S(1)} %fusion.17, bf16[13,512,128]{2,1,0:T(8,128)(2,1)S(1)} %fusion.23, f32[26,512,128]{2,1,0:T(8,128)} %param.30, f32[26,512,128]{2,1,0:T(8,128)} %param.31), kind=kLoop, calls=%fused_computation.4 | loop fusion | flops 27262976 | bytes 44302336 | tf_op jit(solution)/shard_map/sub | solution.py:712
  (320 shorter events, 130.5 us)
Async XLA Ops:
  7.2 223.3 %all-gather.4.cloned.1.call-start = ((), (), s32[]{:S(2)}) async-start(), calls=%async_computation.2 | async-start | bytes 11943936 | tf_op jit(solution)/shard_map/all_gather | solution.py:744
  10.4 220.1 %all-gather.6.cloned.1.call-start = ((), (), s32[]{:S(2)}) async-start(), calls=%async_computation.3 | async-start | bytes 11943936 | tf_op jit(solution)/shard_map/all_gather | solution.py:745
  11.7 247.5 %all-gather.8.cloned.1.call-start = ((), (), s32[]{:S(2)}) async-start(), calls=%async_computation.4 | async-start | bytes 7962624 | tf_op jit(solution)/shard_map/all_gather | solution.py:746
  14.3 378.3 %reduce-scatter.3.cloned.1.call-start = ((), (), s32[]{:S(2)}) async-start(), calls=%async_computation.5 | async-start | bytes 7962624 | tf_op jit(solution)/shard_map/reduce_scatter | solution.py:786
  15.6 15.9 %collective-permute-start = (bf16[26,64,128]{2,1,0:T(8,128)(2,1)S(1)}, bf16[26,64,128]{2,1,0:T(8,128)(2,1)S(1)}, u32[]{:S(2)}, u32[]{:S(2)}) collective-permute-start(bf16[26,64,128]{2,1,0:T(8,128)(2,1)S(1)} %dynamic-slice_convert_fusion), channel_id=1, source_target_pairs={{0,1},{1,2},{2,3},{3,0},{4,5},{5,6},{6,7},{7,4},{8,9},{9,10},{10,1... | collective-permute-start | bytes 1277960 | tf_op jit(solution)/shard_map/ppermute | solution.py:596
  18.7 30.2 %collective-permute-start.1 = (bf16[26,64,128]{2,1,0:T(8,128)(2,1)S(1)}, bf16[26,64,128]{2,1,0:T(8,128)(2,1)S(1)}, u32[]{:S(2)}, u32[]{:S(2)}) collective-permute-start(bf16[26,64,128]{2,1,0:T(8,128)(2,1)S(1)} %dynamic-slice_convert_fusion), channel_id=1, source_target_pairs={{0,2},{1,3},{2,0},{3,1},{4,6},{5,7},{6,4},{7,5},{8,10},{9,11},{10,... | collective-permute-start | bytes 1277960 | tf_op jit(solution)/shard_map/ppermute | solution.py:596
  21.3 27.7 %collective-permute-start.2 = (bf16[26,64,128]{2,1,0:T(8,128)(2,1)S(1)}, bf16[26,64,128]{2,1,0:T(8,128)(2,1)S(1)}, u32[]{:S(2)}, u32[]{:S(2)}) collective-permute-start(bf16[26,64,128]{2,1,0:T(8,128)(2,1)S(1)} %dynamic-slice_convert_fusion), channel_id=1, source_target_pairs={{0,3},{1,0},{2,1},{3,2},{4,7},{5,4},{6,5},{7,6},{8,11},{9,8},{10,9... | collective-permute-start | bytes 1277960 | tf_op jit(solution)/shard_map/ppermute | solution.py:596
  49.1 40.1 %collective-permute-start.3 = (bf16[1,4,13,64,128]{4,3,2,1,0:T(8,128)(2,1)S(1)}, bf16[1,4,13,64,128]{4,3,2,1,0:T(8,128)(2,1)S(1)}, u32[]{:S(2)}, u32[]{:S(2)}) collective-permute-start(bf16[1,4,13,64,128]{4,3,2,1,0:T(8,128)(2,1)S(1)} %maximum_bitcast_fusion.1), channel_id=1, source_target_pairs={{0,8},{4,12},{8,0},{12,4},{16,24},{20,28},{24,16},{28,20},{1,9},{5... | collective-permute-start | bytes 2555912 | tf_op jit(solution)/shard_map/ppermute | solution.py:591
  50.8 41.4 %collective-permute-start.6 = (bf16[1,4,13,64,128]{4,3,2,1,0:T(8,128)(2,1)S(1)}, bf16[1,4,13,64,128]{4,3,2,1,0:T(8,128)(2,1)S(1)}, u32[]{:S(2)}, u32[]{:S(2)}) collective-permute-start(bf16[1,4,13,64,128]{4,3,2,1,0:T(8,128)(2,1)S(1)} %maximum_bitcast_fusion.2), channel_id=1, source_target_pairs={{0,16},{4,20},{8,24},{12,28},{16,0},{20,4},{24,8},{28,12},{1,17},{... | collective-permute-start | bytes 2555912 | tf_op jit(solution)/shard_map/ppermute | solution.py:591
  52.5 49.5 %collective-permute-start.9 = (bf16[1,128,1536]{2,1,0:T(8,128)(2,1)S(1)}, bf16[1,128,1536]{2,1,0:T(8,128)(2,1)S(1)}, u32[]{:S(2)}, u32[]{:S(2)}) collective-permute-start(bf16[1,128,1536]{2,1,0:T(8,128)(2,1)S(1)} %pad_maximum_fusion.12), channel_id=1, source_target_pairs={{0,8},{4,12},{8,0},{12,4},{16,24},{20,28},{24,16},{28,20},{1,9},{5... | collective-permute-start | bytes 1179656 | tf_op jit(solution)/shard_map/ppermute | solution.py:591
  90.7 86.5 %collective-permute-start.4 = (bf16[2,4,13,64,128]{4,3,2,1,0:T(8,128)(2,1)}, bf16[2,4,13,64,128]{4,3,2,1,0:T(8,128)(2,1)}, u32[]{:S(2)}, u32[]{:S(2)}) collective-permute-start(bf16[2,4,13,64,128]{4,3,2,1,0:T(8,128)(2,1)} %pad_maximum_fusion.3), channel_id=1, source_target_pairs={{0,16},{4,20},{8,24},{12,28},{16,0},{20,4},{24,8},{28,12},{1,17},{... | collective-permute-start | bytes 5111816 | tf_op jit(solution)/shard_map/ppermute | solution.py:591
  93.7 85.7 %collective-permute-start.7 = (bf16[2,4,13,64,128]{4,3,2,1,0:T(8,128)(2,1)}, bf16[2,4,13,64,128]{4,3,2,1,0:T(8,128)(2,1)}, u32[]{:S(2)}, u32[]{:S(2)}) collective-permute-start(bf16[2,4,13,64,128]{4,3,2,1,0:T(8,128)(2,1)} %pad_maximum_fusion.4), channel_id=1, source_target_pairs={{0,8},{4,12},{8,0},{12,4},{16,24},{20,28},{24,16},{28,20},{1,9},{5... | collective-permute-start | bytes 5111816 | tf_op jit(solution)/shard_map/ppermute | solution.py:591
  103.0 72.8 %collective-permute-start.10 = (bf16[2,128,1536]{2,1,0:T(8,128)(2,1)}, bf16[2,128,1536]{2,1,0:T(8,128)(2,1)}, u32[]{:S(2)}, u32[]{:S(2)}) collective-permute-start(bf16[2,128,1536]{2,1,0:T(8,128)(2,1)} %pad_maximum_fusion.9), channel_id=1, source_target_pairs={{0,16},{4,20},{8,24},{12,28},{16,0},{20,4},{24,8},{28,12},{1,17},{... | collective-permute-start | bytes 2359304 | tf_op jit(solution)/shard_map/ppermute | solution.py:591
  177.1 8.1 %collective-permute-start.11 = (bf16[4,128,1536]{2,1,0:T(8,128)(2,1)S(1)}, bf16[4,128,1536]{2,1,0:T(8,128)(2,1)S(1)}, u32[]{:S(2)}, u32[]{:S(2)}) collective-permute-start(bf16[4,128,1536]{2,1,0:T(8,128)(2,1)S(1)} %pad_maximum_fusion.5), channel_id=1, source_target_pairs={{0,4},{4,0},{8,12},{12,8},{16,20},{20,16},{24,28},{28,24},{1,5},{5... | collective-permute-start | bytes 4718600 | tf_op jit(solution)/shard_map/ppermute | solution.py:591
  178.9 6.8 collective-permute-start.5
  181.8 9.9 %collective-permute-start.8 = (bf16[4,4,13,64,128]{4,3,2,1,0:T(8,128)(2,1)S(1)}, bf16[4,4,13,64,128]{4,3,2,1,0:T(8,128)(2,1)}, u32[]{:S(2)}, u32[]{:S(2)}) collective-permute-start(bf16[4,4,13,64,128]{4,3,2,1,0:T(8,128)(2,1)S(1)} %pad_maximum_fusion.1.own_b), channel_id=1, source_target_pairs={{0,4},{4,0},{8,12},{12,8},{16,20},{20,16},{24,28},{28,24},{1,5},{5... | collective-permute-start | bytes 10223624 | tf_op jit(solution)/shard_map/ppermute | solution.py:591
  291.1 234.4 %reduce-scatter.5.cloned.1.call-start = ((), (), s32[]{:S(2)}) async-start(), calls=%async_computation.6 | async-start | bytes 11943936 | tf_op jit(solution)/shard_map/reduce_scatter | solution.py:807
  296.0 54.5 %collective-permute-start.13 = (bf16[2,128,1536]{2,1,0:T(8,128)(2,1)}, bf16[2,128,1536]{2,1,0:T(8,128)(2,1)}, u32[]{:S(2)}, u32[]{:S(2)}) collective-permute-start(bf16[2,128,1536]{2,1,0:T(8,128)(2,1)} %add_bitcast_fusion.10), channel_id=1, source_target_pairs={{0,8},{4,12},{8,0},{12,4},{16,24},{20,28},{24,16},{28,20},{1,9},{5... | collective-permute-start | bytes 2359304 | tf_op jit(solution)/shard_map/ppermute | solution.py:591
  348.2 36.9 %collective-permute-start.15 = (bf16[3,4,64,3456]{3,2,1,0:T(8,128)(2,1)}, bf16[3,4,64,3456]{3,2,1,0:T(8,128)(2,1)}, u32[]{:S(2)}, u32[]{:S(2)}) collective-permute-start(bf16[3,4,64,3456]{3,2,1,0:T(8,128)(2,1)} %get-tuple-element.96), channel_id=1, source_target_pairs={{0,4},{4,0},{8,12},{12,8},{16,20},{20,16},{24,28},{28,24},{1,5},{5... | collective-permute-start | bytes 15925256 | tf_op jit(solution)/shard_map/ppermute | solution.py:591
  372.6 11.4 %collective-permute-start.17 = (bf16[128,1536]{1,0:T(8,128)(2,1)S(1)}, bf16[128,1536]{1,0:T(8,128)(2,1)S(1)}, u32[]{:S(2)}, u32[]{:S(2)}) collective-permute-start(bf16[128,1536]{1,0:T(8,128)(2,1)S(1)} %add_bitcast_fusion.13), channel_id=1, source_target_pairs={{0,16},{4,20},{8,24},{12,28},{16,0},{20,4},{24,8},{28,12},{1,17},{... | collective-permute-start | bytes 1179656 | tf_op jit(solution)/shard_map/ppermute | solution.py:591
  394.7 22.6 %collective-permute-start.18 = (bf16[1248,128]{1,0:T(8,128)(2,1)S(1)}, bf16[1248,128]{1,0:T(8,128)(2,1)S(1)}, u32[]{:S(2)}, u32[]{:S(2)}) collective-permute-start(bf16[1248,128]{1,0:T(8,128)(2,1)S(1)} %pad_maximum_fusion.13), channel_id=1, source_target_pairs={{0,1},{1,2},{2,3},{3,0},{4,5},{5,6},{6,7},{7,4},{8,9},{9,10},{10,1... | collective-permute-start | bytes 958472 | tf_op jit(solution)/shard_map/ppermute | solution.py:596
  406.9 23.0 %collective-permute-start.19 = (bf16[1248,128]{1,0:T(8,128)(2,1)S(1)}, bf16[1248,128]{1,0:T(8,128)(2,1)S(1)}, u32[]{:S(2)}, u32[]{:S(2)}) collective-permute-start(bf16[1248,128]{1,0:T(8,128)(2,1)S(1)} %pad_maximum_fusion.14), channel_id=1, source_target_pairs={{0,2},{1,3},{2,0},{3,1},{4,6},{5,7},{6,4},{7,5},{8,10},{9,11},{10,... | collective-permute-start | bytes 958472 | tf_op jit(solution)/shard_map/ppermute | solution.py:596
  409.5 20.5 %collective-permute-start.20 = (bf16[1248,128]{1,0:T(8,128)(2,1)S(1)}, bf16[1248,128]{1,0:T(8,128)(2,1)S(1)}, u32[]{:S(2)}, u32[]{:S(2)}) collective-permute-start(bf16[1248,128]{1,0:T(8,128)(2,1)S(1)} %pad_maximum_fusion.15), channel_id=1, source_target_pairs={{0,3},{1,0},{2,1},{3,2},{4,7},{5,4},{6,5},{7,6},{8,11},{9,8},{10,9... | collective-permute-start | bytes 958472 | tf_op jit(solution)/shard_map/ppermute | solution.py:596
  411.0 223.1 %all-reduce.4.cloned.1.call-start = ((), (), s32[]{:S(2)}) async-start(), calls=%async_computation.7 | async-start | bytes 5308416 | tf_op jit(solution)/shard_map/psum | solution.py:858
  413.9 52.6 %collective-permute-start.14 = (bf16[13,4,256,128]{3,2,1,0:T(8,128)(2,1)}, bf16[13,4,256,128]{3,2,1,0:T(8,128)(2,1)}, u32[]{:S(2)}, u32[]{:S(2)}) collective-permute-start(bf16[13,4,256,128]{3,2,1,0:T(8,128)(2,1)} %get-tuple-element.94), channel_id=1, source_target_pairs={{0,4},{4,0},{8,12},{12,8},{16,20},{20,16},{24,28},{28,24},{1,5},{5... | collective-permute-start | bytes 10223624 | tf_op jit(solution)/shard_map/ppermute | solution.py:591
  413.9 47.5 %collective-permute-start.16 = (bf16[3,2,32,3456]{3,2,0,1:T(8,128)(2,1)}, bf16[3,2,32,3456]{3,2,0,1:T(8,128)(2,1)}, u32[]{:S(2)}, u32[]{:S(2)}) collective-permute-start(bf16[3,2,32,3456]{3,2,0,1:T(8,128)(2,1)} %get-tuple-element.158), channel_id=1, source_target_pairs={{0,8},{4,12},{8,0},{12,4},{16,24},{20,28},{24,16},{28,20},{1,9},{5... | collective-permute-start | bytes 3981320 | tf_op jit(solution)/shard_map/ppermute | solution.py:591
  417.3 46.7 %collective-permute-start.21 = (bf16[3,2,32,3456]{3,2,0,1:T(8,128)(2,1)}, bf16[3,2,32,3456]{3,2,0,1:T(8,128)(2,1)}, u32[]{:S(2)}, u32[]{:S(2)}) collective-permute-start(bf16[3,2,32,3456]{3,2,0,1:T(8,128)(2,1)} %get-tuple-element.156), channel_id=1, source_target_pairs={{0,16},{4,20},{8,24},{12,28},{16,0},{20,4},{24,8},{28,12},{1,17},{... | collective-permute-start | bytes 3981320 | tf_op jit(solution)/shard_map/ppermute | solution.py:591
  430.8 43.8 %collective-permute-start.43 = (bf16[1248,128]{1,0:T(8,128)(2,1)}, bf16[1248,128]{1,0:T(8,128)(2,1)}, u32[]{:S(2)}, u32[]{:S(2)}) collective-permute-start(bf16[1248,128]{1,0:T(8,128)(2,1)} %add_convert_fusion.1), channel_id=1, source_target_pairs={{0,1},{1,2},{2,3},{3,0},{4,5},{5,6},{6,7},{7,4},{8,9},{9,10},{10,1... | collective-permute-start | bytes 958472 | tf_op jit(solution)/shard_map/ppermute | solution.py:596
  438.2 39.6 %collective-permute-start.44 = (bf16[1248,128]{1,0:T(8,128)(2,1)}, bf16[1248,128]{1,0:T(8,128)(2,1)}, u32[]{:S(2)}, u32[]{:S(2)}) collective-permute-start(bf16[1248,128]{1,0:T(8,128)(2,1)} %add_convert_fusion.1), channel_id=1, source_target_pairs={{0,2},{1,3},{2,0},{3,1},{4,6},{5,7},{6,4},{7,5},{8,10},{9,11},{10,... | collective-permute-start | bytes 958472 | tf_op jit(solution)/shard_map/ppermute | solution.py:596
  461.5 18.6 %collective-permute-start.45 = (bf16[1248,128]{1,0:T(8,128)(2,1)}, bf16[1248,128]{1,0:T(8,128)(2,1)S(1)}, u32[]{:S(2)}, u32[]{:S(2)}) collective-permute-start(bf16[1248,128]{1,0:T(8,128)(2,1)} %add_convert_fusion.1), channel_id=1, source_target_pairs={{0,3},{1,0},{2,1},{3,2},{4,7},{5,4},{6,5},{7,6},{8,11},{9,8},{10,9... | collective-permute-start | bytes 958472 | tf_op jit(solution)/shard_map/ppermute | solution.py:596
  464.0 25.2 %collective-permute-start.23 = (bf16[3,32,3456]{2,1,0:T(8,128)(2,1)S(1)}, bf16[3,32,3456]{2,1,0:T(8,128)(2,1)S(1)}, u32[]{:S(2)}, u32[]{:S(2)}) collective-permute-start(bf16[3,32,3456]{2,1,0:T(8,128)(2,1)S(1)} %add_bitcast_fusion.12), channel_id=1, source_target_pairs={{0,16},{4,20},{8,24},{12,28},{16,0},{20,4},{24,8},{28,12},{1,17},{... | collective-permute-start | bytes 1990664 | tf_op jit(solution)/shard_map/ppermute | solution.py:591
  466.6 27.1 %collective-permute-start.26 = (bf16[13,4,256,128]{3,2,1,0:T(8,128)(2,1)}, bf16[13,4,256,128]{3,2,1,0:T(8,128)(2,1)S(1)}, u32[]{:S(2)}, u32[]{:S(2)}) collective-permute-start(bf16[13,4,256,128]{3,2,1,0:T(8,128)(2,1)} %get-tuple-element.118), channel_id=1, source_target_pairs={{0,4},{4,0},{8,12},{12,8},{16,20},{20,16},{24,28},{28,24},{1,5},{5... | collective-permute-start | bytes 10223624 | tf_op jit(solution)/shard_map/ppermute | solution.py:591
  474.6 17.7 %collective-permute-start.24 = (bf16[3,32,3456]{2,1,0:T(8,128)(2,1)S(1)}, bf16[3,32,3456]{2,1,0:T(8,128)(2,1)S(1)}, u32[]{:S(2)}, u32[]{:S(2)}) collective-permute-start(bf16[3,32,3456]{2,1,0:T(8,128)(2,1)S(1)} %add_bitcast_fusion.11), channel_id=1, source_target_pairs={{0,8},{4,12},{8,0},{12,4},{16,24},{20,28},{24,16},{28,20},{1,9},{5... | collective-permute-start | bytes 1990664 | tf_op jit(solution)/shard_map/ppermute | solution.py:591
  477.8 65.0 %collective-permute-start.22 = (bf16[13,4,2,64,128]{4,3,0,1,2:T(8,128)(2,1)}, bf16[13,4,2,64,128]{4,3,0,1,2:T(8,128)(2,1)}, u32[]{:S(2)}, u32[]{:S(2)}) collective-permute-start(bf16[13,4,2,64,128]{4,3,0,1,2:T(8,128)(2,1)} %get-tuple-element.151), channel_id=1, source_target_pairs={{0,8},{4,12},{8,0},{12,4},{16,24},{20,28},{24,16},{28,20},{1,9},{5... | collective-permute-start | bytes 5111816 | tf_op jit(solution)/shard_map/ppermute | solution.py:591
  497.1 51.3 %collective-permute-start.27 = (bf16[13,4,2,64,128]{4,3,0,1,2:T(8,128)(2,1)}, bf16[13,4,2,64,128]{4,3,0,1,2:T(8,128)(2,1)}, u32[]{:S(2)}, u32[]{:S(2)}) collective-permute-start(bf16[13,4,2,64,128]{4,3,0,1,2:T(8,128)(2,1)} %get-tuple-element.153), channel_id=1, source_target_pairs={{0,16},{4,20},{8,24},{12,28},{16,0},{20,4},{24,8},{28,12},{1,17},{... | collective-permute-start | bytes 5111816 | tf_op jit(solution)/shard_map/ppermute | solution.py:591
  544.9 20.9 %collective-permute-start.25 = (bf16[13,4,64,128]{3,2,0,1:T(8,128)(2,1)}, bf16[13,4,64,128]{3,2,0,1:T(8,128)(2,1)}, u32[]{:S(2)}, u32[]{:S(2)}) collective-permute-start(bf16[13,4,64,128]{3,2,0,1:T(8,128)(2,1)} %add_bitcast_fusion.9), channel_id=1, source_target_pairs={{0,16},{4,20},{8,24},{12,28},{16,0},{20,4},{24,8},{28,12},{1,17},{... | collective-permute-start | bytes 2555912 | tf_op jit(solution)/shard_map/ppermute | solution.py:591
  550.1 20.3 %collective-permute-start.28 = (bf16[13,4,64,128]{3,2,0,1:T(8,128)(2,1)S(1)}, bf16[13,4,64,128]{3,2,0,1:T(8,128)(2,1)S(1)}, u32[]{:S(2)}, u32[]{:S(2)}) collective-permute-start(bf16[13,4,64,128]{3,2,0,1:T(8,128)(2,1)S(1)} %add_bitcast_fusion.8), channel_id=1, source_target_pairs={{0,8},{4,12},{8,0},{12,4},{16,24},{20,28},{24,16},{28,20},{1,9},{5... | collective-permute-start | bytes 2555912 | tf_op jit(solution)/shard_map/ppermute | solution.py:591
  635.5 16.6 %collective-permute-start.34 = (bf16[1664,128]{1,0:T(8,128)(2,1)S(1)}, bf16[1664,128]{1,0:T(8,128)(2,1)S(1)}, u32[]{:S(2)}, u32[]{:S(2)}) collective-permute-start(bf16[1664,128]{1,0:T(8,128)(2,1)S(1)} %get-tuple-element.165), channel_id=1, source_target_pairs={{0,1},{1,2},{2,3},{3,0},{4,5},{5,6},{6,7},{7,4},{8,9},{9,10},{10,1... | collective-permute-start | bytes 1277960 | tf_op jit(solution)/shard_map/ppermute | solution.py:596
  635.6 31.7 %collective-permute-start.35 = (bf16[1664,128]{1,0:T(8,128)(2,1)S(1)}, bf16[1664,128]{1,0:T(8,128)(2,1)S(1)}, u32[]{:S(2)}, u32[]{:S(2)}) collective-permute-start(bf16[1664,128]{1,0:T(8,128)(2,1)S(1)} %get-tuple-element.167), channel_id=1, source_target_pairs={{0,2},{1,3},{2,0},{3,1},{4,6},{5,7},{6,4},{7,5},{8,10},{9,11},{10,... | collective-permute-start | bytes 1277960 | tf_op jit(solution)/shard_map/ppermute | solution.py:596
  637.3 30.1 %collective-permute-start.36 = (bf16[1664,128]{1,0:T(8,128)(2,1)S(1)}, bf16[1664,128]{1,0:T(8,128)(2,1)S(1)}, u32[]{:S(2)}, u32[]{:S(2)}) collective-permute-start(bf16[1664,128]{1,0:T(8,128)(2,1)S(1)} %get-tuple-element.166), channel_id=1, source_target_pairs={{0,3},{1,0},{2,1},{3,2},{4,7},{5,4},{6,5},{7,6},{8,11},{9,8},{10,9... | collective-permute-start | bytes 1277960 | tf_op jit(solution)/shard_map/ppermute | solution.py:596
  668.7 22.0 %collective-permute-start.37 = (bf16[1,13,64,128]{3,2,1,0:T(8,128)(2,1)S(1)}, bf16[1,13,64,128]{3,2,1,0:T(8,128)(2,1)S(1)}, u32[]{:S(2)}, u32[]{:S(2)}) collective-permute-start(bf16[1,13,64,128]{3,2,1,0:T(8,128)(2,1)S(1)} %bitcast.239), channel_id=1, source_target_pairs={{0,8},{4,12},{8,0},{12,4},{16,24},{20,28},{24,16},{28,20},{1,9},{5... | collective-permute-start | bytes 638984 | tf_op jit(solution)/shard_map/ppermute | solution.py:591
  670.2 22.1 %collective-permute-start.40 = (bf16[1,13,64,128]{3,2,1,0:T(8,128)(2,1)S(1)}, bf16[1,13,64,128]{3,2,1,0:T(8,128)(2,1)S(1)}, u32[]{:S(2)}, u32[]{:S(2)}) collective-permute-start(bf16[1,13,64,128]{3,2,1,0:T(8,128)(2,1)S(1)} %bitcast.235), channel_id=1, source_target_pairs={{0,16},{4,20},{8,24},{12,28},{16,0},{20,4},{24,8},{28,12},{1,17},{... | collective-permute-start | bytes 638984 | tf_op jit(solution)/shard_map/ppermute | solution.py:591
  671.7 5.9 collective-permute-start.30
  677.7 4.2 collective-permute-start.31
  681.9 12.0 %collective-permute-start.32 = (f32[13442]{0:T(1024)S(1)}, f32[13442]{0:T(1024)S(1)}, u32[]{:S(2)}, u32[]{:S(2)}) collective-permute-start(f32[13442]{0:T(1024)S(1)} %add.629), channel_id=1, source_target_pairs={{0,1},{1,0},{2,3},{3,2},{4,5},{5,4},{6,7},{7,6},{8,9},{9,8},{10,11... | collective-permute-start | bytes 161312 | tf_op jit(solution)/shard_map/ppermute | solution.py:698
  690.8 10.2 %collective-permute-start.38 = (bf16[2,13,64,128]{3,2,1,0:T(8,128)(2,1)S(1)}, bf16[2,13,64,128]{3,2,1,0:T(8,128)(2,1)S(1)}, u32[]{:S(2)}, u32[]{:S(2)}) collective-permute-start(bf16[2,13,64,128]{3,2,1,0:T(8,128)(2,1)S(1)} %pad_maximum_fusion.10), channel_id=1, source_target_pairs={{0,16},{4,20},{8,24},{12,28},{16,0},{20,4},{24,8},{28,12},{1,17},{... | collective-permute-start | bytes 1277960 | tf_op jit(solution)/shard_map/ppermute | solution.py:591
  692.4 9.8 %collective-permute-start.41 = (bf16[2,13,64,128]{3,2,1,0:T(8,128)(2,1)S(1)}, bf16[2,13,64,128]{3,2,1,0:T(8,128)(2,1)S(1)}, u32[]{:S(2)}, u32[]{:S(2)}) collective-permute-start(bf16[2,13,64,128]{3,2,1,0:T(8,128)(2,1)S(1)} %pad_maximum_fusion.11), channel_id=1, source_target_pairs={{0,8},{4,12},{8,0},{12,4},{16,24},{20,28},{24,16},{28,20},{1,9},{5... | collective-permute-start | bytes 1277960 | tf_op jit(solution)/shard_map/ppermute | solution.py:591
  694.0 5.8 collective-permute-start.33
  (64 other events, 926.3 us)
Sparse Core Ops, SparseCore 0:
  10.5 89.1 all-gather.3
  102.2 90.0 all-gather.5
  194.8 54.9 all-gather.7
  291.3 74.8 reduce-scatter.2
  411.1 114.3 reduce-scatter.4
  528.5 105.5 all-reduce.3

commit v4 on v3

--- a/solution.py
+++ b/solution.py
@@ -18,6 +18,7 @@
 SLOTS = 32
 LOW = 128
 VMEM_BYTES = 60 * 2**20
+HINT = 10**10
 
 
 BETA_ONE = 0.9
@@ -542,7 +543,7 @@
     keep_ref[0] = both_ref[:, core]
 
 
-def row_gradient(hits, grad_summed, start, stop, group, core, pieces):
+def row_gradient(hits, grad_summed, start, stop, group, core, pieces, hint):
     unused, samples, rows = hits.shape
     half = rows // group // 2
     shape = jax.ShapeDtypeStruct((stop - start, group, half, LOW), jnp.bfloat16)
@@ -567,7 +568,7 @@
             input_output_aliases={3: 0, 4: 1} if results else {},
             compiler_params=pltpu.CompilerParams(vmem_limit_bytes=VMEM_BYTES),
             cost_estimate=pl.CostEstimate(
-                flops=10**12,
+                flops=hint,
                 bytes_accessed=2 * (last - first) * rows * (samples + LOW),
                 transcendentals=0,
             ),
@@ -836,7 +837,7 @@
     row_sums = []
     grad_rows = after(grad_summed, late_sum.received)
     for first, last, order in spans:
-        send, keep = row_gradient(hits, grad_rows, first, last, group, core, 2)
+        send, keep = row_gradient(hits, grad_rows, first, last, group, core, 2, 10**12 if first == 0 else HINT)
         shape = (last - first, group) + (2,) * len(bits) + (part, width)
         row_sums.append(HalvingSum(keep.reshape(shape), flip(send, 1).reshape(shape), bits, order, 2))
         if len(row_sums) == 1:
@@ -844,14 +845,15 @@
                 late_sum.step(keep)
             for item in up_sums:
                 item.step(late_sum.sent)
-            one_total = GroupSum(share_one, late_sum.result())
-            one_total.scatter(*[item.sent for item in up_sums])
-            one_total.gather()
-            grad_rows = after(grad_rows, one_total.sent)
+            grad_rows = after(grad_rows, [item.sent for item in up_sums] + [late_sum.sent, share_one])
     row_p, row_q = row_sums
+    one_total = GroupSum(share_one, late_sum.result())
+    one_total.scatter(keep)
+    first_sent = list(one_total.sent)
     for step in bits[1:]:
         for item in up_sums:
-            item.step(one_total.sent)
+            item.step(*first_sent)
+    one_total.gather(*[item.sent for item in up_sums])
     for item in row_sums:
         item.step(up_p.sent, up_q.sent)
     share_up = jnp.concatenate([item.result() for item in up_sums], axis=1)

time: 734 us -> 720 us (0.981)
  waiting for transfers between devices: 249 us -> 231 us
    reduce_scatter x1, waiting for transfers between devices: 26.7 us -> 0.01 us  [on_device(): lax.psum_scatter(grad_down, 'rep', scatter_dimension=1, tiled=True)]
    ppermute x12, waiting for transfers between devices: 55 us -> 71.2 us  [shift(): lax.ppermute(value, 'grp', [(i, (i + step) % size) for i in range(size)])]
    psum x1, waiting for transfers between devices: 60.9 us -> 45.2 us  [on_device(): share_up, share_down = lax.psum((share_up, share_down), 'grp')]
    ppermute x29, waiting for transfers between devices: 94.5 us -> 103 us  [flip(): lax.ppermute(value, 'rep', [(i, i ^ bit) for i in range(lax.axis_size('re...]
  transfers between devices with their start and end apart: 52 -> 52, of which waited for: 25 -> 25; matrix products, arithmetic and copies ran while one was open for 15% -> 16% of each run, Pallas kernels for 30% -> 30%
where the time goes in v4:
time: 720 us; the launch traced here: 711 us
  Pallas kernels  243 us (34%)
  waiting for transfers between devices  231 us (32%)
  other arithmetic  88.5 us (12%)
  starting transfers between devices  79.2 us (11%)
  local copies, waits for them, and re-layouts  53.7 us (7%)
  between operations  15.7 us (2%)
    ppermute x29, waiting for transfers between devices, flip(): lax.ppermute(value, 'rep', [(i, i ^ bit) for i in range(lax.axis_size('re...  103 us
    ppermute x12, waiting for transfers between devices, shift(): lax.ppermute(value, 'grp', [(i, (i + step) % size) for i in range(size)])  71.2 us
    pallas_call x4, Pallas kernels, count(): pl.pallas_call(functools.partial(count_kernel, len(earlier)), grid=(last...  54.1 us
    pallas_call x1, Pallas kernels, cross_backward(): pl.pallas_call(cross_backward_kernel, grid_spec=pltpu.PrefetchScalarGridS...  50.9 us
    psum x1, waiting for transfers between devices, on_device(): share_up, share_down = lax.psum((share_up, share_down), 'grp')  45.2 us
    pallas_call x4, Pallas kernels, row_gradient(): pl.pallas_call(functools.partial(row_kernel, len(results)), grid_spec=plt...  42.5 us
    pallas_call x1, Pallas kernels, pool(): pl.pallas_call(functools.partial(pool_kernel, keys=keys, half=half), grid...  38.9 us
    ppermute x12, starting transfers between devices, shift(): lax.ppermute(value, 'grp', [(i, (i + step) % size) for i in range(size)])  37.4 us
  transfers between devices with their start and end apart: 52, of which 25 were waited for; matrix products, arithmetic and copies ran while one was open for 16% of the time, Pallas kernels for 30%

profile of v4, /device:TPU:0, one launch (start us, length us, event | category | flops | bytes accessed | tf_op | source)
XLA Modules:
  0.0 711.1 jit_solution(9932443106605904466)
XLA Ops:
  7.2 3.1 convert_element_type.79
  15.6 3.1 collective-permute-start
  18.7 2.6 collective-permute-start.1
  22.6 8.8 %collective-permute-done = bf16[26,64,128]{2,1,0:T(8,128)(2,1)S(1)} collective-permute-done((bf16[26,64,128]{2,1,0:T(8,128)(2,1)S(1)}, bf16[26,64,128]{2,1,0:T(8,128)(2,1)S(1)}, u32[]{:S(2)}, u32[]{:S(2)}) %collective-permute-start) | collective-permute-done | bytes 426016 | tf_op jit(solution)/shard_map/ppermute | solution.py:597
  31.5 17.4 %collective-permute-done.1 = bf16[26,64,128]{2,1,0:T(8,128)(2,1)S(1)} collective-permute-done((bf16[26,64,128]{2,1,0:T(8,128)(2,1)S(1)}, bf16[26,64,128]{2,1,0:T(8,128)(2,1)S(1)}, u32[]{:S(2)}, u32[]{:S(2)}) %collective-permute-start.1) | collective-permute-done | bytes 426016 | tf_op jit(solution)/shard_map/ppermute | solution.py:597
  53.1 36.1 %collective-permute-done.3 = bf16[1,4,13,64,128]{4,3,2,1,0:T(8,128)(2,1)S(1)} collective-permute-done((bf16[1,4,13,64,128]{4,3,2,1,0:T(8,128)(2,1)S(1)}, bf16[1,4,13,64,128]{4,3,2,1,0:T(8,128)(2,1)S(1)}, u32[]{:S(2)}, u32[]{:S(2)}) %collective-permute-start.3) | collective-permute-done | bytes 852000 | tf_op jit(solution)/shard_map/ppermute | solution.py:592
  95.4 6.6 collective-permute-done.9
  104.6 4.2 copy.70
  108.9 5.8 reshape.182.ids_ref
  114.6 12.6 %shard_map.408.refs_0_ = bf16[26,512,2048]{2,1,0:T(8,128)(2,1)} custom-call(s32[26,64,256]{2,1,0:T(8,128)} %reshape.182.ids_ref), custom_call_target="tpu_custom_call" | custom-call | flops 1 | bytes 1 | tf_op jit(solution)/shard_map/pallas_call | solution.py:113
  127.2 14.4 %shard_map.409.refs_0_ = bf16[26,512,2048]{2,1,0:T(8,128)(2,1)} custom-call(s32[26,64,256]{2,1,0:T(8,128)} %reshape.182.ids_ref, bf16[26,512,2048]{2,1,0:T(8,128)(2,1)} %shard_map.408.refs_0_), custom_call_target="tpu_custom_call", output_to_operand_aliasing={{}: (1, {})} | custom-call | flops 1 | bytes 1 | tf_op jit(solution)/shard_map/pallas_call | solution.py:113
  141.6 12.7 %shard_map.410.refs_0_ = bf16[26,512,2048]{2,1,0:T(8,128)(2,1)} custom-call(s32[26,64,256]{2,1,0:T(8,128)} %reshape.182.ids_ref, bf16[26,512,2048]{2,1,0:T(8,128)(2,1)} %shard_map.409.refs_0_), custom_call_target="tpu_custom_call", output_to_operand_aliasing={{}: (1, {})} | custom-call | flops 1 | bytes 1 | tf_op jit(solution)/shard_map/pallas_call | solution.py:113
  154.3 14.4 %shard_map.411.hits_ref = bf16[26,512,2048]{2,1,0:T(8,128)(2,1)} custom-call(s32[26,64,256]{2,1,0:T(8,128)} %reshape.182.ids_ref, bf16[26,512,2048]{2,1,0:T(8,128)(2,1)} %shard_map.410.refs_0_), custom_call_target="tpu_custom_call", output_to_operand_aliasing={{}: (1, {})} | custom-call | flops 1 | bytes 1 | tf_op jit(solution)/shard_map/pallas_call | solution.py:113
  188.9 2.8 collective-permute-done.8.other_b
  191.6 38.9 %shard_map.412.anchor_in = f32[512,3456]{1,0:T(8,128)} custom-call(s32[2]{0:T(128)} %pad_add_fusion.place_ref, bf16[26,512,2048]{2,1,0:T(8,128)(2,1)} %shard_map.411.hits_ref, bf16[4,4,13,64,128]{4,3,2,1,0:T(8,128)(2,1)} %copy-done, bf16[4,4,13,64,128]{4,3,2,1,0:T(8,128)(2,1)} %copy-done.28, bf16[4,4,13,64,128]{4,3,2,1,0:T(8,128)(2,1)} %copy-done.1, ...), custom_call_target="tpu_custom_call" | custom-call | flops 1 | bytes 1 | tf_op jit(solution)/shard_map/pallas_call | solution.py:180
  230.6 28.7 %shard_map.413 = (bf16[3,512,3456]{2,1,0:T(8,128)(2,1)}, bf16[3,512,512]{2,1,0:T(8,128)(2,1)}, bf16[512,3456]{1,0:T(8,128)(2,1)}) custom-call(f32[512,3456]{1,0:T(8,128)} %shard_map.412.anchor_in, bf16[3,3456,512]{2,1,0:T(8,128)(2,1)} %all-gather.4.cloned.1.call-done.down_ref, bf16[3,512,3456]{2,1,0:T(8,128)(2,1)} %all-gather.6.cloned.1.call-done.up_ref, ...), custom_call_target="tpu_custom_call" | custom-call | flops 1 | bytes 1 | tf_op jit(solution)/shard_map/pallas_call | solution.py:249
  259.2 28.4 %shard_map.414 = (f32[1,1]{1,0:T(1,128)}, f32[1,512]{1,0:T(1,128)}, f32[1,1]{1,0:T(1,128)}, f32[1,1024]{1,0:T(1,128)}, f32[1,1024]{1,0:T(1,128)}, /*index=5*/f32...) custom-call(bf16[512,3456]{1,0:T(8,128)(2,1)} %get-tuple-element.75.input_ref, ...), custom_call_target="tpu_custom_call" | custom-call | flops 1 | bytes 1 | tf_op jit(solution)/shard_map/pallas_call | solution.py:361
  291.1 3.5 collective-permute-done.12
  297.2 50.9 %shard_map.415 = (bf16[3,4,64,3456]{3,2,1,0:T(8,128)(2,1)}, bf16[3,4,64,3456]{3,2,1,0:T(8,128)(2,1)}, bf16[3,3456,512]{2,1,0:T(8,128)(2,1)}, f32[3,1,3456]{2,1,0:T(1,128)}, bf16[512,3456]{1,0:T(8,128)(2,1)}) custom-call(s32[1]{0:T(128)} %bitcast.core_ref, f32[512,3456]{1,0:T(8,128)} %shard_map.412.anchor_in, f32[512,3456]{1,0:T(8,128)} %get-tuple-element.80.grad_in, ...), custom_call_target="tpu_custom_call" | custom-call | flops 999999995904 | bytes 70778880 | tf_op jit(solution)/shard_map/pallas_call | solution.py:488
  351.0 9.8 %shard_map.416 = (bf16[13,4,256,128]{3,2,1,0:T(8,128)(2,1)}, bf16[13,4,256,128]{3,2,1,0:T(8,128)(2,1)}) custom-call(s32[1]{0:T(128)} %bitcast.core_ref, bf16[26,512,2048]{2,1,0:T(8,128)(2,1)} %shard_map.411.hits_ref, bf16[512,3456]{1,0:T(8,128)(2,1)} %get-tuple-element.105.grad_ref), custom_call_target="tpu_custom_call" | custom-call | flops 999999995904 | bytes 15728640 | tf_op jit(solution)/shard_map/pallas_call | solution.py:554
  360.8 11.4 %shard_map.417 = (bf16[13,4,256,128]{3,2,1,0:T(8,128)(2,1)}, bf16[13,4,256,128]{3,2,1,0:T(8,128)(2,1)}) custom-call(s32[1]{0:T(128)} %bitcast.core_ref, bf16[26,512,2048]{2,1,0:T(8,128)(2,1)} %shard_map.411.hits_ref, bf16[512,3456]{1,0:T(8,128)(2,1)} %get-tuple-element.105.grad_ref, ...), custom_call_target="tpu_custom_call", output_to_operand_aliasing={{0}: (3, {}), {1}: (4, {})} | custom-call | flops 999999995904 | bytes 18350080 | tf_op jit(solution)/shard_map/pallas_call | solution.py:554
  375.7 5.1 fusion.41
  381.0 2.7 concatenate.87
  388.0 3.2 fusion.40
  397.8 9.8 %shard_map.418 = (bf16[13,4,256,128]{3,2,1,0:T(8,128)(2,1)}, bf16[13,4,256,128]{3,2,1,0:T(8,128)(2,1)}) custom-call(s32[1]{0:T(128)} %bitcast.core_ref, bf16[26,512,2048]{2,1,0:T(8,128)(2,1)} %shard_map.411.hits_ref, bf16[512,3456]{1,0:T(8,128)(2,1)} %get-tuple-element.105.grad_ref), custom_call_target="tpu_custom_call" | custom-call | flops 10000000000 | bytes 15728640 | tf_op jit(solution)/shard_map/pallas_call | solution.py:554
  407.6 11.5 %shard_map.419 = (bf16[13,4,256,128]{3,2,1,0:T(8,128)(2,1)}, bf16[13,4,256,128]{3,2,1,0:T(8,128)(2,1)}) custom-call(s32[1]{0:T(128)} %bitcast.core_ref, bf16[26,512,2048]{2,1,0:T(8,128)(2,1)} %shard_map.411.hits_ref, bf16[512,3456]{1,0:T(8,128)(2,1)} %get-tuple-element.105.grad_ref, ...), custom_call_target="tpu_custom_call", output_to_operand_aliasing={{0}: (3, {}), {1}: (4, {})} | custom-call | flops 10000000000 | bytes 18350080 | tf_op jit(solution)/shard_map/pallas_call | solution.py:554
  424.2 15.8 %collective-permute-start.42 = (bf16[1248,128]{1,0:T(8,128)(2,1)S(1)}, bf16[1248,128]{1,0:T(8,128)(2,1)S(1)}, u32[]{:S(2)}, u32[]{:S(2)}) collective-permute-start(bf16[1248,128]{1,0:T(8,128)(2,1)S(1)} %pad_maximum_fusion.16), channel_id=1, source_target_pairs={{0,3},{1,0},{2,1},{3,2},{4,7},{5,4},{6,5},{7,6},{8,11},{9,8},{10,9... | collective-permute-start | bytes 958472 | tf_op jit(solution)/shard_map/ppermute | solution.py:597
  440.1 12.5 %collective-permute-done.18 = bf16[3,2,32,3456]{3,2,0,1:T(8,128)(2,1)} collective-permute-done((bf16[3,2,32,3456]{3,2,0,1:T(8,128)(2,1)}, bf16[3,2,32,3456]{3,2,0,1:T(8,128)(2,1)}, u32[]{:S(2)}, u32[]{:S(2)}) %collective-permute-start.18) | collective-permute-done | bytes 1327136 | tf_op jit(solution)/shard_map/ppermute | solution.py:592
  452.6 5.5 collective-permute-start.40
  462.7 4.9 add_bitcast_fusion.2
  472.0 8.2 %collective-permute-done.43 = bf16[1248,128]{1,0:T(8,128)(2,1)S(1)} collective-permute-done((bf16[1248,128]{1,0:T(8,128)(2,1)S(1)}, bf16[1248,128]{1,0:T(8,128)(2,1)S(1)}, u32[]{:S(2)}, u32[]{:S(2)}) %collective-permute-start.43) | collective-permute-done | bytes 319520 | tf_op jit(solution)/shard_map/ppermute | solution.py:597
  481.6 14.8 %collective-permute-done.44 = bf16[1248,128]{1,0:T(8,128)(2,1)S(1)} collective-permute-done((bf16[1248,128]{1,0:T(8,128)(2,1)S(1)}, bf16[1248,128]{1,0:T(8,128)(2,1)S(1)}, u32[]{:S(2)}, u32[]{:S(2)}) %collective-permute-start.44) | collective-permute-done | bytes 319520 | tf_op jit(solution)/shard_map/ppermute | solution.py:597
  499.1 6.9 collective-permute-done.45
  509.5 3.4 add_bitcast_fusion
  518.8 2.6 slice_convert_fusion
  522.8 4.0 collective-permute-done.19
  533.2 20.0 %collective-permute-done.24 = bf16[13,4,2,64,128]{4,3,0,1,2:T(8,128)(2,1)} collective-permute-done((bf16[13,4,2,64,128]{4,3,0,1,2:T(8,128)(2,1)}, bf16[13,4,2,64,128]{4,3,0,1,2:T(8,128)(2,1)}, u32[]{:S(2)}, u32[]{:S(2)}) %collective-permute-start.24) | collective-permute-done | bytes 1703968 | tf_op jit(solution)/shard_map/ppermute | solution.py:592
  556.3 4.9 multiply_subtract_fusion.2
  561.2 8.6 %collective-permute-done.22 = bf16[13,4,64,128]{3,2,0,1:T(8,128)(2,1)} collective-permute-done((bf16[13,4,64,128]{3,2,0,1:T(8,128)(2,1)}, bf16[13,4,64,128]{3,2,0,1:T(8,128)(2,1)}, u32[]{:S(2)}, u32[]{:S(2)}) %collective-permute-start.22) | collective-permute-done | bytes 852000 | tf_op jit(solution)/shard_map/ppermute | solution.py:592
  575.0 45.2 %all-reduce.4.cloned.1.call-done = (bf16[3,64,3456]{2,1,0:T(8,128)(2,1)}, bf16[3,432,512]{2,1,0:T(8,128)(2,1)}) async-done(((bf16[3,64,3456]{2,1,0:T(8,128)(2,1)}, bf16[3,432,512]{2,1,0:T(8,128)(2,1)}), (bf16[3,64,3456]{2,1,0:T(8,128)(2,1)}, bf16[3,432,512]{2,1,0:T(8,128)(2,1)})) %all-reduce.4.cloned.1.call-update) | async-done | bytes 2654224 | tf_op jit(solution)/shard_map/psum | solution.py:860
  623.4 3.0 collective-permute-start.33
  626.4 7.1 %multiply_subtract_fusion = (f32[3,64,3456]{2,1,0:T(8,128)}, f32[3,64,3456]{2,1,0:T(8,128)}, f32[3,64,3456]{2,1,0:T(8,128)}) fusion(f32[3,64,3456]{2,1,0:T(8,128)S(1)} %copy-done.5, bf16[3,64,3456]{2,1,0:T(8,128)(2,1)S(1)} %copy-done.41, f32[3,64,3456]{2,1,0:T(8,128)} %param.36, f32[3,64,3456]{2,1,0:T(8,128)} %param.37), kind=kLoop, calls=%fused_computation.21 | loop fusion | flops 10616832 | bytes 17252352 | tf_op jit(solution)/shard_map/sub | solution.py:713
  633.6 4.7 multiply_subtract_fusion.1
  638.3 15.2 %collective-permute-done.32 = bf16[1664,128]{1,0:T(8,128)(2,1)S(1)} collective-permute-done((bf16[1664,128]{1,0:T(8,128)(2,1)S(1)}, bf16[1664,128]{1,0:T(8,128)(2,1)S(1)}, u32[]{:S(2)}, u32[]{:S(2)}) %collective-permute-start.32) | collective-permute-done | bytes 426016 | tf_op jit(solution)/shard_map/ppermute | solution.py:597
  658.9 4.9 collective-permute-done.27
  668.0 8.8 %collective-permute-start.29 = (f32[13442]{0:T(1024)S(1)}, f32[13442]{0:T(1024)S(1)}, u32[]{:S(2)}, u32[]{:S(2)}) collective-permute-start(f32[13442]{0:T(1024)S(1)} %add.626), channel_id=1, source_target_pairs={{0,1},{1,0},{2,3},{3,2},{4,5},{5,4},{6,7},{7,6},{8,9},{9,8},{10,11... | collective-permute-start | bytes 161312 | tf_op jit(solution)/shard_map/ppermute | solution.py:699
  681.5 4.3 collective-permute-done.30
  691.1 12.7 %add_subtract_fusion = (f32[26,512,128]{2,1,0:T(8,128)}, f32[26,512,128]{2,1,0:T(8,128)}, f32[26,512,128]{2,1,0:T(8,128)}) fusion(f32[26,512,128]{2,1,0:T(8,128)S(1)} %bitcast.229, bf16[13,512,128]{2,1,0:T(8,128)(2,1)S(1)} %fusion.17, bf16[13,512,128]{2,1,0:T(8,128)(2,1)S(1)} %fusion.23, f32[26,512,128]{2,1,0:T(8,128)} %param.30, f32[26,512,128]{2,1,0:T(8,128)} %param.31), kind=kLoop, calls=%fused_computation.4 | loop fusion | flops 27262976 | bytes 44302336 | tf_op jit(solution)/shard_map/sub | solution.py:713
  (322 shorter events, 129.1 us)
Async XLA Ops:
  7.2 223.3 %all-gather.4.cloned.1.call-start = ((), (), s32[]{:S(2)}) async-start(), calls=%async_computation.2 | async-start | bytes 11943936 | tf_op jit(solution)/shard_map/all_gather | solution.py:745
  10.4 220.1 %all-gather.6.cloned.1.call-start = ((), (), s32[]{:S(2)}) async-start(), calls=%async_computation.3 | async-start | bytes 11943936 | tf_op jit(solution)/shard_map/all_gather | solution.py:746
  11.7 247.5 %all-gather.8.cloned.1.call-start = ((), (), s32[]{:S(2)}) async-start(), calls=%async_computation.4 | async-start | bytes 7962624 | tf_op jit(solution)/shard_map/all_gather | solution.py:747
  14.3 383.5 %reduce-scatter.3.cloned.1.call-start = ((), (), s32[]{:S(2)}) async-start(), calls=%async_computation.5 | async-start | bytes 7962624 | tf_op jit(solution)/shard_map/reduce_scatter | solution.py:787
  15.6 15.9 %collective-permute-start = (bf16[26,64,128]{2,1,0:T(8,128)(2,1)S(1)}, bf16[26,64,128]{2,1,0:T(8,128)(2,1)S(1)}, u32[]{:S(2)}, u32[]{:S(2)}) collective-permute-start(bf16[26,64,128]{2,1,0:T(8,128)(2,1)S(1)} %dynamic-slice_convert_fusion), channel_id=1, source_target_pairs={{0,1},{1,2},{2,3},{3,0},{4,5},{5,6},{6,7},{7,4},{8,9},{9,10},{10,1... | collective-permute-start | bytes 1277960 | tf_op jit(solution)/shard_map/ppermute | solution.py:597
  18.7 30.2 %collective-permute-start.1 = (bf16[26,64,128]{2,1,0:T(8,128)(2,1)S(1)}, bf16[26,64,128]{2,1,0:T(8,128)(2,1)S(1)}, u32[]{:S(2)}, u32[]{:S(2)}) collective-permute-start(bf16[26,64,128]{2,1,0:T(8,128)(2,1)S(1)} %dynamic-slice_convert_fusion), channel_id=1, source_target_pairs={{0,2},{1,3},{2,0},{3,1},{4,6},{5,7},{6,4},{7,5},{8,10},{9,11},{10,... | collective-permute-start | bytes 1277960 | tf_op jit(solution)/shard_map/ppermute | solution.py:597
  21.3 27.7 %collective-permute-start.2 = (bf16[26,64,128]{2,1,0:T(8,128)(2,1)S(1)}, bf16[26,64,128]{2,1,0:T(8,128)(2,1)S(1)}, u32[]{:S(2)}, u32[]{:S(2)}) collective-permute-start(bf16[26,64,128]{2,1,0:T(8,128)(2,1)S(1)} %dynamic-slice_convert_fusion), channel_id=1, source_target_pairs={{0,3},{1,0},{2,1},{3,2},{4,7},{5,4},{6,5},{7,6},{8,11},{9,8},{10,9... | collective-permute-start | bytes 1277960 | tf_op jit(solution)/shard_map/ppermute | solution.py:597
  49.1 40.1 %collective-permute-start.3 = (bf16[1,4,13,64,128]{4,3,2,1,0:T(8,128)(2,1)S(1)}, bf16[1,4,13,64,128]{4,3,2,1,0:T(8,128)(2,1)S(1)}, u32[]{:S(2)}, u32[]{:S(2)}) collective-permute-start(bf16[1,4,13,64,128]{4,3,2,1,0:T(8,128)(2,1)S(1)} %maximum_bitcast_fusion.1), channel_id=1, source_target_pairs={{0,8},{4,12},{8,0},{12,4},{16,24},{20,28},{24,16},{28,20},{1,9},{5... | collective-permute-start | bytes 2555912 | tf_op jit(solution)/shard_map/ppermute | solution.py:592
  50.8 41.4 %collective-permute-start.6 = (bf16[1,4,13,64,128]{4,3,2,1,0:T(8,128)(2,1)S(1)}, bf16[1,4,13,64,128]{4,3,2,1,0:T(8,128)(2,1)S(1)}, u32[]{:S(2)}, u32[]{:S(2)}) collective-permute-start(bf16[1,4,13,64,128]{4,3,2,1,0:T(8,128)(2,1)S(1)} %maximum_bitcast_fusion.2), channel_id=1, source_target_pairs={{0,16},{4,20},{8,24},{12,28},{16,0},{20,4},{24,8},{28,12},{1,17},{... | collective-permute-start | bytes 2555912 | tf_op jit(solution)/shard_map/ppermute | solution.py:592
  52.5 49.5 %collective-permute-start.9 = (bf16[1,128,1536]{2,1,0:T(8,128)(2,1)S(1)}, bf16[1,128,1536]{2,1,0:T(8,128)(2,1)S(1)}, u32[]{:S(2)}, u32[]{:S(2)}) collective-permute-start(bf16[1,128,1536]{2,1,0:T(8,128)(2,1)S(1)} %pad_maximum_fusion.12), channel_id=1, source_target_pairs={{0,8},{4,12},{8,0},{12,4},{16,24},{20,28},{24,16},{28,20},{1,9},{5... | collective-permute-start | bytes 1179656 | tf_op jit(solution)/shard_map/ppermute | solution.py:592
  90.7 86.5 %collective-permute-start.4 = (bf16[2,4,13,64,128]{4,3,2,1,0:T(8,128)(2,1)}, bf16[2,4,13,64,128]{4,3,2,1,0:T(8,128)(2,1)}, u32[]{:S(2)}, u32[]{:S(2)}) collective-permute-start(bf16[2,4,13,64,128]{4,3,2,1,0:T(8,128)(2,1)} %pad_maximum_fusion.3), channel_id=1, source_target_pairs={{0,16},{4,20},{8,24},{12,28},{16,0},{20,4},{24,8},{28,12},{1,17},{... | collective-permute-start | bytes 5111816 | tf_op jit(solution)/shard_map/ppermute | solution.py:592
  93.7 85.7 %collective-permute-start.7 = (bf16[2,4,13,64,128]{4,3,2,1,0:T(8,128)(2,1)}, bf16[2,4,13,64,128]{4,3,2,1,0:T(8,128)(2,1)}, u32[]{:S(2)}, u32[]{:S(2)}) collective-permute-start(bf16[2,4,13,64,128]{4,3,2,1,0:T(8,128)(2,1)} %pad_maximum_fusion.4), channel_id=1, source_target_pairs={{0,8},{4,12},{8,0},{12,4},{16,24},{20,28},{24,16},{28,20},{1,9},{5... | collective-permute-start | bytes 5111816 | tf_op jit(solution)/shard_map/ppermute | solution.py:592
  103.0 72.8 %collective-permute-start.10 = (bf16[2,128,1536]{2,1,0:T(8,128)(2,1)}, bf16[2,128,1536]{2,1,0:T(8,128)(2,1)}, u32[]{:S(2)}, u32[]{:S(2)}) collective-permute-start(bf16[2,128,1536]{2,1,0:T(8,128)(2,1)} %pad_maximum_fusion.9), channel_id=1, source_target_pairs={{0,16},{4,20},{8,24},{12,28},{16,0},{20,4},{24,8},{28,12},{1,17},{... | collective-permute-start | bytes 2359304 | tf_op jit(solution)/shard_map/ppermute | solution.py:592
  177.1 8.2 %collective-permute-start.11 = (bf16[4,128,1536]{2,1,0:T(8,128)(2,1)S(1)}, bf16[4,128,1536]{2,1,0:T(8,128)(2,1)S(1)}, u32[]{:S(2)}, u32[]{:S(2)}) collective-permute-start(bf16[4,128,1536]{2,1,0:T(8,128)(2,1)S(1)} %pad_maximum_fusion.5), channel_id=1, source_target_pairs={{0,4},{4,0},{8,12},{12,8},{16,20},{20,16},{24,28},{28,24},{1,5},{5... | collective-permute-start | bytes 4718600 | tf_op jit(solution)/shard_map/ppermute | solution.py:592
  178.9 6.8 collective-permute-start.5
  181.8 9.9 %collective-permute-start.8 = (bf16[4,4,13,64,128]{4,3,2,1,0:T(8,128)(2,1)S(1)}, bf16[4,4,13,64,128]{4,3,2,1,0:T(8,128)(2,1)}, u32[]{:S(2)}, u32[]{:S(2)}) collective-permute-start(bf16[4,4,13,64,128]{4,3,2,1,0:T(8,128)(2,1)S(1)} %pad_maximum_fusion.1.own_b), channel_id=1, source_target_pairs={{0,4},{4,0},{8,12},{12,8},{16,20},{20,16},{24,28},{28,24},{1,5},{5... | collective-permute-start | bytes 10223624 | tf_op jit(solution)/shard_map/ppermute | solution.py:592
  291.1 224.3 %reduce-scatter.5.cloned.1.call-start = ((), (), s32[]{:S(2)}) async-start(), calls=%async_computation.6 | async-start | bytes 11943936 | tf_op jit(solution)/shard_map/reduce_scatter | solution.py:808
  295.9 55.0 %collective-permute-start.13 = (bf16[2,128,1536]{2,1,0:T(8,128)(2,1)}, bf16[2,128,1536]{2,1,0:T(8,128)(2,1)}, u32[]{:S(2)}, u32[]{:S(2)}) collective-permute-start(bf16[2,128,1536]{2,1,0:T(8,128)(2,1)} %add_bitcast_fusion.10), channel_id=1, source_target_pairs={{0,8},{4,12},{8,0},{12,4},{16,24},{20,28},{24,16},{28,20},{1,9},{5... | collective-permute-start | bytes 2359304 | tf_op jit(solution)/shard_map/ppermute | solution.py:592
  348.0 40.0 %collective-permute-start.15 = (bf16[3,4,64,3456]{3,2,1,0:T(8,128)(2,1)}, bf16[3,4,64,3456]{3,2,1,0:T(8,128)(2,1)}, u32[]{:S(2)}, u32[]{:S(2)}) collective-permute-start(bf16[3,4,64,3456]{3,2,1,0:T(8,128)(2,1)} %get-tuple-element.97), channel_id=1, source_target_pairs={{0,4},{4,0},{8,12},{12,8},{16,20},{20,16},{24,28},{28,24},{1,5},{5... | collective-permute-start | bytes 15925256 | tf_op jit(solution)/shard_map/ppermute | solution.py:592
  348.2 272.1 %all-reduce.4.cloned.1.call-start = ((), (), s32[]{:S(2)}) async-start(), calls=%async_computation.7 | async-start | bytes 5308416 | tf_op jit(solution)/shard_map/psum | solution.py:860
  373.9 12.1 %collective-permute-start.17 = (bf16[128,1536]{1,0:T(8,128)(2,1)}, bf16[128,1536]{1,0:T(8,128)(2,1)}, u32[]{:S(2)}, u32[]{:S(2)}) collective-permute-start(bf16[128,1536]{1,0:T(8,128)(2,1)} %add_bitcast_fusion.13), channel_id=1, source_target_pairs={{0,16},{4,20},{8,24},{12,28},{16,0},{20,4},{24,8},{28,12},{1,17},{... | collective-permute-start | bytes 1179656 | tf_op jit(solution)/shard_map/ppermute | solution.py:592
  383.7 77.4 %collective-permute-start.14 = (bf16[13,4,256,128]{3,2,1,0:T(8,128)(2,1)}, bf16[13,4,256,128]{3,2,1,0:T(8,128)(2,1)}, u32[]{:S(2)}, u32[]{:S(2)}) collective-permute-start(bf16[13,4,256,128]{3,2,1,0:T(8,128)(2,1)} %get-tuple-element.95), channel_id=1, source_target_pairs={{0,4},{4,0},{8,12},{12,8},{16,20},{20,16},{24,28},{28,24},{1,5},{5... | collective-permute-start | bytes 10223624 | tf_op jit(solution)/shard_map/ppermute | solution.py:592
  393.8 58.8 %collective-permute-start.18 = (bf16[3,2,32,3456]{3,2,0,1:T(8,128)(2,1)}, bf16[3,2,32,3456]{3,2,0,1:T(8,128)(2,1)}, u32[]{:S(2)}, u32[]{:S(2)}) collective-permute-start(bf16[3,2,32,3456]{3,2,0,1:T(8,128)(2,1)} %get-tuple-element.158), channel_id=1, source_target_pairs={{0,16},{4,20},{8,24},{12,28},{16,0},{20,4},{24,8},{28,12},{1,17},{... | collective-permute-start | bytes 3981320 | tf_op jit(solution)/shard_map/ppermute | solution.py:592
  397.0 61.0 %collective-permute-start.16 = (bf16[3,2,32,3456]{3,2,0,1:T(8,128)(2,1)}, bf16[3,2,32,3456]{3,2,0,1:T(8,128)(2,1)}, u32[]{:S(2)}, u32[]{:S(2)}) collective-permute-start(bf16[3,2,32,3456]{3,2,0,1:T(8,128)(2,1)} %get-tuple-element.160), channel_id=1, source_target_pairs={{0,8},{4,12},{8,0},{12,4},{16,24},{20,28},{24,16},{28,20},{1,9},{5... | collective-permute-start | bytes 3981320 | tf_op jit(solution)/shard_map/ppermute | solution.py:592
  424.2 43.4 %collective-permute-start.42 = (bf16[1248,128]{1,0:T(8,128)(2,1)S(1)}, bf16[1248,128]{1,0:T(8,128)(2,1)S(1)}, u32[]{:S(2)}, u32[]{:S(2)}) collective-permute-start(bf16[1248,128]{1,0:T(8,128)(2,1)S(1)} %pad_maximum_fusion.16), channel_id=1, source_target_pairs={{0,3},{1,0},{2,1},{3,2},{4,7},{5,4},{6,5},{7,6},{8,11},{9,8},{10,9... | collective-permute-start | bytes 958472 | tf_op jit(solution)/shard_map/ppermute | solution.py:597
  440.0 28.1 %collective-permute-start.41 = (bf16[1248,128]{1,0:T(8,128)(2,1)S(1)}, bf16[1248,128]{1,0:T(8,128)(2,1)S(1)}, u32[]{:S(2)}, u32[]{:S(2)}) collective-permute-start(bf16[1248,128]{1,0:T(8,128)(2,1)S(1)} %pad_maximum_fusion.15), channel_id=1, source_target_pairs={{0,2},{1,3},{2,0},{3,1},{4,6},{5,7},{6,4},{7,5},{8,10},{9,11},{10,... | collective-permute-start | bytes 958472 | tf_op jit(solution)/shard_map/ppermute | solution.py:597
  452.6 15.7 %collective-permute-start.40 = (bf16[1248,128]{1,0:T(8,128)(2,1)S(1)}, bf16[1248,128]{1,0:T(8,128)(2,1)S(1)}, u32[]{:S(2)}, u32[]{:S(2)}) collective-permute-start(bf16[1248,128]{1,0:T(8,128)(2,1)S(1)} %pad_maximum_fusion.14), channel_id=1, source_target_pairs={{0,1},{1,2},{2,3},{3,0},{4,5},{5,6},{6,7},{7,4},{8,9},{9,10},{10,1... | collective-permute-start | bytes 958472 | tf_op jit(solution)/shard_map/ppermute | solution.py:597
  459.2 47.6 %collective-permute-start.20 = (bf16[3,32,3456]{2,1,0:T(8,128)(2,1)S(1)}, bf16[3,32,3456]{2,1,0:T(8,128)(2,1)S(1)}, u32[]{:S(2)}, u32[]{:S(2)}) collective-permute-start(bf16[3,32,3456]{2,1,0:T(8,128)(2,1)S(1)} %add_bitcast_fusion.12), channel_id=1, source_target_pairs={{0,16},{4,20},{8,24},{12,28},{16,0},{20,4},{24,8},{28,12},{1,17},{... | collective-permute-start | bytes 1990664 | tf_op jit(solution)/shard_map/ppermute | solution.py:592
  461.1 47.1 %collective-permute-start.21 = (bf16[3,32,3456]{2,1,0:T(8,128)(2,1)S(1)}, bf16[3,32,3456]{2,1,0:T(8,128)(2,1)S(1)}, u32[]{:S(2)}, u32[]{:S(2)}) collective-permute-start(bf16[3,32,3456]{2,1,0:T(8,128)(2,1)S(1)} %add_bitcast_fusion.11), channel_id=1, source_target_pairs={{0,8},{4,12},{8,0},{12,4},{16,24},{20,28},{24,16},{28,20},{1,9},{5... | collective-permute-start | bytes 1990664 | tf_op jit(solution)/shard_map/ppermute | solution.py:592
  467.7 59.2 %collective-permute-start.19 = (bf16[13,4,2,64,128]{4,3,0,1,2:T(8,128)(2,1)}, bf16[13,4,2,64,128]{4,3,0,1,2:T(8,128)(2,1)}, u32[]{:S(2)}, u32[]{:S(2)}) collective-permute-start(bf16[13,4,2,64,128]{4,3,0,1,2:T(8,128)(2,1)} %get-tuple-element.153), channel_id=1, source_target_pairs={{0,8},{4,12},{8,0},{12,4},{16,24},{20,28},{24,16},{28,20},{1,9},{5... | collective-permute-start | bytes 5111816 | tf_op jit(solution)/shard_map/ppermute | solution.py:592
  468.1 41.3 %collective-permute-start.23 = (bf16[13,4,256,128]{3,2,1,0:T(8,128)(2,1)S(1)}, bf16[13,4,256,128]{3,2,1,0:T(8,128)(2,1)S(1)}, u32[]{:S(2)}, u32[]{:S(2)}) collective-permute-start(bf16[13,4,256,128]{3,2,1,0:T(8,128)(2,1)S(1)} %copy-done.29), channel_id=1, source_target_pairs={{0,4},{4,0},{8,12},{12,8},{16,20},{20,16},{24,28},{28,24},{1,5},{5... | collective-permute-start | bytes 10223624 | tf_op jit(solution)/shard_map/ppermute | solution.py:592
  468.4 11.8 %collective-permute-start.43 = (bf16[1248,128]{1,0:T(8,128)(2,1)S(1)}, bf16[1248,128]{1,0:T(8,128)(2,1)S(1)}, u32[]{:S(2)}, u32[]{:S(2)}) collective-permute-start(bf16[1248,128]{1,0:T(8,128)(2,1)S(1)} %add_convert_fusion.1), channel_id=1, source_target_pairs={{0,1},{1,2},{2,3},{3,0},{4,5},{5,6},{6,7},{7,4},{8,9},{9,10},{10,1... | collective-permute-start | bytes 958472 | tf_op jit(solution)/shard_map/ppermute | solution.py:597
  480.2 16.2 %collective-permute-start.44 = (bf16[1248,128]{1,0:T(8,128)(2,1)S(1)}, bf16[1248,128]{1,0:T(8,128)(2,1)S(1)}, u32[]{:S(2)}, u32[]{:S(2)}) collective-permute-start(bf16[1248,128]{1,0:T(8,128)(2,1)S(1)} %add_convert_fusion.1), channel_id=1, source_target_pairs={{0,2},{1,3},{2,0},{3,1},{4,6},{5,7},{6,4},{7,5},{8,10},{9,11},{10,... | collective-permute-start | bytes 958472 | tf_op jit(solution)/shard_map/ppermute | solution.py:597
  496.4 9.6 %collective-permute-start.45 = (bf16[1248,128]{1,0:T(8,128)(2,1)S(1)}, bf16[1248,128]{1,0:T(8,128)(2,1)S(1)}, u32[]{:S(2)}, u32[]{:S(2)}) collective-permute-start(bf16[1248,128]{1,0:T(8,128)(2,1)S(1)} %add_convert_fusion.1), channel_id=1, source_target_pairs={{0,3},{1,0},{2,1},{3,2},{4,7},{5,4},{6,5},{7,6},{8,11},{9,8},{10,9... | collective-permute-start | bytes 958472 | tf_op jit(solution)/shard_map/ppermute | solution.py:597
  512.8 40.5 %collective-permute-start.24 = (bf16[13,4,2,64,128]{4,3,0,1,2:T(8,128)(2,1)}, bf16[13,4,2,64,128]{4,3,0,1,2:T(8,128)(2,1)}, u32[]{:S(2)}, u32[]{:S(2)}) collective-permute-start(bf16[13,4,2,64,128]{4,3,0,1,2:T(8,128)(2,1)} %get-tuple-element.155), channel_id=1, source_target_pairs={{0,16},{4,20},{8,24},{12,28},{16,0},{20,4},{24,8},{28,12},{1,17},{... | collective-permute-start | bytes 5111816 | tf_op jit(solution)/shard_map/ppermute | solution.py:592
  529.0 40.8 %collective-permute-start.22 = (bf16[13,4,64,128]{3,2,0,1:T(8,128)(2,1)}, bf16[13,4,64,128]{3,2,0,1:T(8,128)(2,1)}, u32[]{:S(2)}, u32[]{:S(2)}) collective-permute-start(bf16[13,4,64,128]{3,2,0,1:T(8,128)(2,1)} %add_bitcast_fusion.9), channel_id=1, source_target_pairs={{0,16},{4,20},{8,24},{12,28},{16,0},{20,4},{24,8},{28,12},{1,17},{... | collective-permute-start | bytes 2555912 | tf_op jit(solution)/shard_map/ppermute | solution.py:592
  554.8 17.5 %collective-permute-start.25 = (bf16[13,4,64,128]{3,2,0,1:T(8,128)(2,1)S(1)}, bf16[13,4,64,128]{3,2,0,1:T(8,128)(2,1)S(1)}, u32[]{:S(2)}, u32[]{:S(2)}) collective-permute-start(bf16[13,4,64,128]{3,2,0,1:T(8,128)(2,1)S(1)} %add_bitcast_fusion.8), channel_id=1, source_target_pairs={{0,8},{4,12},{8,0},{12,4},{16,24},{20,28},{24,16},{28,20},{1,9},{5... | collective-permute-start | bytes 2555912 | tf_op jit(solution)/shard_map/ppermute | solution.py:592
  621.7 16.6 %collective-permute-start.31 = (bf16[1664,128]{1,0:T(8,128)(2,1)S(1)}, bf16[1664,128]{1,0:T(8,128)(2,1)S(1)}, u32[]{:S(2)}, u32[]{:S(2)}) collective-permute-start(bf16[1664,128]{1,0:T(8,128)(2,1)S(1)} %get-tuple-element.167), channel_id=1, source_target_pairs={{0,1},{1,2},{2,3},{3,0},{4,5},{5,6},{6,7},{7,4},{8,9},{9,10},{10,1... | collective-permute-start | bytes 1277960 | tf_op jit(solution)/shard_map/ppermute | solution.py:597
  621.7 31.7 %collective-permute-start.32 = (bf16[1664,128]{1,0:T(8,128)(2,1)S(1)}, bf16[1664,128]{1,0:T(8,128)(2,1)S(1)}, u32[]{:S(2)}, u32[]{:S(2)}) collective-permute-start(bf16[1664,128]{1,0:T(8,128)(2,1)S(1)} %get-tuple-element.169), channel_id=1, source_target_pairs={{0,2},{1,3},{2,0},{3,1},{4,6},{5,7},{6,4},{7,5},{8,10},{9,11},{10,... | collective-permute-start | bytes 1277960 | tf_op jit(solution)/shard_map/ppermute | solution.py:597
  623.4 30.1 %collective-permute-start.33 = (bf16[1664,128]{1,0:T(8,128)(2,1)S(1)}, bf16[1664,128]{1,0:T(8,128)(2,1)S(1)}, u32[]{:S(2)}, u32[]{:S(2)}) collective-permute-start(bf16[1664,128]{1,0:T(8,128)(2,1)S(1)} %get-tuple-element.168), channel_id=1, source_target_pairs={{0,3},{1,0},{2,1},{3,2},{4,7},{5,4},{6,5},{7,6},{8,11},{9,8},{10,9... | collective-permute-start | bytes 1277960 | tf_op jit(solution)/shard_map/ppermute | solution.py:597
  654.8 22.0 %collective-permute-start.34 = (bf16[1,13,64,128]{3,2,1,0:T(8,128)(2,1)S(1)}, bf16[1,13,64,128]{3,2,1,0:T(8,128)(2,1)S(1)}, u32[]{:S(2)}, u32[]{:S(2)}) collective-permute-start(bf16[1,13,64,128]{3,2,1,0:T(8,128)(2,1)S(1)} %bitcast.239), channel_id=1, source_target_pairs={{0,8},{4,12},{8,0},{12,4},{16,24},{20,28},{24,16},{28,20},{1,9},{5... | collective-permute-start | bytes 638984 | tf_op jit(solution)/shard_map/ppermute | solution.py:592
  656.4 22.1 %collective-permute-start.37 = (bf16[1,13,64,128]{3,2,1,0:T(8,128)(2,1)S(1)}, bf16[1,13,64,128]{3,2,1,0:T(8,128)(2,1)S(1)}, u32[]{:S(2)}, u32[]{:S(2)}) collective-permute-start(bf16[1,13,64,128]{3,2,1,0:T(8,128)(2,1)S(1)} %bitcast.235), channel_id=1, source_target_pairs={{0,16},{4,20},{8,24},{12,28},{16,0},{20,4},{24,8},{28,12},{1,17},{... | collective-permute-start | bytes 638984 | tf_op jit(solution)/shard_map/ppermute | solution.py:592
  657.9 5.9 collective-permute-start.27
  663.8 4.2 collective-permute-start.28
  668.0 12.0 %collective-permute-start.29 = (f32[13442]{0:T(1024)S(1)}, f32[13442]{0:T(1024)S(1)}, u32[]{:S(2)}, u32[]{:S(2)}) collective-permute-start(f32[13442]{0:T(1024)S(1)} %add.626), channel_id=1, source_target_pairs={{0,1},{1,0},{2,3},{3,2},{4,5},{5,4},{6,7},{7,6},{8,9},{9,8},{10,11... | collective-permute-start | bytes 161312 | tf_op jit(solution)/shard_map/ppermute | solution.py:699
  676.9 10.2 %collective-permute-start.35 = (bf16[2,13,64,128]{3,2,1,0:T(8,128)(2,1)S(1)}, bf16[2,13,64,128]{3,2,1,0:T(8,128)(2,1)S(1)}, u32[]{:S(2)}, u32[]{:S(2)}) collective-permute-start(bf16[2,13,64,128]{3,2,1,0:T(8,128)(2,1)S(1)} %pad_maximum_fusion.10), channel_id=1, source_target_pairs={{0,16},{4,20},{8,24},{12,28},{16,0},{20,4},{24,8},{28,12},{1,17},{... | collective-permute-start | bytes 1277960 | tf_op jit(solution)/shard_map/ppermute | solution.py:592
  678.5 9.8 %collective-permute-start.38 = (bf16[2,13,64,128]{3,2,1,0:T(8,128)(2,1)S(1)}, bf16[2,13,64,128]{3,2,1,0:T(8,128)(2,1)S(1)}, u32[]{:S(2)}, u32[]{:S(2)}) collective-permute-start(bf16[2,13,64,128]{3,2,1,0:T(8,128)(2,1)S(1)} %pad_maximum_fusion.11), channel_id=1, source_target_pairs={{0,8},{4,12},{8,0},{12,4},{16,24},{20,28},{24,16},{28,20},{1,9},{5... | collective-permute-start | bytes 1277960 | tf_op jit(solution)/shard_map/ppermute | solution.py:592
  680.1 5.8 collective-permute-start.30
  (65 other events, 973.2 us)
Sparse Core Ops, SparseCore 0:
  10.5 89.1 all-gather.3
  102.2 90.0 all-gather.5
  194.8 54.9 all-gather.7
  291.2 74.8 reduce-scatter.2
  369.9 121.3 reduce-scatter.4
  515.6 104.6 all-reduce.3

commit v5 on v4

--- a/solution.py
+++ b/solution.py
@@ -17,6 +17,7 @@
 GROUP = 8
 SLOTS = 32
 LOW = 128
+PAIR = 2
 VMEM_BYTES = 60 * 2**20
 HINT = 10**10
 
@@ -537,41 +538,40 @@
 
 def row_kernel(earlier, core_ref, hits_ref, grad_ref, *refs):
     send_ref, keep_ref, both_ref = refs[earlier:]
-    both_ref[...] = left_product(hits_ref[0], grad_ref[...]).astype(jnp.bfloat16).reshape(both_ref.shape)
     core = core_ref[0]
-    send_ref[0] = both_ref[:, 1 - core]
-    keep_ref[0] = both_ref[:, core]
+    for index in range(PAIR):
+        grad = grad_ref[:, index * LOW : (index + 1) * LOW]
+        rows = left_product(grad, hits_ref[index]).T
+        both_ref[index] = rows.astype(jnp.bfloat16).reshape(both_ref.shape[1:])
+        send_ref[index] = both_ref[index, :, 1 - core]
+        keep_ref[index] = both_ref[index, :, core]
 
 
 def row_gradient(hits, grad_summed, start, stop, group, core, pieces, hint):
     unused, samples, rows = hits.shape
     half = rows // group // 2
     shape = jax.ShapeDtypeStruct((stop - start, group, half, LOW), jnp.bfloat16)
-    cuts = [start + (stop - start) * piece // pieces for piece in range(pieces + 1)]
+    cuts = [start + (stop - start) // PAIR * piece // pieces * PAIR for piece in range(pieces + 1)]
     results = []
     for first, last in zip(cuts[:-1], cuts[1:]):
-        spec = pl.BlockSpec((1, group, half, LOW), functools.partial(row_block, first - start))
+        spec = pl.BlockSpec((PAIR, group, half, LOW), functools.partial(row_block, (first - start) // PAIR))
         results = pl.pallas_call(
             functools.partial(row_kernel, len(results)),
             grid_spec=pltpu.PrefetchScalarGridSpec(
                 num_scalar_prefetch=1,
-                grid=(last - first,),
+                grid=((last - first) // PAIR,),
                 in_specs=[
-                    pl.BlockSpec((1, samples, rows), functools.partial(hits_block, first)),
-                    pl.BlockSpec((samples, LOW), functools.partial(column_block, first)),
+                    pl.BlockSpec((PAIR, samples, rows), functools.partial(hits_block, first // PAIR)),
+                    pl.BlockSpec((samples, PAIR * LOW), functools.partial(column_block, first // PAIR)),
                 ]
                 + [pl.BlockSpec(memory_space=pl.ANY)] * len(results),
                 out_specs=[spec, spec],
-                scratch_shapes=[pltpu.VMEM((group, 2, half, LOW), jnp.bfloat16)],
+                scratch_shapes=[pltpu.VMEM((PAIR, group, 2, half, LOW), jnp.bfloat16)],
             ),
             out_shape=[shape, shape],
             input_output_aliases={3: 0, 4: 1} if results else {},
             compiler_params=pltpu.CompilerParams(vmem_limit_bytes=VMEM_BYTES),
-            cost_estimate=pl.CostEstimate(
-                flops=hint,
-                bytes_accessed=2 * (last - first) * rows * (samples + LOW),
-                transcendentals=0,
-            ),
+            cost_estimate=pl.CostEstimate(flops=hint, bytes_accessed=1, transcendentals=0),
         )(core, hits, grad_summed, *results)
     return results
 
@@ -755,6 +755,8 @@
     own_part = own_part.astype(jnp.bfloat16)
     own_parts = [own_part] + [shift(own_part, step) for step in range(1, group)]
     half = features // 2
+    even = (half + 1) // PAIR * PAIR
+    row_spans = ((0, even, up_down), (even, features, down_up))
     spans = ((0, half, up_down), (half, features, down_up))
     table_halves = []
     table_keys = []
@@ -836,8 +838,8 @@
     up_p, up_q = up_sums
     row_sums = []
     grad_rows = after(grad_summed, late_sum.received)
-    for first, last, order in spans:
-        send, keep = row_gradient(hits, grad_rows, first, last, group, core, 2, 10**12 if first == 0 else HINT)
+    for first, last, order in row_spans:
+        send, keep = row_gradient(hits, grad_rows, first, last, group, core, 1, 10**12 if first == 0 else HINT)
         shape = (last - first, group) + (2,) * len(bits) + (part, width)
         row_sums.append(HalvingSum(keep.reshape(shape), flip(send, 1).reshape(shape), bits, order, 2))
         if len(row_sums) == 1:
@@ -848,12 +850,11 @@
             grad_rows = after(grad_rows, [item.sent for item in up_sums] + [late_sum.sent, share_one])
     row_p, row_q = row_sums
     one_total = GroupSum(share_one, late_sum.result())
-    one_total.scatter(keep)
-    first_sent = list(one_total.sent)
+    one_total.scatter(keep, row_p.received)
+    one_total.gather()
     for step in bits[1:]:
         for item in up_sums:
-            item.step(*first_sent)
-    one_total.gather(*[item.sent for item in up_sums])
+            item.step(one_total.sent)
     for item in row_sums:
         item.step(up_p.sent, up_q.sent)
     share_up = jnp.concatenate([item.result() for item in up_sums], axis=1)

time: 720 us -> 709 us (0.985)
  Pallas kernels: 243 us -> 232 us
    pallas_call x4 -> x2, Pallas kernels: 42.5 us -> 30.9 us  [row_gradient(): pl.pallas_call(functools.partial(row_kernel, len(results)), grid_spec=plt...]
    ppermute x29, waiting for transfers between devices: 103 us -> 114 us  [flip(): lax.ppermute(value, 'rep', [(i, i ^ bit) for i in range(lax.axis_size('re...]
    ppermute x12, waiting for transfers between devices: 71.2 us -> 61 us  [shift(): lax.ppermute(value, 'grp', [(i, (i + step) % size) for i in range(size)])]
  transfers between devices with their start and end apart: 52 -> 52, of which waited for: 25 -> 25; matrix products, arithmetic and copies ran while one was open for 16% -> 16% of each run, Pallas kernels for 30% -> 29%
where the time goes in v5:
time: 709 us; the launch traced here: 699 us
  waiting for transfers between devices  232 us (33%)
  Pallas kernels  232 us (33%)
  other arithmetic  89.2 us (13%)
  starting transfers between devices  78.7 us (11%)
  local copies, waits for them, and re-layouts  51.8 us (7%)
  between operations  15.6 us (2%)
    ppermute x29, waiting for transfers between devices, flip(): lax.ppermute(value, 'rep', [(i, i ^ bit) for i in range(lax.axis_size('re...  114 us
    ppermute x12, waiting for transfers between devices, shift(): lax.ppermute(value, 'grp', [(i, (i + step) % size) for i in range(size)])  61 us
    pallas_call x4, Pallas kernels, count(): pl.pallas_call(functools.partial(count_kernel, len(earlier)), grid=(last...  54.1 us
    pallas_call x1, Pallas kernels, cross_backward(): pl.pallas_call(cross_backward_kernel, grid_spec=pltpu.PrefetchScalarGridS...  51.1 us
    psum x1, waiting for transfers between devices, on_device(): share_up, share_down = lax.psum((share_up, share_down), 'grp')  45.5 us
    pallas_call x1, Pallas kernels, pool(): pl.pallas_call(functools.partial(pool_kernel, keys=keys, half=half), grid...  38.9 us
    ppermute x12, starting transfers between devices, shift(): lax.ppermute(value, 'grp', [(i, (i + step) % size) for i in range(size)])  38.3 us
    sub x7, other arithmetic, adamw(): return (weight - rate * moved, first, second)  33.7 us
  transfers between devices with their start and end apart: 52, of which 25 were waited for; matrix products, arithmetic and copies ran while one was open for 16% of the time, Pallas kernels for 29%

profile of v5, /device:TPU:0, one launch (start us, length us, event | category | flops | bytes accessed | tf_op | source)
XLA Modules:
  0.0 699.5 jit_solution(3671474460362392790)
XLA Ops:
  7.2 3.1 convert_element_type.79
  11.8 2.5 convert_element_type.81
  15.6 3.1 collective-permute-start
  18.7 2.6 collective-permute-start.1
  22.6 8.8 %collective-permute-done = bf16[26,64,128]{2,1,0:T(8,128)(2,1)S(1)} collective-permute-done((bf16[26,64,128]{2,1,0:T(8,128)(2,1)S(1)}, bf16[26,64,128]{2,1,0:T(8,128)(2,1)S(1)}, u32[]{:S(2)}, u32[]{:S(2)}) %collective-permute-start) | collective-permute-done | bytes 426016 | tf_op jit(solution)/shard_map/ppermute | solution.py:597
  31.5 17.4 %collective-permute-done.1 = bf16[26,64,128]{2,1,0:T(8,128)(2,1)S(1)} collective-permute-done((bf16[26,64,128]{2,1,0:T(8,128)(2,1)S(1)}, bf16[26,64,128]{2,1,0:T(8,128)(2,1)S(1)}, u32[]{:S(2)}, u32[]{:S(2)}) %collective-permute-start.1) | collective-permute-done | bytes 426016 | tf_op jit(solution)/shard_map/ppermute | solution.py:597
  53.1 36.1 %collective-permute-done.3 = bf16[1,4,13,64,128]{4,3,2,1,0:T(8,128)(2,1)S(1)} collective-permute-done((bf16[1,4,13,64,128]{4,3,2,1,0:T(8,128)(2,1)S(1)}, bf16[1,4,13,64,128]{4,3,2,1,0:T(8,128)(2,1)S(1)}, u32[]{:S(2)}, u32[]{:S(2)}) %collective-permute-start.3) | collective-permute-done | bytes 852000 | tf_op jit(solution)/shard_map/ppermute | solution.py:592
  95.4 6.6 collective-permute-done.9
  104.6 4.2 copy.66
  108.9 5.8 reshape.182.ids_ref
  114.6 12.6 %shard_map.408.refs_0_ = bf16[26,512,2048]{2,1,0:T(8,128)(2,1)} custom-call(s32[26,64,256]{2,1,0:T(8,128)} %reshape.182.ids_ref), custom_call_target="tpu_custom_call" | custom-call | flops 1 | bytes 1 | tf_op jit(solution)/shard_map/pallas_call | solution.py:114
  127.3 14.4 %shard_map.409.refs_0_ = bf16[26,512,2048]{2,1,0:T(8,128)(2,1)} custom-call(s32[26,64,256]{2,1,0:T(8,128)} %reshape.182.ids_ref, bf16[26,512,2048]{2,1,0:T(8,128)(2,1)} %shard_map.408.refs_0_), custom_call_target="tpu_custom_call", output_to_operand_aliasing={{}: (1, {})} | custom-call | flops 1 | bytes 1 | tf_op jit(solution)/shard_map/pallas_call | solution.py:114
  141.6 12.6 %shard_map.410.refs_0_ = bf16[26,512,2048]{2,1,0:T(8,128)(2,1)} custom-call(s32[26,64,256]{2,1,0:T(8,128)} %reshape.182.ids_ref, bf16[26,512,2048]{2,1,0:T(8,128)(2,1)} %shard_map.409.refs_0_), custom_call_target="tpu_custom_call", output_to_operand_aliasing={{}: (1, {})} | custom-call | flops 1 | bytes 1 | tf_op jit(solution)/shard_map/pallas_call | solution.py:114
  154.3 14.5 %shard_map.411.hits_ref = bf16[26,512,2048]{2,1,0:T(8,128)(2,1)} custom-call(s32[26,64,256]{2,1,0:T(8,128)} %reshape.182.ids_ref, bf16[26,512,2048]{2,1,0:T(8,128)(2,1)} %shard_map.410.refs_0_), custom_call_target="tpu_custom_call", output_to_operand_aliasing={{}: (1, {})} | custom-call | flops 1 | bytes 1 | tf_op jit(solution)/shard_map/pallas_call | solution.py:114
  188.8 2.8 collective-permute-done.8.other_b
  191.6 38.9 %shard_map.412.anchor_in = f32[512,3456]{1,0:T(8,128)} custom-call(s32[2]{0:T(128)} %pad_add_fusion.place_ref, bf16[26,512,2048]{2,1,0:T(8,128)(2,1)} %shard_map.411.hits_ref, bf16[4,4,13,64,128]{4,3,2,1,0:T(8,128)(2,1)} %copy-done, bf16[4,4,13,64,128]{4,3,2,1,0:T(8,128)(2,1)} %copy-done.23, bf16[4,4,13,64,128]{4,3,2,1,0:T(8,128)(2,1)} %copy-done.1, ...), custom_call_target="tpu_custom_call" | custom-call | flops 1 | bytes 1 | tf_op jit(solution)/shard_map/pallas_call | solution.py:181
  230.6 28.6 %shard_map.413 = (bf16[3,512,3456]{2,1,0:T(8,128)(2,1)}, bf16[3,512,512]{2,1,0:T(8,128)(2,1)}, bf16[512,3456]{1,0:T(8,128)(2,1)}) custom-call(f32[512,3456]{1,0:T(8,128)} %shard_map.412.anchor_in, bf16[3,3456,512]{2,1,0:T(8,128)(2,1)} %all-gather.4.cloned.1.call-done.down_ref, bf16[3,512,3456]{2,1,0:T(8,128)(2,1)} %all-gather.6.cloned.1.call-done.up_ref, ...), custom_call_target="tpu_custom_call" | custom-call | flops 1 | bytes 1 | tf_op jit(solution)/shard_map/pallas_call | solution.py:250
  259.2 28.5 %shard_map.414 = (f32[1,1]{1,0:T(1,128)}, f32[1,512]{1,0:T(1,128)}, f32[1,1]{1,0:T(1,128)}, f32[1,1024]{1,0:T(1,128)}, f32[1,1024]{1,0:T(1,128)}, /*index=5*/f32...) custom-call(bf16[512,3456]{1,0:T(8,128)(2,1)} %get-tuple-element.70.input_ref, ...), custom_call_target="tpu_custom_call" | custom-call | flops 1 | bytes 1 | tf_op jit(solution)/shard_map/pallas_call | solution.py:362
  291.2 3.5 collective-permute-done.12
  297.2 51.1 %shard_map.415 = (bf16[3,4,64,3456]{3,2,1,0:T(8,128)(2,1)}, bf16[3,4,64,3456]{3,2,1,0:T(8,128)(2,1)}, bf16[3,3456,512]{2,1,0:T(8,128)(2,1)}, f32[3,1,3456]{2,1,0:T(1,128)}, bf16[512,3456]{1,0:T(8,128)(2,1)}) custom-call(s32[1]{0:T(128)} %bitcast.core_ref, f32[512,3456]{1,0:T(8,128)} %shard_map.412.anchor_in, f32[512,3456]{1,0:T(8,128)} %get-tuple-element.75.grad_in, ...), custom_call_target="tpu_custom_call" | custom-call | flops 999999995904 | bytes 70778880 | tf_op jit(solution)/shard_map/pallas_call | solution.py:489
  351.2 16.5 %shard_map.416 = (bf16[14,4,256,128]{3,2,1,0:T(8,128)(2,1)}, bf16[14,4,256,128]{3,2,1,0:T(8,128)(2,1)}) custom-call(s32[1]{0:T(128)} %bitcast.core_ref, bf16[26,512,2048]{2,1,0:T(8,128)(2,1)} %shard_map.411.hits_ref, bf16[512,3456]{1,0:T(8,128)(2,1)} %get-tuple-element.98.grad_ref), custom_call_target="tpu_custom_call" | custom-call | flops 999999995904 | bytes 1 | tf_op jit(solution)/shard_map/pallas_call | solution.py:558
  369.7 2.9 fusion.41
  374.1 6.6 collective-permute-done.17
  381.7 4.4 fusion.40
  391.2 14.4 %shard_map.417 = (bf16[12,4,256,128]{3,2,1,0:T(8,128)(2,1)}, bf16[12,4,256,128]{3,2,1,0:T(8,128)(2,1)}) custom-call(s32[1]{0:T(128)} %bitcast.core_ref, bf16[26,512,2048]{2,1,0:T(8,128)(2,1)} %shard_map.411.hits_ref, bf16[512,3456]{1,0:T(8,128)(2,1)} %get-tuple-element.98.grad_ref), custom_call_target="tpu_custom_call" | custom-call | flops 10000000000 | bytes 1 | tf_op jit(solution)/shard_map/pallas_call | solution.py:558
  410.4 11.5 %collective-permute-start.18 = (bf16[1248,128]{1,0:T(8,128)(2,1)}, bf16[1248,128]{1,0:T(8,128)(2,1)}, u32[]{:S(2)}, u32[]{:S(2)}) collective-permute-start(bf16[1248,128]{1,0:T(8,128)(2,1)} %pad_maximum_fusion.13), channel_id=1, source_target_pairs={{0,1},{1,2},{2,3},{3,0},{4,5},{5,6},{6,7},{7,4},{8,9},{9,10},{10,1... | collective-permute-start | bytes 958472 | tf_op jit(solution)/shard_map/ppermute | solution.py:597
  428.8 3.8 collective-permute-done.18
  432.6 12.6 %collective-permute-done.19 = bf16[1248,128]{1,0:T(8,128)(2,1)} collective-permute-done((bf16[1248,128]{1,0:T(8,128)(2,1)}, bf16[1248,128]{1,0:T(8,128)(2,1)}, u32[]{:S(2)}, u32[]{:S(2)}) %collective-permute-start.19) | collective-permute-done | bytes 319520 | tf_op jit(solution)/shard_map/ppermute | solution.py:597
  446.7 7.4 %collective-permute-start.43 = (bf16[1248,128]{1,0:T(8,128)(2,1)S(1)}, bf16[1248,128]{1,0:T(8,128)(2,1)S(1)}, u32[]{:S(2)}, u32[]{:S(2)}) collective-permute-start(bf16[1248,128]{1,0:T(8,128)(2,1)S(1)} %add_convert_fusion.1), channel_id=1, source_target_pairs={{0,1},{1,2},{2,3},{3,0},{4,5},{5,6},{6,7},{7,4},{8,9},{9,10},{10,1... | collective-permute-start | bytes 958472 | tf_op jit(solution)/shard_map/ppermute | solution.py:597
  462.0 5.1 add_bitcast_fusion
  472.2 3.2 collective-permute-done.44
  476.9 6.3 collective-permute-done.23
  484.4 13.8 %collective-permute-done.24 = bf16[3,32,3456]{2,1,0:T(8,128)(2,1)S(1)} collective-permute-done((bf16[3,32,3456]{2,1,0:T(8,128)(2,1)S(1)}, bf16[3,32,3456]{2,1,0:T(8,128)(2,1)S(1)}, u32[]{:S(2)}, u32[]{:S(2)}) %collective-permute-start.24) | collective-permute-done | bytes 663584 | tf_op jit(solution)/shard_map/ppermute | solution.py:592
  499.4 2.6 add_bitcast_fusion.2
  506.7 2.6 reshape.205
  513.3 3.1 multiply_subtract_fusion.3
  516.4 19.6 %collective-permute-done.22 = bf16[14,4,2,64,128]{4,3,0,1,2:T(8,128)(2,1)} collective-permute-done((bf16[14,4,2,64,128]{4,3,0,1,2:T(8,128)(2,1)}, bf16[14,4,2,64,128]{4,3,0,1,2:T(8,128)(2,1)}, u32[]{:S(2)}, u32[]{:S(2)}) %collective-permute-start.22) | collective-permute-done | bytes 1835040 | tf_op jit(solution)/shard_map/ppermute | solution.py:592
  542.8 3.4 multiply_subtract_fusion.2
  546.2 12.3 %collective-permute-done.25 = bf16[14,4,64,128]{3,2,0,1:T(8,128)(2,1)S(1)} collective-permute-done((bf16[14,4,64,128]{3,2,0,1:T(8,128)(2,1)S(1)}, bf16[14,4,64,128]{3,2,0,1:T(8,128)(2,1)S(1)}, u32[]{:S(2)}, u32[]{:S(2)}) %collective-permute-start.25) | collective-permute-done | bytes 917536 | tf_op jit(solution)/shard_map/ppermute | solution.py:592
  563.1 45.5 %all-reduce.4.cloned.1.call-done = (bf16[3,64,3456]{2,1,0:T(8,128)(2,1)}, bf16[3,432,512]{2,1,0:T(8,128)(2,1)}) async-done(((bf16[3,64,3456]{2,1,0:T(8,128)(2,1)}, bf16[3,432,512]{2,1,0:T(8,128)(2,1)}), (bf16[3,64,3456]{2,1,0:T(8,128)(2,1)}, bf16[3,432,512]{2,1,0:T(8,128)(2,1)})) %all-reduce.4.cloned.1.call-update) | async-done | bytes 2654224 | tf_op jit(solution)/shard_map/psum | solution.py:861
  611.8 3.0 collective-permute-start.36
  614.8 7.1 %multiply_subtract_fusion = (f32[3,64,3456]{2,1,0:T(8,128)}, f32[3,64,3456]{2,1,0:T(8,128)}, f32[3,64,3456]{2,1,0:T(8,128)}) fusion(f32[3,64,3456]{2,1,0:T(8,128)S(1)} %copy-done.4, bf16[3,64,3456]{2,1,0:T(8,128)(2,1)S(1)} %copy-done.37, f32[3,64,3456]{2,1,0:T(8,128)} %param.36, f32[3,64,3456]{2,1,0:T(8,128)} %param.37), kind=kLoop, calls=%fused_computation.21 | loop fusion | flops 10616832 | bytes 17252352 | tf_op jit(solution)/shard_map/sub | solution.py:713
  622.0 4.7 multiply_subtract_fusion.1
  626.7 15.2 %collective-permute-done.35 = bf16[1664,128]{1,0:T(8,128)(2,1)S(1)} collective-permute-done((bf16[1664,128]{1,0:T(8,128)(2,1)S(1)}, bf16[1664,128]{1,0:T(8,128)(2,1)S(1)}, u32[]{:S(2)}, u32[]{:S(2)}) %collective-permute-start.35) | collective-permute-done | bytes 426016 | tf_op jit(solution)/shard_map/ppermute | solution.py:597
  647.3 4.9 collective-permute-done.30
  656.4 8.8 %collective-permute-start.32 = (f32[13442]{0:T(1024)S(1)}, f32[13442]{0:T(1024)S(1)}, u32[]{:S(2)}, u32[]{:S(2)}) collective-permute-start(f32[13442]{0:T(1024)S(1)} %add.630), channel_id=1, source_target_pairs={{0,1},{1,0},{2,3},{3,2},{4,5},{5,4},{6,7},{7,6},{8,9},{9,8},{10,11... | collective-permute-start | bytes 161312 | tf_op jit(solution)/shard_map/ppermute | solution.py:699
  669.9 4.3 collective-permute-done.33
  679.5 12.7 %add_subtract_fusion = (f32[26,512,128]{2,1,0:T(8,128)}, f32[26,512,128]{2,1,0:T(8,128)}, f32[26,512,128]{2,1,0:T(8,128)}) fusion(f32[26,512,128]{2,1,0:T(8,128)S(1)} %bitcast.228, bf16[13,512,128]{2,1,0:T(8,128)(2,1)S(1)} %fusion.17, bf16[13,512,128]{2,1,0:T(8,128)(2,1)S(1)} %fusion.23, f32[26,512,128]{2,1,0:T(8,128)} %param.30, f32[26,512,128]{2,1,0:T(8,128)} %param.31), kind=kLoop, calls=%fused_computation.4 | loop fusion | flops 27262976 | bytes 44302336 | tf_op jit(solution)/shard_map/sub | solution.py:713
  (308 shorter events, 127.9 us)
Async XLA Ops:
  7.2 223.3 %all-gather.4.cloned.1.call-start = ((), (), s32[]{:S(2)}) async-start(), calls=%async_computation.2 | async-start | bytes 11943936 | tf_op jit(solution)/shard_map/all_gather | solution.py:745
  10.4 220.1 %all-gather.6.cloned.1.call-start = ((), (), s32[]{:S(2)}) async-start(), calls=%async_computation.3 | async-start | bytes 11943936 | tf_op jit(solution)/shard_map/all_gather | solution.py:746
  11.7 247.5 %all-gather.8.cloned.1.call-start = ((), (), s32[]{:S(2)}) async-start(), calls=%async_computation.4 | async-start | bytes 7962624 | tf_op jit(solution)/shard_map/all_gather | solution.py:747
  14.3 376.9 %reduce-scatter.3.cloned.1.call-start = ((), (), s32[]{:S(2)}) async-start(), calls=%async_computation.5 | async-start | bytes 7962624 | tf_op jit(solution)/shard_map/reduce_scatter | solution.py:789
  15.6 15.9 %collective-permute-start = (bf16[26,64,128]{2,1,0:T(8,128)(2,1)S(1)}, bf16[26,64,128]{2,1,0:T(8,128)(2,1)S(1)}, u32[]{:S(2)}, u32[]{:S(2)}) collective-permute-start(bf16[26,64,128]{2,1,0:T(8,128)(2,1)S(1)} %dynamic-slice_convert_fusion), channel_id=1, source_target_pairs={{0,1},{1,2},{2,3},{3,0},{4,5},{5,6},{6,7},{7,4},{8,9},{9,10},{10,1... | collective-permute-start | bytes 1277960 | tf_op jit(solution)/shard_map/ppermute | solution.py:597
  18.7 30.2 %collective-permute-start.1 = (bf16[26,64,128]{2,1,0:T(8,128)(2,1)S(1)}, bf16[26,64,128]{2,1,0:T(8,128)(2,1)S(1)}, u32[]{:S(2)}, u32[]{:S(2)}) collective-permute-start(bf16[26,64,128]{2,1,0:T(8,128)(2,1)S(1)} %dynamic-slice_convert_fusion), channel_id=1, source_target_pairs={{0,2},{1,3},{2,0},{3,1},{4,6},{5,7},{6,4},{7,5},{8,10},{9,11},{10,... | collective-permute-start | bytes 1277960 | tf_op jit(solution)/shard_map/ppermute | solution.py:597
  21.3 27.7 %collective-permute-start.2 = (bf16[26,64,128]{2,1,0:T(8,128)(2,1)S(1)}, bf16[26,64,128]{2,1,0:T(8,128)(2,1)S(1)}, u32[]{:S(2)}, u32[]{:S(2)}) collective-permute-start(bf16[26,64,128]{2,1,0:T(8,128)(2,1)S(1)} %dynamic-slice_convert_fusion), channel_id=1, source_target_pairs={{0,3},{1,0},{2,1},{3,2},{4,7},{5,4},{6,5},{7,6},{8,11},{9,8},{10,9... | collective-permute-start | bytes 1277960 | tf_op jit(solution)/shard_map/ppermute | solution.py:597
  49.1 40.1 %collective-permute-start.3 = (bf16[1,4,13,64,128]{4,3,2,1,0:T(8,128)(2,1)S(1)}, bf16[1,4,13,64,128]{4,3,2,1,0:T(8,128)(2,1)S(1)}, u32[]{:S(2)}, u32[]{:S(2)}) collective-permute-start(bf16[1,4,13,64,128]{4,3,2,1,0:T(8,128)(2,1)S(1)} %maximum_bitcast_fusion.1), channel_id=1, source_target_pairs={{0,8},{4,12},{8,0},{12,4},{16,24},{20,28},{24,16},{28,20},{1,9},{5... | collective-permute-start | bytes 2555912 | tf_op jit(solution)/shard_map/ppermute | solution.py:592
  50.8 41.4 %collective-permute-start.6 = (bf16[1,4,13,64,128]{4,3,2,1,0:T(8,128)(2,1)S(1)}, bf16[1,4,13,64,128]{4,3,2,1,0:T(8,128)(2,1)S(1)}, u32[]{:S(2)}, u32[]{:S(2)}) collective-permute-start(bf16[1,4,13,64,128]{4,3,2,1,0:T(8,128)(2,1)S(1)} %maximum_bitcast_fusion.2), channel_id=1, source_target_pairs={{0,16},{4,20},{8,24},{12,28},{16,0},{20,4},{24,8},{28,12},{1,17},{... | collective-permute-start | bytes 2555912 | tf_op jit(solution)/shard_map/ppermute | solution.py:592
  52.5 49.5 %collective-permute-start.9 = (bf16[1,128,1536]{2,1,0:T(8,128)(2,1)S(1)}, bf16[1,128,1536]{2,1,0:T(8,128)(2,1)S(1)}, u32[]{:S(2)}, u32[]{:S(2)}) collective-permute-start(bf16[1,128,1536]{2,1,0:T(8,128)(2,1)S(1)} %pad_maximum_fusion.12), channel_id=1, source_target_pairs={{0,8},{4,12},{8,0},{12,4},{16,24},{20,28},{24,16},{28,20},{1,9},{5... | collective-permute-start | bytes 1179656 | tf_op jit(solution)/shard_map/ppermute | solution.py:592
  90.7 86.5 %collective-permute-start.4 = (bf16[2,4,13,64,128]{4,3,2,1,0:T(8,128)(2,1)}, bf16[2,4,13,64,128]{4,3,2,1,0:T(8,128)(2,1)}, u32[]{:S(2)}, u32[]{:S(2)}) collective-permute-start(bf16[2,4,13,64,128]{4,3,2,1,0:T(8,128)(2,1)} %pad_maximum_fusion.3), channel_id=1, source_target_pairs={{0,16},{4,20},{8,24},{12,28},{16,0},{20,4},{24,8},{28,12},{1,17},{... | collective-permute-start | bytes 5111816 | tf_op jit(solution)/shard_map/ppermute | solution.py:592
  93.7 85.7 %collective-permute-start.7 = (bf16[2,4,13,64,128]{4,3,2,1,0:T(8,128)(2,1)}, bf16[2,4,13,64,128]{4,3,2,1,0:T(8,128)(2,1)}, u32[]{:S(2)}, u32[]{:S(2)}) collective-permute-start(bf16[2,4,13,64,128]{4,3,2,1,0:T(8,128)(2,1)} %pad_maximum_fusion.4), channel_id=1, source_target_pairs={{0,8},{4,12},{8,0},{12,4},{16,24},{20,28},{24,16},{28,20},{1,9},{5... | collective-permute-start | bytes 5111816 | tf_op jit(solution)/shard_map/ppermute | solution.py:592
  103.0 72.8 %collective-permute-start.10 = (bf16[2,128,1536]{2,1,0:T(8,128)(2,1)}, bf16[2,128,1536]{2,1,0:T(8,128)(2,1)}, u32[]{:S(2)}, u32[]{:S(2)}) collective-permute-start(bf16[2,128,1536]{2,1,0:T(8,128)(2,1)} %pad_maximum_fusion.9), channel_id=1, source_target_pairs={{0,16},{4,20},{8,24},{12,28},{16,0},{20,4},{24,8},{28,12},{1,17},{... | collective-permute-start | bytes 2359304 | tf_op jit(solution)/shard_map/ppermute | solution.py:592
  177.1 8.1 %collective-permute-start.11 = (bf16[4,128,1536]{2,1,0:T(8,128)(2,1)S(1)}, bf16[4,128,1536]{2,1,0:T(8,128)(2,1)S(1)}, u32[]{:S(2)}, u32[]{:S(2)}) collective-permute-start(bf16[4,128,1536]{2,1,0:T(8,128)(2,1)S(1)} %pad_maximum_fusion.5), channel_id=1, source_target_pairs={{0,4},{4,0},{8,12},{12,8},{16,20},{20,16},{24,28},{28,24},{1,5},{5... | collective-permute-start | bytes 4718600 | tf_op jit(solution)/shard_map/ppermute | solution.py:592
  178.9 6.8 collective-permute-start.5
  181.8 9.9 %collective-permute-start.8 = (bf16[4,4,13,64,128]{4,3,2,1,0:T(8,128)(2,1)S(1)}, bf16[4,4,13,64,128]{4,3,2,1,0:T(8,128)(2,1)}, u32[]{:S(2)}, u32[]{:S(2)}) collective-permute-start(bf16[4,4,13,64,128]{4,3,2,1,0:T(8,128)(2,1)S(1)} %pad_maximum_fusion.1.own_b), channel_id=1, source_target_pairs={{0,4},{4,0},{8,12},{12,8},{16,20},{20,16},{24,28},{28,24},{1,5},{5... | collective-permute-start | bytes 10223624 | tf_op jit(solution)/shard_map/ppermute | solution.py:592
  291.2 213.0 %reduce-scatter.5.cloned.1.call-start = ((), (), s32[]{:S(2)}) async-start(), calls=%async_computation.6 | async-start | bytes 11943936 | tf_op jit(solution)/shard_map/reduce_scatter | solution.py:810
  296.0 55.2 %collective-permute-start.13 = (bf16[2,128,1536]{2,1,0:T(8,128)(2,1)}, bf16[2,128,1536]{2,1,0:T(8,128)(2,1)}, u32[]{:S(2)}, u32[]{:S(2)}) collective-permute-start(bf16[2,128,1536]{2,1,0:T(8,128)(2,1)} %add_bitcast_fusion.10), channel_id=1, source_target_pairs={{0,8},{4,12},{8,0},{12,4},{16,24},{20,28},{24,16},{28,20},{1,9},{5... | collective-permute-start | bytes 2359304 | tf_op jit(solution)/shard_map/ppermute | solution.py:592
  348.3 33.4 %collective-permute-start.15 = (bf16[3,4,64,3456]{3,2,1,0:T(8,128)(2,1)}, bf16[3,4,64,3456]{3,2,1,0:T(8,128)(2,1)}, u32[]{:S(2)}, u32[]{:S(2)}) collective-permute-start(bf16[3,4,64,3456]{3,2,1,0:T(8,128)(2,1)} %get-tuple-element.90), channel_id=1, source_target_pairs={{0,4},{4,0},{8,12},{12,8},{16,20},{20,16},{24,28},{28,24},{1,5},{5... | collective-permute-start | bytes 15925256 | tf_op jit(solution)/shard_map/ppermute | solution.py:592
  348.4 260.2 %all-reduce.4.cloned.1.call-start = ((), (), s32[]{:S(2)}) async-start(), calls=%async_computation.7 | async-start | bytes 5308416 | tf_op jit(solution)/shard_map/psum | solution.py:861
  368.8 11.9 %collective-permute-start.17 = (bf16[128,1536]{1,0:T(8,128)(2,1)S(1)}, bf16[128,1536]{1,0:T(8,128)(2,1)S(1)}, u32[]{:S(2)}, u32[]{:S(2)}) collective-permute-start(bf16[128,1536]{1,0:T(8,128)(2,1)S(1)} %add_bitcast_fusion.13), channel_id=1, source_target_pairs={{0,16},{4,20},{8,24},{12,28},{16,0},{20,4},{24,8},{28,12},{1,17},{... | collective-permute-start | bytes 1179656 | tf_op jit(solution)/shard_map/ppermute | solution.py:592
  372.6 33.0 %collective-permute-start.14 = (bf16[14,4,256,128]{3,2,1,0:T(8,128)(2,1)}, bf16[14,4,256,128]{3,2,1,0:T(8,128)(2,1)}, u32[]{:S(2)}, u32[]{:S(2)}) collective-permute-start(bf16[14,4,256,128]{3,2,1,0:T(8,128)(2,1)} %get-tuple-element.88), channel_id=1, source_target_pairs={{0,4},{4,0},{8,12},{12,8},{16,20},{20,16},{24,28},{28,24},{1,5},{5... | collective-permute-start | bytes 11010056 | tf_op jit(solution)/shard_map/ppermute | solution.py:592
  388.5 67.3 %collective-permute-start.16 = (bf16[3,2,32,3456]{3,2,0,1:T(8,128)(2,1)}, bf16[3,2,32,3456]{3,2,0,1:T(8,128)(2,1)}, u32[]{:S(2)}, u32[]{:S(2)}) collective-permute-start(bf16[3,2,32,3456]{3,2,0,1:T(8,128)(2,1)} %get-tuple-element.150), channel_id=1, source_target_pairs={{0,8},{4,12},{8,0},{12,4},{16,24},{20,28},{24,16},{28,20},{1,9},{5... | collective-permute-start | bytes 3981320 | tf_op jit(solution)/shard_map/ppermute | solution.py:592
  389.8 69.4 %collective-permute-start.21 = (bf16[3,2,32,3456]{3,2,0,1:T(8,128)(2,1)}, bf16[3,2,32,3456]{3,2,0,1:T(8,128)(2,1)}, u32[]{:S(2)}, u32[]{:S(2)}) collective-permute-start(bf16[3,2,32,3456]{3,2,0,1:T(8,128)(2,1)} %get-tuple-element.148), channel_id=1, source_target_pairs={{0,16},{4,20},{8,24},{12,28},{16,0},{20,4},{24,8},{28,12},{1,17},{... | collective-permute-start | bytes 3981320 | tf_op jit(solution)/shard_map/ppermute | solution.py:592
  410.4 22.2 %collective-permute-start.18 = (bf16[1248,128]{1,0:T(8,128)(2,1)}, bf16[1248,128]{1,0:T(8,128)(2,1)}, u32[]{:S(2)}, u32[]{:S(2)}) collective-permute-start(bf16[1248,128]{1,0:T(8,128)(2,1)} %pad_maximum_fusion.13), channel_id=1, source_target_pairs={{0,1},{1,2},{2,3},{3,0},{4,5},{5,6},{6,7},{7,4},{8,9},{9,10},{10,1... | collective-permute-start | bytes 958472 | tf_op jit(solution)/shard_map/ppermute | solution.py:597
  422.6 22.6 %collective-permute-start.19 = (bf16[1248,128]{1,0:T(8,128)(2,1)}, bf16[1248,128]{1,0:T(8,128)(2,1)}, u32[]{:S(2)}, u32[]{:S(2)}) collective-permute-start(bf16[1248,128]{1,0:T(8,128)(2,1)} %pad_maximum_fusion.14), channel_id=1, source_target_pairs={{0,2},{1,3},{2,0},{3,1},{4,6},{5,7},{6,4},{7,5},{8,10},{9,11},{10,... | collective-permute-start | bytes 958472 | tf_op jit(solution)/shard_map/ppermute | solution.py:597
  425.8 19.4 %collective-permute-start.20 = (bf16[1248,128]{1,0:T(8,128)(2,1)}, bf16[1248,128]{1,0:T(8,128)(2,1)}, u32[]{:S(2)}, u32[]{:S(2)}) collective-permute-start(bf16[1248,128]{1,0:T(8,128)(2,1)} %pad_maximum_fusion.15), channel_id=1, source_target_pairs={{0,3},{1,0},{2,1},{3,2},{4,7},{5,4},{6,5},{7,6},{8,11},{9,8},{10,9... | collective-permute-start | bytes 958472 | tf_op jit(solution)/shard_map/ppermute | solution.py:597
  432.6 66.8 %collective-permute-start.26 = (bf16[12,4,256,128]{3,2,1,0:T(8,128)(2,1)}, bf16[12,4,256,128]{3,2,1,0:T(8,128)(2,1)S(1)}, u32[]{:S(2)}, u32[]{:S(2)}) collective-permute-start(bf16[12,4,256,128]{3,2,1,0:T(8,128)(2,1)} %get-tuple-element.110), channel_id=1, source_target_pairs={{0,4},{4,0},{8,12},{12,8},{16,20},{20,16},{24,28},{28,24},{1,5},{5... | collective-permute-start | bytes 9437192 | tf_op jit(solution)/shard_map/ppermute | solution.py:592
  446.7 22.3 %collective-permute-start.43 = (bf16[1248,128]{1,0:T(8,128)(2,1)S(1)}, bf16[1248,128]{1,0:T(8,128)(2,1)S(1)}, u32[]{:S(2)}, u32[]{:S(2)}) collective-permute-start(bf16[1248,128]{1,0:T(8,128)(2,1)S(1)} %add_convert_fusion.1), channel_id=1, source_target_pairs={{0,1},{1,2},{2,3},{3,0},{4,5},{5,6},{6,7},{7,4},{8,9},{9,10},{10,1... | collective-permute-start | bytes 958472 | tf_op jit(solution)/shard_map/ppermute | solution.py:597
  454.1 21.3 %collective-permute-start.44 = (bf16[1248,128]{1,0:T(8,128)(2,1)S(1)}, bf16[1248,128]{1,0:T(8,128)(2,1)S(1)}, u32[]{:S(2)}, u32[]{:S(2)}) collective-permute-start(bf16[1248,128]{1,0:T(8,128)(2,1)S(1)} %add_convert_fusion.1), channel_id=1, source_target_pairs={{0,2},{1,3},{2,0},{3,1},{4,6},{5,7},{6,4},{7,5},{8,10},{9,11},{10,... | collective-permute-start | bytes 958472 | tf_op jit(solution)/shard_map/ppermute | solution.py:597
  455.7 20.4 %collective-permute-start.45 = (bf16[1248,128]{1,0:T(8,128)(2,1)S(1)}, bf16[1248,128]{1,0:T(8,128)(2,1)S(1)}, u32[]{:S(2)}, u32[]{:S(2)}) collective-permute-start(bf16[1248,128]{1,0:T(8,128)(2,1)S(1)} %add_convert_fusion.1), channel_id=1, source_target_pairs={{0,3},{1,0},{2,1},{3,2},{4,7},{5,4},{6,5},{7,6},{8,11},{9,8},{10,9... | collective-permute-start | bytes 958472 | tf_op jit(solution)/shard_map/ppermute | solution.py:597
  459.2 24.0 %collective-permute-start.23 = (bf16[3,32,3456]{2,1,0:T(8,128)(2,1)S(1)}, bf16[3,32,3456]{2,1,0:T(8,128)(2,1)S(1)}, u32[]{:S(2)}, u32[]{:S(2)}) collective-permute-start(bf16[3,32,3456]{2,1,0:T(8,128)(2,1)S(1)} %add_bitcast_fusion.12), channel_id=1, source_target_pairs={{0,16},{4,20},{8,24},{12,28},{16,0},{20,4},{24,8},{28,12},{1,17},{... | collective-permute-start | bytes 1990664 | tf_op jit(solution)/shard_map/ppermute | solution.py:592
  469.0 29.2 %collective-permute-start.24 = (bf16[3,32,3456]{2,1,0:T(8,128)(2,1)S(1)}, bf16[3,32,3456]{2,1,0:T(8,128)(2,1)S(1)}, u32[]{:S(2)}, u32[]{:S(2)}) collective-permute-start(bf16[3,32,3456]{2,1,0:T(8,128)(2,1)S(1)} %add_bitcast_fusion.11), channel_id=1, source_target_pairs={{0,8},{4,12},{8,0},{12,4},{16,24},{20,28},{24,16},{28,20},{1,9},{5... | collective-permute-start | bytes 1990664 | tf_op jit(solution)/shard_map/ppermute | solution.py:592
  475.4 60.6 %collective-permute-start.22 = (bf16[14,4,2,64,128]{4,3,0,1,2:T(8,128)(2,1)}, bf16[14,4,2,64,128]{4,3,0,1,2:T(8,128)(2,1)}, u32[]{:S(2)}, u32[]{:S(2)}) collective-permute-start(bf16[14,4,2,64,128]{4,3,0,1,2:T(8,128)(2,1)} %get-tuple-element.143), channel_id=1, source_target_pairs={{0,8},{4,12},{8,0},{12,4},{16,24},{20,28},{24,16},{28,20},{1,9},{5... | collective-permute-start | bytes 5505032 | tf_op jit(solution)/shard_map/ppermute | solution.py:592
  502.0 38.9 %collective-permute-start.27 = (bf16[12,4,2,64,128]{4,3,0,1,2:T(8,128)(2,1)}, bf16[12,4,2,64,128]{4,3,0,1,2:T(8,128)(2,1)}, u32[]{:S(2)}, u32[]{:S(2)}) collective-permute-start(bf16[12,4,2,64,128]{4,3,0,1,2:T(8,128)(2,1)} %get-tuple-element.145), channel_id=1, source_target_pairs={{0,16},{4,20},{8,24},{12,28},{16,0},{20,4},{24,8},{28,12},{1,17},{... | collective-permute-start | bytes 4718600 | tf_op jit(solution)/shard_map/ppermute | solution.py:592
  537.4 21.1 %collective-permute-start.25 = (bf16[14,4,64,128]{3,2,0,1:T(8,128)(2,1)S(1)}, bf16[14,4,64,128]{3,2,0,1:T(8,128)(2,1)S(1)}, u32[]{:S(2)}, u32[]{:S(2)}) collective-permute-start(bf16[14,4,64,128]{3,2,0,1:T(8,128)(2,1)S(1)} %add_bitcast_fusion.8), channel_id=1, source_target_pairs={{0,16},{4,20},{8,24},{12,28},{16,0},{20,4},{24,8},{28,12},{1,17},{... | collective-permute-start | bytes 2752520 | tf_op jit(solution)/shard_map/ppermute | solution.py:592
  542.1 18.3 %collective-permute-start.28 = (bf16[12,4,64,128]{3,2,0,1:T(8,128)(2,1)S(1)}, bf16[12,4,64,128]{3,2,0,1:T(8,128)(2,1)S(1)}, u32[]{:S(2)}, u32[]{:S(2)}) collective-permute-start(bf16[12,4,64,128]{3,2,0,1:T(8,128)(2,1)S(1)} %add_bitcast_fusion.9), channel_id=1, source_target_pairs={{0,8},{4,12},{8,0},{12,4},{16,24},{20,28},{24,16},{28,20},{1,9},{5... | collective-permute-start | bytes 2359304 | tf_op jit(solution)/shard_map/ppermute | solution.py:592
  610.1 16.6 %collective-permute-start.34 = (bf16[1664,128]{1,0:T(8,128)(2,1)S(1)}, bf16[1664,128]{1,0:T(8,128)(2,1)S(1)}, u32[]{:S(2)}, u32[]{:S(2)}) collective-permute-start(bf16[1664,128]{1,0:T(8,128)(2,1)S(1)} %get-tuple-element.157), channel_id=1, source_target_pairs={{0,1},{1,2},{2,3},{3,0},{4,5},{5,6},{6,7},{7,4},{8,9},{9,10},{10,1... | collective-permute-start | bytes 1277960 | tf_op jit(solution)/shard_map/ppermute | solution.py:597
  610.1 31.7 %collective-permute-start.35 = (bf16[1664,128]{1,0:T(8,128)(2,1)S(1)}, bf16[1664,128]{1,0:T(8,128)(2,1)S(1)}, u32[]{:S(2)}, u32[]{:S(2)}) collective-permute-start(bf16[1664,128]{1,0:T(8,128)(2,1)S(1)} %get-tuple-element.159), channel_id=1, source_target_pairs={{0,2},{1,3},{2,0},{3,1},{4,6},{5,7},{6,4},{7,5},{8,10},{9,11},{10,... | collective-permute-start | bytes 1277960 | tf_op jit(solution)/shard_map/ppermute | solution.py:597
  611.8 30.1 %collective-permute-start.36 = (bf16[1664,128]{1,0:T(8,128)(2,1)S(1)}, bf16[1664,128]{1,0:T(8,128)(2,1)S(1)}, u32[]{:S(2)}, u32[]{:S(2)}) collective-permute-start(bf16[1664,128]{1,0:T(8,128)(2,1)S(1)} %get-tuple-element.158), channel_id=1, source_target_pairs={{0,3},{1,0},{2,1},{3,2},{4,7},{5,4},{6,5},{7,6},{8,11},{9,8},{10,9... | collective-permute-start | bytes 1277960 | tf_op jit(solution)/shard_map/ppermute | solution.py:597
  643.2 22.0 %collective-permute-start.37 = (bf16[1,13,64,128]{3,2,1,0:T(8,128)(2,1)S(1)}, bf16[1,13,64,128]{3,2,1,0:T(8,128)(2,1)S(1)}, u32[]{:S(2)}, u32[]{:S(2)}) collective-permute-start(bf16[1,13,64,128]{3,2,1,0:T(8,128)(2,1)S(1)} %bitcast.237), channel_id=1, source_target_pairs={{0,8},{4,12},{8,0},{12,4},{16,24},{20,28},{24,16},{28,20},{1,9},{5... | collective-permute-start | bytes 638984 | tf_op jit(solution)/shard_map/ppermute | solution.py:592
  644.8 22.1 %collective-permute-start.40 = (bf16[1,13,64,128]{3,2,1,0:T(8,128)(2,1)S(1)}, bf16[1,13,64,128]{3,2,1,0:T(8,128)(2,1)S(1)}, u32[]{:S(2)}, u32[]{:S(2)}) collective-permute-start(bf16[1,13,64,128]{3,2,1,0:T(8,128)(2,1)S(1)} %bitcast.233), channel_id=1, source_target_pairs={{0,16},{4,20},{8,24},{12,28},{16,0},{20,4},{24,8},{28,12},{1,17},{... | collective-permute-start | bytes 638984 | tf_op jit(solution)/shard_map/ppermute | solution.py:592
  646.2 5.9 collective-permute-start.30
  652.2 4.2 collective-permute-start.31
  656.4 12.0 %collective-permute-start.32 = (f32[13442]{0:T(1024)S(1)}, f32[13442]{0:T(1024)S(1)}, u32[]{:S(2)}, u32[]{:S(2)}) collective-permute-start(f32[13442]{0:T(1024)S(1)} %add.630), channel_id=1, source_target_pairs={{0,1},{1,0},{2,3},{3,2},{4,5},{5,4},{6,7},{7,6},{8,9},{9,8},{10,11... | collective-permute-start | bytes 161312 | tf_op jit(solution)/shard_map/ppermute | solution.py:699
  665.3 10.2 %collective-permute-start.38 = (bf16[2,13,64,128]{3,2,1,0:T(8,128)(2,1)S(1)}, bf16[2,13,64,128]{3,2,1,0:T(8,128)(2,1)S(1)}, u32[]{:S(2)}, u32[]{:S(2)}) collective-permute-start(bf16[2,13,64,128]{3,2,1,0:T(8,128)(2,1)S(1)} %pad_maximum_fusion.10), channel_id=1, source_target_pairs={{0,16},{4,20},{8,24},{12,28},{16,0},{20,4},{24,8},{28,12},{1,17},{... | collective-permute-start | bytes 1277960 | tf_op jit(solution)/shard_map/ppermute | solution.py:592
  666.9 9.8 %collective-permute-start.41 = (bf16[2,13,64,128]{3,2,1,0:T(8,128)(2,1)S(1)}, bf16[2,13,64,128]{3,2,1,0:T(8,128)(2,1)S(1)}, u32[]{:S(2)}, u32[]{:S(2)}) collective-permute-start(bf16[2,13,64,128]{3,2,1,0:T(8,128)(2,1)S(1)} %pad_maximum_fusion.11), channel_id=1, source_target_pairs={{0,8},{4,12},{8,0},{12,4},{16,24},{20,28},{24,16},{28,20},{1,9},{5... | collective-permute-start | bytes 1277960 | tf_op jit(solution)/shard_map/ppermute | solution.py:592
  668.5 5.8 collective-permute-start.33
  (59 other events, 972.2 us)
Sparse Core Ops, SparseCore 0:
  10.5 89.1 all-gather.3
  102.2 90.0 all-gather.5
  194.8 54.9 all-gather.7
  291.3 74.8 reduce-scatter.2
  370.0 126.5 reduce-scatter.4
  504.3 104.2 all-reduce.3

commit v6 on v5

--- a/solution.py
+++ b/solution.py
@@ -865,7 +865,10 @@
     row_parts = [item.result() for item in row_sums]
     row_total = GroupSum(jnp.concatenate(row_parts, axis=0).transpose(1, 0, 2, 3))
     row_total.scatter(share_up, share_down)
-    small = SmallSum(after(small_grad, row_total.sent))
+    small = SmallSum(after(small_grad, row_parts))
+    small.step()
+    small.step()
+    small.value = after(small.value, row_total.sent)
     small.finish()
     row_share = row_total.total.reshape(features, part, width)
     share_one, share_late = one_total.result()

time: 709 us -> 707 us (level)
  transfers between devices with their start and end apart: 52 -> 52, of which waited for: 25 -> 26; matrix products, arithmetic and copies ran while one was open for 16% -> 17% of each run, Pallas kernels for 29% -> 29%
where the time goes in v6:
time: 707 us; the launch traced here: 698 us
  waiting for transfers between devices  232 us (33%)
  Pallas kernels  232 us (33%)
  other arithmetic  89.2 us (13%)
  starting transfers between devices  77.6 us (11%)
  local copies, waits for them, and re-layouts  51.8 us (7%)
  between operations  15.7 us (2%)
    ppermute x29, waiting for transfers between devices, flip(): lax.ppermute(value, 'rep', [(i, i ^ bit) for i in range(lax.axis_size('re...  119 us
    ppermute x12, waiting for transfers between devices, shift(): lax.ppermute(value, 'grp', [(i, (i + step) % size) for i in range(size)])  61 us
    pallas_call x4, Pallas kernels, count(): pl.pallas_call(functools.partial(count_kernel, len(earlier)), grid=(last...  54.1 us
    pallas_call x1, Pallas kernels, cross_backward(): pl.pallas_call(cross_backward_kernel, grid_spec=pltpu.PrefetchScalarGridS...  51.1 us
    psum x1, waiting for transfers between devices, on_device(): share_up, share_down = lax.psum((share_up, share_down), 'grp')  45.1 us
    pallas_call x1, Pallas kernels, pool(): pl.pallas_call(functools.partial(pool_kernel, keys=keys, half=half), grid...  38.9 us
    ppermute x12, starting transfers between devices, shift(): lax.ppermute(value, 'grp', [(i, (i + step) % size) for i in range(size)])  38.3 us
    sub x7, other arithmetic, adamw(): return (weight - rate * moved, first, second)  33.7 us
  transfers between devices with their start and end apart: 52, of which 26 were waited for; matrix products, arithmetic and copies ran while one was open for 17% of the time, Pallas kernels for 29%

profile of v6, /device:TPU:0, one launch (start us, length us, event | category | flops | bytes accessed | tf_op | source)
XLA Modules:
  0.0 698.0 jit_solution(15568151416910264813)
XLA Ops:
  7.2 3.1 convert_element_type.79
  11.8 2.5 convert_element_type.81
  15.6 3.1 collective-permute-start
  18.7 2.6 collective-permute-start.1
  22.6 8.8 %collective-permute-done = bf16[26,64,128]{2,1,0:T(8,128)(2,1)S(1)} collective-permute-done((bf16[26,64,128]{2,1,0:T(8,128)(2,1)S(1)}, bf16[26,64,128]{2,1,0:T(8,128)(2,1)S(1)}, u32[]{:S(2)}, u32[]{:S(2)}) %collective-permute-start) | collective-permute-done | bytes 426016 | tf_op jit(solution)/shard_map/ppermute | solution.py:597
  31.5 17.4 %collective-permute-done.1 = bf16[26,64,128]{2,1,0:T(8,128)(2,1)S(1)} collective-permute-done((bf16[26,64,128]{2,1,0:T(8,128)(2,1)S(1)}, bf16[26,64,128]{2,1,0:T(8,128)(2,1)S(1)}, u32[]{:S(2)}, u32[]{:S(2)}) %collective-permute-start.1) | collective-permute-done | bytes 426016 | tf_op jit(solution)/shard_map/ppermute | solution.py:597
  53.1 36.1 %collective-permute-done.3 = bf16[1,4,13,64,128]{4,3,2,1,0:T(8,128)(2,1)S(1)} collective-permute-done((bf16[1,4,13,64,128]{4,3,2,1,0:T(8,128)(2,1)S(1)}, bf16[1,4,13,64,128]{4,3,2,1,0:T(8,128)(2,1)S(1)}, u32[]{:S(2)}, u32[]{:S(2)}) %collective-permute-start.3) | collective-permute-done | bytes 852000 | tf_op jit(solution)/shard_map/ppermute | solution.py:592
  95.4 6.6 collective-permute-done.9
  104.6 4.2 copy.66
  108.9 5.8 reshape.182.ids_ref
  114.6 12.6 %shard_map.408.refs_0_ = bf16[26,512,2048]{2,1,0:T(8,128)(2,1)} custom-call(s32[26,64,256]{2,1,0:T(8,128)} %reshape.182.ids_ref), custom_call_target="tpu_custom_call" | custom-call | flops 1 | bytes 1 | tf_op jit(solution)/shard_map/pallas_call | solution.py:114
  127.3 14.4 %shard_map.409.refs_0_ = bf16[26,512,2048]{2,1,0:T(8,128)(2,1)} custom-call(s32[26,64,256]{2,1,0:T(8,128)} %reshape.182.ids_ref, bf16[26,512,2048]{2,1,0:T(8,128)(2,1)} %shard_map.408.refs_0_), custom_call_target="tpu_custom_call", output_to_operand_aliasing={{}: (1, {})} | custom-call | flops 1 | bytes 1 | tf_op jit(solution)/shard_map/pallas_call | solution.py:114
  141.6 12.6 %shard_map.410.refs_0_ = bf16[26,512,2048]{2,1,0:T(8,128)(2,1)} custom-call(s32[26,64,256]{2,1,0:T(8,128)} %reshape.182.ids_ref, bf16[26,512,2048]{2,1,0:T(8,128)(2,1)} %shard_map.409.refs_0_), custom_call_target="tpu_custom_call", output_to_operand_aliasing={{}: (1, {})} | custom-call | flops 1 | bytes 1 | tf_op jit(solution)/shard_map/pallas_call | solution.py:114
  154.3 14.5 %shard_map.411.hits_ref = bf16[26,512,2048]{2,1,0:T(8,128)(2,1)} custom-call(s32[26,64,256]{2,1,0:T(8,128)} %reshape.182.ids_ref, bf16[26,512,2048]{2,1,0:T(8,128)(2,1)} %shard_map.410.refs_0_), custom_call_target="tpu_custom_call", output_to_operand_aliasing={{}: (1, {})} | custom-call | flops 1 | bytes 1 | tf_op jit(solution)/shard_map/pallas_call | solution.py:114
  188.8 2.8 collective-permute-done.8.other_b
  191.6 38.9 %shard_map.412.anchor_in = f32[512,3456]{1,0:T(8,128)} custom-call(s32[2]{0:T(128)} %pad_add_fusion.place_ref, bf16[26,512,2048]{2,1,0:T(8,128)(2,1)} %shard_map.411.hits_ref, bf16[4,4,13,64,128]{4,3,2,1,0:T(8,128)(2,1)} %copy-done, bf16[4,4,13,64,128]{4,3,2,1,0:T(8,128)(2,1)} %copy-done.23, bf16[4,4,13,64,128]{4,3,2,1,0:T(8,128)(2,1)} %copy-done.1, ...), custom_call_target="tpu_custom_call" | custom-call | flops 1 | bytes 1 | tf_op jit(solution)/shard_map/pallas_call | solution.py:181
  230.6 28.6 %shard_map.413 = (bf16[3,512,3456]{2,1,0:T(8,128)(2,1)}, bf16[3,512,512]{2,1,0:T(8,128)(2,1)}, bf16[512,3456]{1,0:T(8,128)(2,1)}) custom-call(f32[512,3456]{1,0:T(8,128)} %shard_map.412.anchor_in, bf16[3,3456,512]{2,1,0:T(8,128)(2,1)} %all-gather.4.cloned.1.call-done.down_ref, bf16[3,512,3456]{2,1,0:T(8,128)(2,1)} %all-gather.6.cloned.1.call-done.up_ref, ...), custom_call_target="tpu_custom_call" | custom-call | flops 1 | bytes 1 | tf_op jit(solution)/shard_map/pallas_call | solution.py:250
  259.2 28.5 %shard_map.414 = (f32[1,1]{1,0:T(1,128)}, f32[1,512]{1,0:T(1,128)}, f32[1,1]{1,0:T(1,128)}, f32[1,1024]{1,0:T(1,128)}, f32[1,1024]{1,0:T(1,128)}, /*index=5*/f32...) custom-call(bf16[512,3456]{1,0:T(8,128)(2,1)} %get-tuple-element.71.input_ref, ...), custom_call_target="tpu_custom_call" | custom-call | flops 1 | bytes 1 | tf_op jit(solution)/shard_map/pallas_call | solution.py:362
  291.2 3.5 collective-permute-done.12
  297.2 51.1 %shard_map.415 = (bf16[3,4,64,3456]{3,2,1,0:T(8,128)(2,1)}, bf16[3,4,64,3456]{3,2,1,0:T(8,128)(2,1)}, bf16[3,3456,512]{2,1,0:T(8,128)(2,1)}, f32[3,1,3456]{2,1,0:T(1,128)}, bf16[512,3456]{1,0:T(8,128)(2,1)}) custom-call(s32[1]{0:T(128)} %bitcast.core_ref, f32[512,3456]{1,0:T(8,128)} %shard_map.412.anchor_in, f32[512,3456]{1,0:T(8,128)} %get-tuple-element.76.grad_in, ...), custom_call_target="tpu_custom_call" | custom-call | flops 999999995904 | bytes 70778880 | tf_op jit(solution)/shard_map/pallas_call | solution.py:489
  351.2 16.5 %shard_map.416 = (bf16[14,4,256,128]{3,2,1,0:T(8,128)(2,1)}, bf16[14,4,256,128]{3,2,1,0:T(8,128)(2,1)}) custom-call(s32[1]{0:T(128)} %bitcast.core_ref, bf16[26,512,2048]{2,1,0:T(8,128)(2,1)} %shard_map.411.hits_ref, bf16[512,3456]{1,0:T(8,128)(2,1)} %get-tuple-element.99.grad_ref), custom_call_target="tpu_custom_call" | custom-call | flops 999999995904 | bytes 1 | tf_op jit(solution)/shard_map/pallas_call | solution.py:558
  369.7 2.9 fusion.41
  374.1 6.6 collective-permute-done.17
  381.7 4.4 fusion.40
  391.2 14.4 %shard_map.417 = (bf16[12,4,256,128]{3,2,1,0:T(8,128)(2,1)}, bf16[12,4,256,128]{3,2,1,0:T(8,128)(2,1)}) custom-call(s32[1]{0:T(128)} %bitcast.core_ref, bf16[26,512,2048]{2,1,0:T(8,128)(2,1)} %shard_map.411.hits_ref, bf16[512,3456]{1,0:T(8,128)(2,1)} %get-tuple-element.99.grad_ref), custom_call_target="tpu_custom_call" | custom-call | flops 10000000000 | bytes 1 | tf_op jit(solution)/shard_map/pallas_call | solution.py:558
  410.4 11.5 %collective-permute-start.18 = (bf16[1248,128]{1,0:T(8,128)(2,1)}, bf16[1248,128]{1,0:T(8,128)(2,1)}, u32[]{:S(2)}, u32[]{:S(2)}) collective-permute-start(bf16[1248,128]{1,0:T(8,128)(2,1)} %pad_maximum_fusion.13), channel_id=1, source_target_pairs={{0,1},{1,2},{2,3},{3,0},{4,5},{5,6},{6,7},{7,4},{8,9},{9,10},{10,1... | collective-permute-start | bytes 958472 | tf_op jit(solution)/shard_map/ppermute | solution.py:597
  428.8 3.8 collective-permute-done.18
  432.6 12.6 %collective-permute-done.19 = bf16[1248,128]{1,0:T(8,128)(2,1)} collective-permute-done((bf16[1248,128]{1,0:T(8,128)(2,1)}, bf16[1248,128]{1,0:T(8,128)(2,1)}, u32[]{:S(2)}, u32[]{:S(2)}) %collective-permute-start.19) | collective-permute-done | bytes 319520 | tf_op jit(solution)/shard_map/ppermute | solution.py:597
  446.7 7.4 %collective-permute-start.43 = (bf16[1248,128]{1,0:T(8,128)(2,1)S(1)}, bf16[1248,128]{1,0:T(8,128)(2,1)S(1)}, u32[]{:S(2)}, u32[]{:S(2)}) collective-permute-start(bf16[1248,128]{1,0:T(8,128)(2,1)S(1)} %add_convert_fusion.1), channel_id=1, source_target_pairs={{0,1},{1,2},{2,3},{3,0},{4,5},{5,6},{6,7},{7,4},{8,9},{9,10},{10,1... | collective-permute-start | bytes 958472 | tf_op jit(solution)/shard_map/ppermute | solution.py:597
  462.0 5.1 add_bitcast_fusion
  472.2 3.2 collective-permute-done.44
  476.9 6.3 collective-permute-done.23
  484.4 13.8 %collective-permute-done.24 = bf16[3,32,3456]{2,1,0:T(8,128)(2,1)S(1)} collective-permute-done((bf16[3,32,3456]{2,1,0:T(8,128)(2,1)S(1)}, bf16[3,32,3456]{2,1,0:T(8,128)(2,1)S(1)}, u32[]{:S(2)}, u32[]{:S(2)}) %collective-permute-start.24) | collective-permute-done | bytes 663584 | tf_op jit(solution)/shard_map/ppermute | solution.py:592
  499.4 2.6 add_bitcast_fusion.2
  506.7 2.6 reshape.205
  513.3 3.1 multiply_subtract_fusion.3
  516.4 19.6 %collective-permute-done.22 = bf16[14,4,2,64,128]{4,3,0,1,2:T(8,128)(2,1)} collective-permute-done((bf16[14,4,2,64,128]{4,3,0,1,2:T(8,128)(2,1)}, bf16[14,4,2,64,128]{4,3,0,1,2:T(8,128)(2,1)}, u32[]{:S(2)}, u32[]{:S(2)}) %collective-permute-start.22) | collective-permute-done | bytes 1835040 | tf_op jit(solution)/shard_map/ppermute | solution.py:592
  542.8 3.4 multiply_subtract_fusion.2
  546.2 12.3 %collective-permute-done.25 = bf16[14,4,64,128]{3,2,0,1:T(8,128)(2,1)S(1)} collective-permute-done((bf16[14,4,64,128]{3,2,0,1:T(8,128)(2,1)S(1)}, bf16[14,4,64,128]{3,2,0,1:T(8,128)(2,1)S(1)}, u32[]{:S(2)}, u32[]{:S(2)}) %collective-permute-start.25) | collective-permute-done | bytes 917536 | tf_op jit(solution)/shard_map/ppermute | solution.py:592
  563.5 45.1 %all-reduce.4.cloned.1.call-done = (bf16[3,64,3456]{2,1,0:T(8,128)(2,1)}, bf16[3,432,512]{2,1,0:T(8,128)(2,1)}) async-done(((bf16[3,64,3456]{2,1,0:T(8,128)(2,1)}, bf16[3,432,512]{2,1,0:T(8,128)(2,1)}), (bf16[3,64,3456]{2,1,0:T(8,128)(2,1)}, bf16[3,432,512]{2,1,0:T(8,128)(2,1)})) %all-reduce.4.cloned.1.call-update) | async-done | bytes 2654224 | tf_op jit(solution)/shard_map/psum | solution.py:861
  611.8 3.0 collective-permute-start.36
  614.8 7.1 %multiply_subtract_fusion = (f32[3,64,3456]{2,1,0:T(8,128)}, f32[3,64,3456]{2,1,0:T(8,128)}, f32[3,64,3456]{2,1,0:T(8,128)}) fusion(f32[3,64,3456]{2,1,0:T(8,128)S(1)} %copy-done.4, bf16[3,64,3456]{2,1,0:T(8,128)(2,1)S(1)} %copy-done.37, f32[3,64,3456]{2,1,0:T(8,128)} %param.36, f32[3,64,3456]{2,1,0:T(8,128)} %param.37), kind=kLoop, calls=%fused_computation.21 | loop fusion | flops 10616832 | bytes 17252352 | tf_op jit(solution)/shard_map/sub | solution.py:713
  622.0 4.7 multiply_subtract_fusion.1
  626.7 15.2 %collective-permute-done.35 = bf16[1664,128]{1,0:T(8,128)(2,1)S(1)} collective-permute-done((bf16[1664,128]{1,0:T(8,128)(2,1)S(1)}, bf16[1664,128]{1,0:T(8,128)(2,1)S(1)}, u32[]{:S(2)}, u32[]{:S(2)}) %collective-permute-start.35) | collective-permute-done | bytes 426016 | tf_op jit(solution)/shard_map/ppermute | solution.py:597
  648.0 8.2 %collective-permute-start.32 = (f32[13442]{0:T(1024)S(1)}, f32[13442]{0:T(1024)S(1)}, u32[]{:S(2)}, u32[]{:S(2)}) collective-permute-start(f32[13442]{0:T(1024)S(1)} %add.630), channel_id=1, source_target_pairs={{0,1},{1,0},{2,3},{3,2},{4,5},{5,4},{6,7},{7,6},{8,9},{9,8},{10,11... | collective-permute-start | bytes 161312 | tf_op jit(solution)/shard_map/ppermute | solution.py:699
  660.4 3.2 collective-permute-done.33
  668.7 4.4 collective-permute-done.38
  678.1 12.7 %add_subtract_fusion = (f32[26,512,128]{2,1,0:T(8,128)}, f32[26,512,128]{2,1,0:T(8,128)}, f32[26,512,128]{2,1,0:T(8,128)}) fusion(f32[26,512,128]{2,1,0:T(8,128)S(1)} %bitcast.228, bf16[13,512,128]{2,1,0:T(8,128)(2,1)S(1)} %fusion.17, bf16[13,512,128]{2,1,0:T(8,128)(2,1)S(1)} %fusion.23, f32[26,512,128]{2,1,0:T(8,128)} %param.30, f32[26,512,128]{2,1,0:T(8,128)} %param.31), kind=kLoop, calls=%fused_computation.4 | loop fusion | flops 27262976 | bytes 44302336 | tf_op jit(solution)/shard_map/sub | solution.py:713
  (308 shorter events, 129.1 us)
Async XLA Ops:
  7.2 223.3 %all-gather.4.cloned.1.call-start = ((), (), s32[]{:S(2)}) async-start(), calls=%async_computation.2 | async-start | bytes 11943936 | tf_op jit(solution)/shard_map/all_gather | solution.py:745
  10.4 220.1 %all-gather.6.cloned.1.call-start = ((), (), s32[]{:S(2)}) async-start(), calls=%async_computation.3 | async-start | bytes 11943936 | tf_op jit(solution)/shard_map/all_gather | solution.py:746
  11.7 247.5 %all-gather.8.cloned.1.call-start = ((), (), s32[]{:S(2)}) async-start(), calls=%async_computation.4 | async-start | bytes 7962624 | tf_op jit(solution)/shard_map/all_gather | solution.py:747
  14.3 376.9 %reduce-scatter.3.cloned.1.call-start = ((), (), s32[]{:S(2)}) async-start(), calls=%async_computation.5 | async-start | bytes 7962624 | tf_op jit(solution)/shard_map/reduce_scatter | solution.py:789
  15.6 15.9 %collective-permute-start = (bf16[26,64,128]{2,1,0:T(8,128)(2,1)S(1)}, bf16[26,64,128]{2,1,0:T(8,128)(2,1)S(1)}, u32[]{:S(2)}, u32[]{:S(2)}) collective-permute-start(bf16[26,64,128]{2,1,0:T(8,128)(2,1)S(1)} %dynamic-slice_convert_fusion), channel_id=1, source_target_pairs={{0,1},{1,2},{2,3},{3,0},{4,5},{5,6},{6,7},{7,4},{8,9},{9,10},{10,1... | collective-permute-start | bytes 1277960 | tf_op jit(solution)/shard_map/ppermute | solution.py:597
  18.7 30.2 %collective-permute-start.1 = (bf16[26,64,128]{2,1,0:T(8,128)(2,1)S(1)}, bf16[26,64,128]{2,1,0:T(8,128)(2,1)S(1)}, u32[]{:S(2)}, u32[]{:S(2)}) collective-permute-start(bf16[26,64,128]{2,1,0:T(8,128)(2,1)S(1)} %dynamic-slice_convert_fusion), channel_id=1, source_target_pairs={{0,2},{1,3},{2,0},{3,1},{4,6},{5,7},{6,4},{7,5},{8,10},{9,11},{10,... | collective-permute-start | bytes 1277960 | tf_op jit(solution)/shard_map/ppermute | solution.py:597
  21.3 27.7 %collective-permute-start.2 = (bf16[26,64,128]{2,1,0:T(8,128)(2,1)S(1)}, bf16[26,64,128]{2,1,0:T(8,128)(2,1)S(1)}, u32[]{:S(2)}, u32[]{:S(2)}) collective-permute-start(bf16[26,64,128]{2,1,0:T(8,128)(2,1)S(1)} %dynamic-slice_convert_fusion), channel_id=1, source_target_pairs={{0,3},{1,0},{2,1},{3,2},{4,7},{5,4},{6,5},{7,6},{8,11},{9,8},{10,9... | collective-permute-start | bytes 1277960 | tf_op jit(solution)/shard_map/ppermute | solution.py:597
  49.1 40.1 %collective-permute-start.3 = (bf16[1,4,13,64,128]{4,3,2,1,0:T(8,128)(2,1)S(1)}, bf16[1,4,13,64,128]{4,3,2,1,0:T(8,128)(2,1)S(1)}, u32[]{:S(2)}, u32[]{:S(2)}) collective-permute-start(bf16[1,4,13,64,128]{4,3,2,1,0:T(8,128)(2,1)S(1)} %maximum_bitcast_fusion.1), channel_id=1, source_target_pairs={{0,8},{4,12},{8,0},{12,4},{16,24},{20,28},{24,16},{28,20},{1,9},{5... | collective-permute-start | bytes 2555912 | tf_op jit(solution)/shard_map/ppermute | solution.py:592
  50.8 41.4 %collective-permute-start.6 = (bf16[1,4,13,64,128]{4,3,2,1,0:T(8,128)(2,1)S(1)}, bf16[1,4,13,64,128]{4,3,2,1,0:T(8,128)(2,1)S(1)}, u32[]{:S(2)}, u32[]{:S(2)}) collective-permute-start(bf16[1,4,13,64,128]{4,3,2,1,0:T(8,128)(2,1)S(1)} %maximum_bitcast_fusion.2), channel_id=1, source_target_pairs={{0,16},{4,20},{8,24},{12,28},{16,0},{20,4},{24,8},{28,12},{1,17},{... | collective-permute-start | bytes 2555912 | tf_op jit(solution)/shard_map/ppermute | solution.py:592
  52.5 49.5 %collective-permute-start.9 = (bf16[1,128,1536]{2,1,0:T(8,128)(2,1)S(1)}, bf16[1,128,1536]{2,1,0:T(8,128)(2,1)S(1)}, u32[]{:S(2)}, u32[]{:S(2)}) collective-permute-start(bf16[1,128,1536]{2,1,0:T(8,128)(2,1)S(1)} %pad_maximum_fusion.12), channel_id=1, source_target_pairs={{0,8},{4,12},{8,0},{12,4},{16,24},{20,28},{24,16},{28,20},{1,9},{5... | collective-permute-start | bytes 1179656 | tf_op jit(solution)/shard_map/ppermute | solution.py:592
  90.7 86.5 %collective-permute-start.4 = (bf16[2,4,13,64,128]{4,3,2,1,0:T(8,128)(2,1)}, bf16[2,4,13,64,128]{4,3,2,1,0:T(8,128)(2,1)}, u32[]{:S(2)}, u32[]{:S(2)}) collective-permute-start(bf16[2,4,13,64,128]{4,3,2,1,0:T(8,128)(2,1)} %pad_maximum_fusion.3), channel_id=1, source_target_pairs={{0,16},{4,20},{8,24},{12,28},{16,0},{20,4},{24,8},{28,12},{1,17},{... | collective-permute-start | bytes 5111816 | tf_op jit(solution)/shard_map/ppermute | solution.py:592
  93.7 85.7 %collective-permute-start.7 = (bf16[2,4,13,64,128]{4,3,2,1,0:T(8,128)(2,1)}, bf16[2,4,13,64,128]{4,3,2,1,0:T(8,128)(2,1)}, u32[]{:S(2)}, u32[]{:S(2)}) collective-permute-start(bf16[2,4,13,64,128]{4,3,2,1,0:T(8,128)(2,1)} %pad_maximum_fusion.4), channel_id=1, source_target_pairs={{0,8},{4,12},{8,0},{12,4},{16,24},{20,28},{24,16},{28,20},{1,9},{5... | collective-permute-start | bytes 5111816 | tf_op jit(solution)/shard_map/ppermute | solution.py:592
  103.0 72.8 %collective-permute-start.10 = (bf16[2,128,1536]{2,1,0:T(8,128)(2,1)}, bf16[2,128,1536]{2,1,0:T(8,128)(2,1)}, u32[]{:S(2)}, u32[]{:S(2)}) collective-permute-start(bf16[2,128,1536]{2,1,0:T(8,128)(2,1)} %pad_maximum_fusion.9), channel_id=1, source_target_pairs={{0,16},{4,20},{8,24},{12,28},{16,0},{20,4},{24,8},{28,12},{1,17},{... | collective-permute-start | bytes 2359304 | tf_op jit(solution)/shard_map/ppermute | solution.py:592
  177.1 8.1 %collective-permute-start.11 = (bf16[4,128,1536]{2,1,0:T(8,128)(2,1)S(1)}, bf16[4,128,1536]{2,1,0:T(8,128)(2,1)S(1)}, u32[]{:S(2)}, u32[]{:S(2)}) collective-permute-start(bf16[4,128,1536]{2,1,0:T(8,128)(2,1)S(1)} %pad_maximum_fusion.5), channel_id=1, source_target_pairs={{0,4},{4,0},{8,12},{12,8},{16,20},{20,16},{24,28},{28,24},{1,5},{5... | collective-permute-start | bytes 4718600 | tf_op jit(solution)/shard_map/ppermute | solution.py:592
  178.9 6.8 collective-permute-start.5
  181.8 9.9 %collective-permute-start.8 = (bf16[4,4,13,64,128]{4,3,2,1,0:T(8,128)(2,1)S(1)}, bf16[4,4,13,64,128]{4,3,2,1,0:T(8,128)(2,1)}, u32[]{:S(2)}, u32[]{:S(2)}) collective-permute-start(bf16[4,4,13,64,128]{4,3,2,1,0:T(8,128)(2,1)S(1)} %pad_maximum_fusion.1.own_b), channel_id=1, source_target_pairs={{0,4},{4,0},{8,12},{12,8},{16,20},{20,16},{24,28},{28,24},{1,5},{5... | collective-permute-start | bytes 10223624 | tf_op jit(solution)/shard_map/ppermute | solution.py:592
  291.2 213.0 %reduce-scatter.5.cloned.1.call-start = ((), (), s32[]{:S(2)}) async-start(), calls=%async_computation.6 | async-start | bytes 11943936 | tf_op jit(solution)/shard_map/reduce_scatter | solution.py:810
  296.0 55.2 %collective-permute-start.13 = (bf16[2,128,1536]{2,1,0:T(8,128)(2,1)}, bf16[2,128,1536]{2,1,0:T(8,128)(2,1)}, u32[]{:S(2)}, u32[]{:S(2)}) collective-permute-start(bf16[2,128,1536]{2,1,0:T(8,128)(2,1)} %add_bitcast_fusion.10), channel_id=1, source_target_pairs={{0,8},{4,12},{8,0},{12,4},{16,24},{20,28},{24,16},{28,20},{1,9},{5... | collective-permute-start | bytes 2359304 | tf_op jit(solution)/shard_map/ppermute | solution.py:592
  348.3 33.4 %collective-permute-start.15 = (bf16[3,4,64,3456]{3,2,1,0:T(8,128)(2,1)}, bf16[3,4,64,3456]{3,2,1,0:T(8,128)(2,1)}, u32[]{:S(2)}, u32[]{:S(2)}) collective-permute-start(bf16[3,4,64,3456]{3,2,1,0:T(8,128)(2,1)} %get-tuple-element.91), channel_id=1, source_target_pairs={{0,4},{4,0},{8,12},{12,8},{16,20},{20,16},{24,28},{28,24},{1,5},{5... | collective-permute-start | bytes 15925256 | tf_op jit(solution)/shard_map/ppermute | solution.py:592
  348.4 260.2 %all-reduce.4.cloned.1.call-start = ((), (), s32[]{:S(2)}) async-start(), calls=%async_computation.7 | async-start | bytes 5308416 | tf_op jit(solution)/shard_map/psum | solution.py:861
  368.8 11.9 %collective-permute-start.17 = (bf16[128,1536]{1,0:T(8,128)(2,1)S(1)}, bf16[128,1536]{1,0:T(8,128)(2,1)S(1)}, u32[]{:S(2)}, u32[]{:S(2)}) collective-permute-start(bf16[128,1536]{1,0:T(8,128)(2,1)S(1)} %add_bitcast_fusion.13), channel_id=1, source_target_pairs={{0,16},{4,20},{8,24},{12,28},{16,0},{20,4},{24,8},{28,12},{1,17},{... | collective-permute-start | bytes 1179656 | tf_op jit(solution)/shard_map/ppermute | solution.py:592
  372.6 33.0 %collective-permute-start.14 = (bf16[14,4,256,128]{3,2,1,0:T(8,128)(2,1)}, bf16[14,4,256,128]{3,2,1,0:T(8,128)(2,1)}, u32[]{:S(2)}, u32[]{:S(2)}) collective-permute-start(bf16[14,4,256,128]{3,2,1,0:T(8,128)(2,1)} %get-tuple-element.89), channel_id=1, source_target_pairs={{0,4},{4,0},{8,12},{12,8},{16,20},{20,16},{24,28},{28,24},{1,5},{5... | collective-permute-start | bytes 11010056 | tf_op jit(solution)/shard_map/ppermute | solution.py:592
  388.5 67.3 %collective-permute-start.16 = (bf16[3,2,32,3456]{3,2,0,1:T(8,128)(2,1)}, bf16[3,2,32,3456]{3,2,0,1:T(8,128)(2,1)}, u32[]{:S(2)}, u32[]{:S(2)}) collective-permute-start(bf16[3,2,32,3456]{3,2,0,1:T(8,128)(2,1)} %get-tuple-element.155), channel_id=1, source_target_pairs={{0,8},{4,12},{8,0},{12,4},{16,24},{20,28},{24,16},{28,20},{1,9},{5... | collective-permute-start | bytes 3981320 | tf_op jit(solution)/shard_map/ppermute | solution.py:592
  389.8 69.4 %collective-permute-start.21 = (bf16[3,2,32,3456]{3,2,0,1:T(8,128)(2,1)}, bf16[3,2,32,3456]{3,2,0,1:T(8,128)(2,1)}, u32[]{:S(2)}, u32[]{:S(2)}) collective-permute-start(bf16[3,2,32,3456]{3,2,0,1:T(8,128)(2,1)} %get-tuple-element.150), channel_id=1, source_target_pairs={{0,16},{4,20},{8,24},{12,28},{16,0},{20,4},{24,8},{28,12},{1,17},{... | collective-permute-start | bytes 3981320 | tf_op jit(solution)/shard_map/ppermute | solution.py:592
  410.4 22.2 %collective-permute-start.18 = (bf16[1248,128]{1,0:T(8,128)(2,1)}, bf16[1248,128]{1,0:T(8,128)(2,1)}, u32[]{:S(2)}, u32[]{:S(2)}) collective-permute-start(bf16[1248,128]{1,0:T(8,128)(2,1)} %pad_maximum_fusion.13), channel_id=1, source_target_pairs={{0,1},{1,2},{2,3},{3,0},{4,5},{5,6},{6,7},{7,4},{8,9},{9,10},{10,1... | collective-permute-start | bytes 958472 | tf_op jit(solution)/shard_map/ppermute | solution.py:597
  422.6 22.6 %collective-permute-start.19 = (bf16[1248,128]{1,0:T(8,128)(2,1)}, bf16[1248,128]{1,0:T(8,128)(2,1)}, u32[]{:S(2)}, u32[]{:S(2)}) collective-permute-start(bf16[1248,128]{1,0:T(8,128)(2,1)} %pad_maximum_fusion.14), channel_id=1, source_target_pairs={{0,2},{1,3},{2,0},{3,1},{4,6},{5,7},{6,4},{7,5},{8,10},{9,11},{10,... | collective-permute-start | bytes 958472 | tf_op jit(solution)/shard_map/ppermute | solution.py:597
  425.8 19.4 %collective-permute-start.20 = (bf16[1248,128]{1,0:T(8,128)(2,1)}, bf16[1248,128]{1,0:T(8,128)(2,1)}, u32[]{:S(2)}, u32[]{:S(2)}) collective-permute-start(bf16[1248,128]{1,0:T(8,128)(2,1)} %pad_maximum_fusion.15), channel_id=1, source_target_pairs={{0,3},{1,0},{2,1},{3,2},{4,7},{5,4},{6,5},{7,6},{8,11},{9,8},{10,9... | collective-permute-start | bytes 958472 | tf_op jit(solution)/shard_map/ppermute | solution.py:597
  432.6 66.8 %collective-permute-start.26 = (bf16[12,4,256,128]{3,2,1,0:T(8,128)(2,1)}, bf16[12,4,256,128]{3,2,1,0:T(8,128)(2,1)S(1)}, u32[]{:S(2)}, u32[]{:S(2)}) collective-permute-start(bf16[12,4,256,128]{3,2,1,0:T(8,128)(2,1)} %get-tuple-element.111), channel_id=1, source_target_pairs={{0,4},{4,0},{8,12},{12,8},{16,20},{20,16},{24,28},{28,24},{1,5},{5... | collective-permute-start | bytes 9437192 | tf_op jit(solution)/shard_map/ppermute | solution.py:592
  446.7 22.3 %collective-permute-start.43 = (bf16[1248,128]{1,0:T(8,128)(2,1)S(1)}, bf16[1248,128]{1,0:T(8,128)(2,1)S(1)}, u32[]{:S(2)}, u32[]{:S(2)}) collective-permute-start(bf16[1248,128]{1,0:T(8,128)(2,1)S(1)} %add_convert_fusion.1), channel_id=1, source_target_pairs={{0,1},{1,2},{2,3},{3,0},{4,5},{5,6},{6,7},{7,4},{8,9},{9,10},{10,1... | collective-permute-start | bytes 958472 | tf_op jit(solution)/shard_map/ppermute | solution.py:597
  454.1 21.3 %collective-permute-start.44 = (bf16[1248,128]{1,0:T(8,128)(2,1)S(1)}, bf16[1248,128]{1,0:T(8,128)(2,1)S(1)}, u32[]{:S(2)}, u32[]{:S(2)}) collective-permute-start(bf16[1248,128]{1,0:T(8,128)(2,1)S(1)} %add_convert_fusion.1), channel_id=1, source_target_pairs={{0,2},{1,3},{2,0},{3,1},{4,6},{5,7},{6,4},{7,5},{8,10},{9,11},{10,... | collective-permute-start | bytes 958472 | tf_op jit(solution)/shard_map/ppermute | solution.py:597
  455.7 20.4 %collective-permute-start.45 = (bf16[1248,128]{1,0:T(8,128)(2,1)S(1)}, bf16[1248,128]{1,0:T(8,128)(2,1)S(1)}, u32[]{:S(2)}, u32[]{:S(2)}) collective-permute-start(bf16[1248,128]{1,0:T(8,128)(2,1)S(1)} %add_convert_fusion.1), channel_id=1, source_target_pairs={{0,3},{1,0},{2,1},{3,2},{4,7},{5,4},{6,5},{7,6},{8,11},{9,8},{10,9... | collective-permute-start | bytes 958472 | tf_op jit(solution)/shard_map/ppermute | solution.py:597
  459.2 24.0 %collective-permute-start.23 = (bf16[3,32,3456]{2,1,0:T(8,128)(2,1)S(1)}, bf16[3,32,3456]{2,1,0:T(8,128)(2,1)S(1)}, u32[]{:S(2)}, u32[]{:S(2)}) collective-permute-start(bf16[3,32,3456]{2,1,0:T(8,128)(2,1)S(1)} %add_bitcast_fusion.12), channel_id=1, source_target_pairs={{0,16},{4,20},{8,24},{12,28},{16,0},{20,4},{24,8},{28,12},{1,17},{... | collective-permute-start | bytes 1990664 | tf_op jit(solution)/shard_map/ppermute | solution.py:592
  469.0 29.2 %collective-permute-start.24 = (bf16[3,32,3456]{2,1,0:T(8,128)(2,1)S(1)}, bf16[3,32,3456]{2,1,0:T(8,128)(2,1)S(1)}, u32[]{:S(2)}, u32[]{:S(2)}) collective-permute-start(bf16[3,32,3456]{2,1,0:T(8,128)(2,1)S(1)} %add_bitcast_fusion.11), channel_id=1, source_target_pairs={{0,8},{4,12},{8,0},{12,4},{16,24},{20,28},{24,16},{28,20},{1,9},{5... | collective-permute-start | bytes 1990664 | tf_op jit(solution)/shard_map/ppermute | solution.py:592
  475.4 60.6 %collective-permute-start.22 = (bf16[14,4,2,64,128]{4,3,0,1,2:T(8,128)(2,1)}, bf16[14,4,2,64,128]{4,3,0,1,2:T(8,128)(2,1)}, u32[]{:S(2)}, u32[]{:S(2)}) collective-permute-start(bf16[14,4,2,64,128]{4,3,0,1,2:T(8,128)(2,1)} %get-tuple-element.145), channel_id=1, source_target_pairs={{0,8},{4,12},{8,0},{12,4},{16,24},{20,28},{24,16},{28,20},{1,9},{5... | collective-permute-start | bytes 5505032 | tf_op jit(solution)/shard_map/ppermute | solution.py:592
  502.0 38.9 %collective-permute-start.27 = (bf16[12,4,2,64,128]{4,3,0,1,2:T(8,128)(2,1)}, bf16[12,4,2,64,128]{4,3,0,1,2:T(8,128)(2,1)}, u32[]{:S(2)}, u32[]{:S(2)}) collective-permute-start(bf16[12,4,2,64,128]{4,3,0,1,2:T(8,128)(2,1)} %get-tuple-element.147), channel_id=1, source_target_pairs={{0,16},{4,20},{8,24},{12,28},{16,0},{20,4},{24,8},{28,12},{1,17},{... | collective-permute-start | bytes 4718600 | tf_op jit(solution)/shard_map/ppermute | solution.py:592
  537.4 21.1 %collective-permute-start.25 = (bf16[14,4,64,128]{3,2,0,1:T(8,128)(2,1)S(1)}, bf16[14,4,64,128]{3,2,0,1:T(8,128)(2,1)S(1)}, u32[]{:S(2)}, u32[]{:S(2)}) collective-permute-start(bf16[14,4,64,128]{3,2,0,1:T(8,128)(2,1)S(1)} %add_bitcast_fusion.8), channel_id=1, source_target_pairs={{0,16},{4,20},{8,24},{12,28},{16,0},{20,4},{24,8},{28,12},{1,17},{... | collective-permute-start | bytes 2752520 | tf_op jit(solution)/shard_map/ppermute | solution.py:592
  542.1 18.3 %collective-permute-start.28 = (bf16[12,4,64,128]{3,2,0,1:T(8,128)(2,1)S(1)}, bf16[12,4,64,128]{3,2,0,1:T(8,128)(2,1)S(1)}, u32[]{:S(2)}, u32[]{:S(2)}) collective-permute-start(bf16[12,4,64,128]{3,2,0,1:T(8,128)(2,1)S(1)} %add_bitcast_fusion.9), channel_id=1, source_target_pairs={{0,8},{4,12},{8,0},{12,4},{16,24},{20,28},{24,16},{28,20},{1,9},{5... | collective-permute-start | bytes 2359304 | tf_op jit(solution)/shard_map/ppermute | solution.py:592
  563.2 79.9 %collective-permute-start.30 = (f32[13442]{0:T(1024)S(1)}, f32[13442]{0:T(1024)S(1)}, u32[]{:S(2)}, u32[]{:S(2)}) collective-permute-start(f32[13442]{0:T(1024)S(1)} %add.622), channel_id=1, source_target_pairs={{0,8},{4,12},{8,0},{12,4},{16,24},{20,28},{24,16},{28,20},{1,9},{5... | collective-permute-start | bytes 161312 | tf_op jit(solution)/shard_map/ppermute | solution.py:699
  610.1 16.6 %collective-permute-start.34 = (bf16[1664,128]{1,0:T(8,128)(2,1)S(1)}, bf16[1664,128]{1,0:T(8,128)(2,1)S(1)}, u32[]{:S(2)}, u32[]{:S(2)}) collective-permute-start(bf16[1664,128]{1,0:T(8,128)(2,1)S(1)} %get-tuple-element.159), channel_id=1, source_target_pairs={{0,1},{1,2},{2,3},{3,0},{4,5},{5,6},{6,7},{7,4},{8,9},{9,10},{10,1... | collective-permute-start | bytes 1277960 | tf_op jit(solution)/shard_map/ppermute | solution.py:597
  610.1 31.7 %collective-permute-start.35 = (bf16[1664,128]{1,0:T(8,128)(2,1)S(1)}, bf16[1664,128]{1,0:T(8,128)(2,1)S(1)}, u32[]{:S(2)}, u32[]{:S(2)}) collective-permute-start(bf16[1664,128]{1,0:T(8,128)(2,1)S(1)} %get-tuple-element.161), channel_id=1, source_target_pairs={{0,2},{1,3},{2,0},{3,1},{4,6},{5,7},{6,4},{7,5},{8,10},{9,11},{10,... | collective-permute-start | bytes 1277960 | tf_op jit(solution)/shard_map/ppermute | solution.py:597
  611.8 30.1 %collective-permute-start.36 = (bf16[1664,128]{1,0:T(8,128)(2,1)S(1)}, bf16[1664,128]{1,0:T(8,128)(2,1)S(1)}, u32[]{:S(2)}, u32[]{:S(2)}) collective-permute-start(bf16[1664,128]{1,0:T(8,128)(2,1)S(1)} %get-tuple-element.160), channel_id=1, source_target_pairs={{0,3},{1,0},{2,1},{3,2},{4,7},{5,4},{6,5},{7,6},{8,11},{9,8},{10,9... | collective-permute-start | bytes 1277960 | tf_op jit(solution)/shard_map/ppermute | solution.py:597
  643.2 4.9 collective-permute-start.31
  644.7 20.1 %collective-permute-start.37 = (bf16[1,13,64,128]{3,2,1,0:T(8,128)(2,1)S(1)}, bf16[1,13,64,128]{3,2,1,0:T(8,128)(2,1)S(1)}, u32[]{:S(2)}, u32[]{:S(2)}) collective-permute-start(bf16[1,13,64,128]{3,2,1,0:T(8,128)(2,1)S(1)} %bitcast.237), channel_id=1, source_target_pairs={{0,8},{4,12},{8,0},{12,4},{16,24},{20,28},{24,16},{28,20},{1,9},{5... | collective-permute-start | bytes 638984 | tf_op jit(solution)/shard_map/ppermute | solution.py:592
  646.3 20.8 %collective-permute-start.40 = (bf16[1,13,64,128]{3,2,1,0:T(8,128)(2,1)S(1)}, bf16[1,13,64,128]{3,2,1,0:T(8,128)(2,1)S(1)}, u32[]{:S(2)}, u32[]{:S(2)}) collective-permute-start(bf16[1,13,64,128]{3,2,1,0:T(8,128)(2,1)S(1)} %bitcast.233), channel_id=1, source_target_pairs={{0,16},{4,20},{8,24},{12,28},{16,0},{20,4},{24,8},{28,12},{1,17},{... | collective-permute-start | bytes 638984 | tf_op jit(solution)/shard_map/ppermute | solution.py:592
  648.0 10.4 %collective-permute-start.32 = (f32[13442]{0:T(1024)S(1)}, f32[13442]{0:T(1024)S(1)}, u32[]{:S(2)}, u32[]{:S(2)}) collective-permute-start(f32[13442]{0:T(1024)S(1)} %add.630), channel_id=1, source_target_pairs={{0,1},{1,0},{2,3},{3,2},{4,5},{5,4},{6,7},{7,6},{8,9},{9,8},{10,11... | collective-permute-start | bytes 161312 | tf_op jit(solution)/shard_map/ppermute | solution.py:699
  658.4 5.1 collective-permute-start.33
  664.9 8.3 %collective-permute-start.38 = (bf16[2,13,64,128]{3,2,1,0:T(8,128)(2,1)S(1)}, bf16[2,13,64,128]{3,2,1,0:T(8,128)(2,1)S(1)}, u32[]{:S(2)}, u32[]{:S(2)}) collective-permute-start(bf16[2,13,64,128]{3,2,1,0:T(8,128)(2,1)S(1)} %pad_maximum_fusion.10), channel_id=1, source_target_pairs={{0,16},{4,20},{8,24},{12,28},{16,0},{20,4},{24,8},{28,12},{1,17},{... | collective-permute-start | bytes 1277960 | tf_op jit(solution)/shard_map/ppermute | solution.py:592
  667.1 8.2 %collective-permute-start.41 = (bf16[2,13,64,128]{3,2,1,0:T(8,128)(2,1)S(1)}, bf16[2,13,64,128]{3,2,1,0:T(8,128)(2,1)S(1)}, u32[]{:S(2)}, u32[]{:S(2)}) collective-permute-start(bf16[2,13,64,128]{3,2,1,0:T(8,128)(2,1)S(1)} %pad_maximum_fusion.11), channel_id=1, source_target_pairs={{0,8},{4,12},{8,0},{12,4},{16,24},{20,28},{24,16},{28,20},{1,9},{5... | collective-permute-start | bytes 1277960 | tf_op jit(solution)/shard_map/ppermute | solution.py:592
  (59 other events, 950.0 us)
Sparse Core Ops, SparseCore 0:
  10.5 89.1 all-gather.3
  102.2 90.0 all-gather.5
  194.8 54.9 all-gather.7
  291.3 74.8 reduce-scatter.2
  370.0 126.5 reduce-scatter.4
  504.3 104.2 all-reduce.3
